TPU v7x, 256 devices: a whole 4x4x8 slice. The times are simulated.
256 devices in a mesh: dp: 16 (over x_hi, z), group: 16 (over x_lo, y, core).
Axes of the slice: x: 4 (x_hi: 2, x_lo: 2; x = x_hi * 2 + x_lo), y: 4, z: 8, core: 2. Of those that a mesh axis runs over, the one named last changes fastest.
Arguments:
- motion_frames: bfloat16 [65536, 256], P(('dp', 'group')), may hold values from -6 to 6
- enc_weight: bfloat16 [768, 2048], replicated, may hold values from -0.21875 to 0.21875
- code_ids: int32 [16, 32768], P('group', 'dp'), may hold values from 0 to 8191
- clip_offsets: int32 [256, 8], P(('dp', 'group')), may hold values from 0 to 127
- codebook: bfloat16 [16, 8192, 128], P('group'), may hold values from -6 to 6
- ema_sums: float32 [16, 8192, 128], P('group', 'dp'), may hold values from -18 to 18
- ema_counts: float32 [16, 8192], P('group', 'dp'), may hold values from 1 to 30
- dec_weight: bfloat16 [2048, 512], replicated, may hold values from -0.125 to 0.125
Outputs:
- decoded: bfloat16 [65536, 256], P(('dp', 'group'))
- commit_error: float32 [16, 32768], P('group', 'dp')
- new_codebook: float32 [16, 8192, 128], P('group', 'dp')
- new_counts: float32 [16, 8192], P('group', 'dp')
Inputs may be any that keep to these rules, and one draw needn't show every extreme that they name: A clip begins at latent frame s * 128 + clip_offsets[s, k] of time block s; repeated offsets may occur.
All inputs are finite; a program needn't handle non-finite values.
Results may differ from a plain program's by a relative error of at most 0.0013.
Values may be sent and summed in bfloat16 or wider, within the bound.
No kernel may reach another device: no remote copies, remote signals or barrier semaphores. Data moves between devices by JAX's collectives and lax.ppermute only.
A program may use at most 64 MiB of HBM per device.

v0:
```python
import math

import jax
import jax.numpy as jnp
from jax import lax
from jax.sharding import PartitionSpec as P

ema_decay = 0.9


def passed_along(shard, axis, by):
    size = lax.axis_size(axis)
    pairs = [(i, i + by) for i in range(size) if 0 <= i + by < size]
    return lax.ppermute(shard, axis, pairs)


def code_tables(table, indices, grouped_rows):
    codes, width = table.shape
    rows = indices.shape[0]
    block_size = math.gcd(codes, 1024)
    block_count = codes // block_size
    tiles = table.reshape(block_count, block_size, width)
    block_starts = jnp.arange(block_count, dtype=jnp.int32) * block_size
    columns = lax.broadcasted_iota(jnp.int32, (1, block_size), 1)

    def one_block(picked, inputs):
        tile_rows, first = inputs
        selector = (indices[:, None] == first + columns).astype(jnp.bfloat16)
        picked = picked + jnp.dot(selector, tile_rows, preferred_element_type=jnp.float32)
        sums = lax.dot_general(
            selector, grouped_rows, (((0,), (0,)), ((), ())), preferred_element_type=jnp.float32
        )
        counts = jnp.sum(selector, axis=0, dtype=jnp.float32)
        return (picked, (sums, counts))

    start_pick = jnp.zeros((rows, width), jnp.float32)
    picked, results = lax.scan(one_block, start_pick, (tiles, block_starts))
    sums, counts = results
    return (picked.astype(jnp.bfloat16), sums.reshape(codes, width), counts.reshape(codes))


def body(
    motion_frames, enc_weight, code_ids, clip_offsets, codebook, ema_sums, ema_counts, dec_weight
):
    feat = motion_frames.shape[1]
    pairs = motion_frames.reshape(-1, 2, feat)
    local_len = pairs.shape[0]
    even_rows = pairs[:, 0]
    odd_rows = pairs[:, 1]
    carried = passed_along(odd_rows[-1:], ("dp", "group"), 1)
    earlier = jnp.concatenate([carried, odd_rows[:-1]], axis=0)
    positions = lax.broadcasted_iota(jnp.int32, (local_len, 1), 0)
    starts = jnp.any(positions == clip_offsets, axis=1, keepdims=True)
    earlier = jnp.where(starts, jnp.zeros_like(earlier), earlier)
    stacked = jnp.concatenate([earlier, even_rows, odd_rows], axis=1)
    latent = jnp.dot(stacked, enc_weight, preferred_element_type=jnp.float32).astype(jnp.bfloat16)
    owned = lax.all_to_all(latent, "group", split_axis=1, concat_axis=0, tiled=True)
    groups_here, codes, width = codebook.shape
    rows = owned.shape[0]
    grouped = owned.reshape(rows, groups_here, width).transpose(1, 0, 2)
    picked, batch_sums, batch_counts = jax.vmap(code_tables)(codebook, code_ids, grouped)
    diff = grouped.astype(jnp.float32) - picked.astype(jnp.float32)
    commit_error = jnp.mean(diff * diff, axis=2)
    sums_all, counts_all = (
        lax.psum(batch_sums.astype(jnp.bfloat16), "dp").astype(jnp.float32),
        lax.psum(batch_counts.astype(jnp.bfloat16), "dp").astype(jnp.float32),
    )
    share = ema_counts.shape[1]
    begin = lax.axis_index("dp") * share
    sums_mine = lax.dynamic_slice_in_dim(sums_all, begin, share, 1)
    counts_mine = lax.dynamic_slice_in_dim(counts_all, begin, share, 1)
    new_counts = ema_decay * ema_counts + (1.0 - ema_decay) * counts_mine
    new_codebook = (ema_decay * ema_sums + (1.0 - ema_decay) * sums_mine) / new_counts[:, :, None]
    back_rows = picked.transpose(1, 0, 2).reshape(rows, groups_here * width)
    frame_rows = lax.all_to_all(back_rows, "group", split_axis=0, concat_axis=1, tiled=True)
    decoded = jnp.dot(frame_rows, dec_weight, preferred_element_type=jnp.float32).astype(
        jnp.bfloat16
    )
    decoded = decoded.reshape(2 * local_len, feat)
    return (decoded, commit_error, new_codebook, new_counts)


def solution(mesh):
    return jax.shard_map(
        body,
        mesh=mesh,
        in_specs=(
            P(("dp", "group"), None),
            P(),
            P("group", "dp"),
            P(("dp", "group"), None),
            P("group", None, None),
            P("group", "dp", None),
            P("group", "dp"),
            P(),
        ),
        out_specs=(
            P(("dp", "group"), None),
            P("group", "dp"),
            P("group", "dp", None),
            P("group", "dp"),
        ),
        check_vma=False,
    )
```

profile of v0, /device:TPU:32, one launch (start us, length us, event | category | flops | bytes accessed | tf_op | source)
XLA Modules:
  0.0 287.7 jit_solution(6091092141197638907)
XLA Ops:
  11.4 4.8 %collective-permute-done = bf16[1,256]{1,0:T(2,128)(2,1)S(1)} collective-permute-done((bf16[1,256]{1,0:T(2,128)(2,1)S(1)}, bf16[1,256]{1,0:T(2,128)(2,1)S(1)}, u32[]{:S(2)}, u32[]{:S(2)}) %collective-permute-start) | collective-permute-done | bytes 544 | tf_op jit(solution)/shard_map/ppermute | solution.py:14
  17.8 4.3 %all-to-all-start = ((bf16[128,16,128]{2,0,1:T(8,128)(2,1)}), bf16[128,16,128]{2,0,1:T(8,128)(2,1)}, u32[]{:S(2)}, u32[]{:S(2)}) async-start(bf16[128,16,128]{2,0,1:T(8,128)(2,1)} %bitcast.81), calls=%async_computation | async-start | bytes 1048576 | tf_op jit(solution)/shard_map/all_to_all | solution.py:57
  22.2 10.8 %all-to-all-done = bf16[128,16,128]{2,0,1:T(8,128)(2,1)} async-done(((bf16[128,16,128]{2,0,1:T(8,128)(2,1)}), bf16[128,16,128]{2,0,1:T(8,128)(2,1)}, u32[]{:S(2)}, u32[]{:S(2)}) %all-to-all-start) | async-done | bytes 524320 | tf_op jit(solution)/shard_map/all_to_all | solution.py:57
  33.0 82.4 %while.15 = (s32[]{:T(128)}, f32[1,2048,128]{2,1,0:T(8,128)}, bf16[8,1,1024,128]{3,2,1,0:T(8,128)(2,1)}, bf16[8,1,1024]{2,1,0:T(2,128)(2,1)S(1)}, s32[1,2048]{1,...) while((s32[]{:T(128)}, f32[1,2048,128]{2,1,0:T(8,128)}, ...), condition=%wide.region_3.4_spmd.clone, body=%wide.region_1.3_spmd.clone.sunk | while | flops 1086849024 | bytes 3462275 | solution.py:37
  34.2 3.5 %fusion.52 = f32[1,2048,128]{2,1,0:T(8,128)} fusion(s32[1024]{0:T(1024)S(1)} %bitcast.85, s32[2048]{0:T(1024)S(1)} %bitcast.93, f32[1,2048,128]{2,1,0:T(8,128)} %get-tuple-element.167, pred[]{:T(512)S(6)} %compare.3, bf16[8,1,1024,128]{3,2,1,0:T(8,128)(2,1)} %get-tuple-element.182, s32[]{:T(128)} %get-tuple-element.166), kind=kOutput, calls=%fused_computation.14.clone.1 | convolution fusion | flops 539492352 | bytes 2372097 | tf_op jit(solution)/shard_map/vmap()/while/body/eval_jaxpr/dot_general | solution.py:29
  37.7 4.5 %fusion.53 = bf16[8,1,1024,128]{3,2,1,0:T(8,128)(2,1)} fusion(bf16[8,1,1024,128]{3,2,1,0:T(8,128)(2,1)} %get-tuple-element.168, s32[]{:T(128)} %get-tuple-element.166, s32[1024]{0:T(1024)S(1)} %bitcast.86, s32[2048]{0:T(1024)S(1)} %bitcast.94, bf16[1,2048,128]{2,1,0:T(8,128)(2,1)} %get-tuple-element.183), kind=kOutput, calls=%fused_computation.16.clone.1 | convolution fusion | flops 538968064 | bytes 1061376 | tf_op jit(solution)/shard_map/vmap()/while/body/eval_jaxpr/dot_general | solution.py:30
  44.4 3.6 %fusion.52 = f32[1,2048,128]{2,1,0:T(8,128)} fusion(s32[1024]{0:T(1024)S(1)} %bitcast.85, s32[2048]{0:T(1024)S(1)} %bitcast.93, f32[1,2048,128]{2,1,0:T(8,128)} %get-tuple-element.167, pred[]{:T(512)S(6)} %compare.3, bf16[8,1,1024,128]{3,2,1,0:T(8,128)(2,1)} %get-tuple-element.182, s32[]{:T(128)} %get-tuple-element.166), kind=kOutput, calls=%fused_computation.14.clone.1 | convolution fusion | flops 539492352 | bytes 2372097 | tf_op jit(solution)/shard_map/vmap()/while/body/eval_jaxpr/dot_general | solution.py:29
  48.0 4.5 %fusion.53 = bf16[8,1,1024,128]{3,2,1,0:T(8,128)(2,1)} fusion(bf16[8,1,1024,128]{3,2,1,0:T(8,128)(2,1)} %get-tuple-element.168, s32[]{:T(128)} %get-tuple-element.166, s32[1024]{0:T(1024)S(1)} %bitcast.86, s32[2048]{0:T(1024)S(1)} %bitcast.94, bf16[1,2048,128]{2,1,0:T(8,128)(2,1)} %get-tuple-element.183), kind=kOutput, calls=%fused_computation.16.clone.1 | convolution fusion | flops 538968064 | bytes 1061376 | tf_op jit(solution)/shard_map/vmap()/while/body/eval_jaxpr/dot_general | solution.py:30
  54.7 3.6 %fusion.52 = f32[1,2048,128]{2,1,0:T(8,128)} fusion(s32[1024]{0:T(1024)S(1)} %bitcast.85, s32[2048]{0:T(1024)S(1)} %bitcast.93, f32[1,2048,128]{2,1,0:T(8,128)} %get-tuple-element.167, pred[]{:T(512)S(6)} %compare.3, bf16[8,1,1024,128]{3,2,1,0:T(8,128)(2,1)} %get-tuple-element.182, s32[]{:T(128)} %get-tuple-element.166), kind=kOutput, calls=%fused_computation.14.clone.1 | convolution fusion | flops 539492352 | bytes 2372097 | tf_op jit(solution)/shard_map/vmap()/while/body/eval_jaxpr/dot_general | solution.py:29
  58.4 4.5 %fusion.53 = bf16[8,1,1024,128]{3,2,1,0:T(8,128)(2,1)} fusion(bf16[8,1,1024,128]{3,2,1,0:T(8,128)(2,1)} %get-tuple-element.168, s32[]{:T(128)} %get-tuple-element.166, s32[1024]{0:T(1024)S(1)} %bitcast.86, s32[2048]{0:T(1024)S(1)} %bitcast.94, bf16[1,2048,128]{2,1,0:T(8,128)(2,1)} %get-tuple-element.183), kind=kOutput, calls=%fused_computation.16.clone.1 | convolution fusion | flops 538968064 | bytes 1061376 | tf_op jit(solution)/shard_map/vmap()/while/body/eval_jaxpr/dot_general | solution.py:30
  65.1 3.6 %fusion.52 = f32[1,2048,128]{2,1,0:T(8,128)} fusion(s32[1024]{0:T(1024)S(1)} %bitcast.85, s32[2048]{0:T(1024)S(1)} %bitcast.93, f32[1,2048,128]{2,1,0:T(8,128)} %get-tuple-element.167, pred[]{:T(512)S(6)} %compare.3, bf16[8,1,1024,128]{3,2,1,0:T(8,128)(2,1)} %get-tuple-element.182, s32[]{:T(128)} %get-tuple-element.166), kind=kOutput, calls=%fused_computation.14.clone.1 | convolution fusion | flops 539492352 | bytes 2372097 | tf_op jit(solution)/shard_map/vmap()/while/body/eval_jaxpr/dot_general | solution.py:29
  68.7 4.5 %fusion.53 = bf16[8,1,1024,128]{3,2,1,0:T(8,128)(2,1)} fusion(bf16[8,1,1024,128]{3,2,1,0:T(8,128)(2,1)} %get-tuple-element.168, s32[]{:T(128)} %get-tuple-element.166, s32[1024]{0:T(1024)S(1)} %bitcast.86, s32[2048]{0:T(1024)S(1)} %bitcast.94, bf16[1,2048,128]{2,1,0:T(8,128)(2,1)} %get-tuple-element.183), kind=kOutput, calls=%fused_computation.16.clone.1 | convolution fusion | flops 538968064 | bytes 1061376 | tf_op jit(solution)/shard_map/vmap()/while/body/eval_jaxpr/dot_general | solution.py:30
  75.4 3.6 %fusion.52 = f32[1,2048,128]{2,1,0:T(8,128)} fusion(s32[1024]{0:T(1024)S(1)} %bitcast.85, s32[2048]{0:T(1024)S(1)} %bitcast.93, f32[1,2048,128]{2,1,0:T(8,128)} %get-tuple-element.167, pred[]{:T(512)S(6)} %compare.3, bf16[8,1,1024,128]{3,2,1,0:T(8,128)(2,1)} %get-tuple-element.182, s32[]{:T(128)} %get-tuple-element.166), kind=kOutput, calls=%fused_computation.14.clone.1 | convolution fusion | flops 539492352 | bytes 2372097 | tf_op jit(solution)/shard_map/vmap()/while/body/eval_jaxpr/dot_general | solution.py:29
  79.0 4.4 %fusion.53 = bf16[8,1,1024,128]{3,2,1,0:T(8,128)(2,1)} fusion(bf16[8,1,1024,128]{3,2,1,0:T(8,128)(2,1)} %get-tuple-element.168, s32[]{:T(128)} %get-tuple-element.166, s32[1024]{0:T(1024)S(1)} %bitcast.86, s32[2048]{0:T(1024)S(1)} %bitcast.94, bf16[1,2048,128]{2,1,0:T(8,128)(2,1)} %get-tuple-element.183), kind=kOutput, calls=%fused_computation.16.clone.1 | convolution fusion | flops 538968064 | bytes 1061376 | tf_op jit(solution)/shard_map/vmap()/while/body/eval_jaxpr/dot_general | solution.py:30
  85.7 3.6 %fusion.52 = f32[1,2048,128]{2,1,0:T(8,128)} fusion(s32[1024]{0:T(1024)S(1)} %bitcast.85, s32[2048]{0:T(1024)S(1)} %bitcast.93, f32[1,2048,128]{2,1,0:T(8,128)} %get-tuple-element.167, pred[]{:T(512)S(6)} %compare.3, bf16[8,1,1024,128]{3,2,1,0:T(8,128)(2,1)} %get-tuple-element.182, s32[]{:T(128)} %get-tuple-element.166), kind=kOutput, calls=%fused_computation.14.clone.1 | convolution fusion | flops 539492352 | bytes 2372097 | tf_op jit(solution)/shard_map/vmap()/while/body/eval_jaxpr/dot_general | solution.py:29
  89.3 4.5 %fusion.53 = bf16[8,1,1024,128]{3,2,1,0:T(8,128)(2,1)} fusion(bf16[8,1,1024,128]{3,2,1,0:T(8,128)(2,1)} %get-tuple-element.168, s32[]{:T(128)} %get-tuple-element.166, s32[1024]{0:T(1024)S(1)} %bitcast.86, s32[2048]{0:T(1024)S(1)} %bitcast.94, bf16[1,2048,128]{2,1,0:T(8,128)(2,1)} %get-tuple-element.183), kind=kOutput, calls=%fused_computation.16.clone.1 | convolution fusion | flops 538968064 | bytes 1061376 | tf_op jit(solution)/shard_map/vmap()/while/body/eval_jaxpr/dot_general | solution.py:30
  96.0 3.6 %fusion.52 = f32[1,2048,128]{2,1,0:T(8,128)} fusion(s32[1024]{0:T(1024)S(1)} %bitcast.85, s32[2048]{0:T(1024)S(1)} %bitcast.93, f32[1,2048,128]{2,1,0:T(8,128)} %get-tuple-element.167, pred[]{:T(512)S(6)} %compare.3, bf16[8,1,1024,128]{3,2,1,0:T(8,128)(2,1)} %get-tuple-element.182, s32[]{:T(128)} %get-tuple-element.166), kind=kOutput, calls=%fused_computation.14.clone.1 | convolution fusion | flops 539492352 | bytes 2372097 | tf_op jit(solution)/shard_map/vmap()/while/body/eval_jaxpr/dot_general | solution.py:29
  99.6 4.4 %fusion.53 = bf16[8,1,1024,128]{3,2,1,0:T(8,128)(2,1)} fusion(bf16[8,1,1024,128]{3,2,1,0:T(8,128)(2,1)} %get-tuple-element.168, s32[]{:T(128)} %get-tuple-element.166, s32[1024]{0:T(1024)S(1)} %bitcast.86, s32[2048]{0:T(1024)S(1)} %bitcast.94, bf16[1,2048,128]{2,1,0:T(8,128)(2,1)} %get-tuple-element.183), kind=kOutput, calls=%fused_computation.16.clone.1 | convolution fusion | flops 538968064 | bytes 1061376 | tf_op jit(solution)/shard_map/vmap()/while/body/eval_jaxpr/dot_general | solution.py:30
  106.4 3.6 %fusion.52 = f32[1,2048,128]{2,1,0:T(8,128)} fusion(s32[1024]{0:T(1024)S(1)} %bitcast.85, s32[2048]{0:T(1024)S(1)} %bitcast.93, f32[1,2048,128]{2,1,0:T(8,128)} %get-tuple-element.167, pred[]{:T(512)S(6)} %compare.3, bf16[8,1,1024,128]{3,2,1,0:T(8,128)(2,1)} %get-tuple-element.182, s32[]{:T(128)} %get-tuple-element.166), kind=kOutput, calls=%fused_computation.14.clone.1 | convolution fusion | flops 539492352 | bytes 2372097 | tf_op jit(solution)/shard_map/vmap()/while/body/eval_jaxpr/dot_general | solution.py:29
  110.0 4.5 %fusion.53 = bf16[8,1,1024,128]{3,2,1,0:T(8,128)(2,1)} fusion(bf16[8,1,1024,128]{3,2,1,0:T(8,128)(2,1)} %get-tuple-element.168, s32[]{:T(128)} %get-tuple-element.166, s32[1024]{0:T(1024)S(1)} %bitcast.86, s32[2048]{0:T(1024)S(1)} %bitcast.94, bf16[1,2048,128]{2,1,0:T(8,128)(2,1)} %get-tuple-element.183), kind=kOutput, calls=%fused_computation.16.clone.1 | convolution fusion | flops 538968064 | bytes 1061376 | tf_op jit(solution)/shard_map/vmap()/while/body/eval_jaxpr/dot_general | solution.py:30
  115.5 2.4 multiply_reduce_fusion
  117.9 4.2 %all-to-all-start.1 = ((bf16[16,128,128]{2,1,0:T(8,128)(2,1)}), bf16[16,128,128]{2,1,0:T(8,128)(2,1)}, u32[]{:S(2)}, u32[]{:S(2)}) async-start(bf16[16,128,128]{2,1,0:T(8,128)(2,1)} %bitcast.82), calls=%async_computation.1 | async-start | bytes 1048576 | tf_op jit(solution)/shard_map/all_to_all | solution.py:75
  122.1 74.6 %psum.15 = bf16[1,8192]{1,0:T(2,128)(2,1)S(1)} all-reduce(bf16[1,8192]{1,0:T(2,128)(2,1)S(1)} %bitcast.89), channel_id=1, replica_groups=mesh['dp'=16,'group'=16] {'dp'}, use_global_device_ids=true, to_apply=%region_6.7 | all-reduce | flops 8192 | bytes 32768 | tf_op jit(solution)/shard_map/psum | solution.py:66
  202.4 76.7 %all-reduce.2.cloned.1.call-done = bf16[1,8192,128]{2,1,0:T(8,128)(2,1)} async-done(((bf16[1,8192,128]{2,1,0:T(8,128)(2,1)}), bf16[1,8192,128]{2,1,0:T(8,128)(2,1)}) %all-reduce.2.cloned.1.call-update) | async-done | bytes 2097168 | tf_op jit(solution)/shard_map/psum | solution.py:65
  (66 shorter events, 31.0 us)
Async XLA Ops:
  7.2 9.1 %copy-start = (bf16[768,2048]{1,0:T(8,128)(2,1)S(1)}, bf16[768,2048]{1,0:T(8,128)(2,1)}, u32[]{:S(2)}) copy-start(bf16[768,2048]{1,0:T(8,128)(2,1)} %param.11) | copy-start | bytes 9437188
  8.3 7.9 %collective-permute-start = (bf16[1,256]{1,0:T(2,128)(2,1)S(1)}, bf16[1,256]{1,0:T(2,128)(2,1)S(1)}, u32[]{:S(2)}, u32[]{:S(2)}) collective-permute-start(bf16[1,256]{1,0:T(2,128)(2,1)S(1)} %slice_bitcast_fusion), channel_id=1, source_target_pairs={{0,1},{1,2},{2,3},{3,4},{4,5},{5,6},{6,7},{7,8},{8,9},{9,10},{10,1... | collective-permute-start | bytes 1544 | tf_op jit(solution)/shard_map/ppermute | solution.py:14
  16.3 16.7 %copy-start.4 = (s32[1,2048]{1,0:T(1,128)S(1)}, s32[1,2048]{1,0:T(1,128)}, u32[]{:S(2)}) copy-start(s32[1,2048]{1,0:T(1,128)} %param.12) | copy-start | bytes 24580
  17.8 15.1 %all-to-all-start = ((bf16[128,16,128]{2,0,1:T(8,128)(2,1)}), bf16[128,16,128]{2,0,1:T(8,128)(2,1)}, u32[]{:S(2)}, u32[]{:S(2)}) async-start(bf16[128,16,128]{2,0,1:T(8,128)(2,1)} %bitcast.81), calls=%async_computation | async-start | bytes 1048576 | tf_op jit(solution)/shard_map/all_to_all | solution.py:57
  22.1 257.0 %all-reduce.2.cloned.1.call-start = ((), (), s32[]{:S(2)}) async-start(), calls=%async_computation.2 | async-start | bytes 4194304 | tf_op jit(solution)/shard_map/psum | solution.py:65
  115.4 81.3 %copy-start.3 = (f32[1,512]{1,0:T(1,128)S(1)}, f32[1,512]{1,0:T(1,128)}, u32[]{:S(2)}) copy-start(f32[1,512]{1,0:T(1,128)} %param.16) | copy-start | bytes 6148
  117.9 79.5 %all-to-all-start.1 = ((bf16[16,128,128]{2,1,0:T(8,128)(2,1)}), bf16[16,128,128]{2,1,0:T(8,128)(2,1)}, u32[]{:S(2)}, u32[]{:S(2)}) async-start(bf16[16,128,128]{2,1,0:T(8,128)(2,1)} %bitcast.82), calls=%async_computation.1 | async-start | bytes 1048576 | tf_op jit(solution)/shard_map/all_to_all | solution.py:75
  122.1 157.0 %copy-start.1 = (f32[1,512,128]{2,1,0:T(8,128)S(1)}, f32[1,512,128]{2,1,0:T(8,128)}, u32[]{:S(2)}) copy-start(f32[1,512,128]{2,1,0:T(8,128)} %param.15) | copy-start | bytes 786436
  196.8 84.1 %copy-start.2 = (f32[1,512]{1,0:T(1,128)}, f32[1,512]{1,0:T(1,128)S(1)}, u32[]{:S(2)}) copy-start(f32[1,512]{1,0:T(1,128)S(1)} %fusion.36) | copy-start | bytes 6148
Sparse Core Ops, SparseCore 0:
  115.6 163.4 all-reduce.1
where the time goes:
time: 290 us; the launch traced here: 288 us
  waiting for transfers between devices  92.3 us (32%)
  blocking collectives  74.6 us (26%)
  matrix products  67.2 us (23%)
  other arithmetic  18.5 us (6%)
  between operations  14.2 us (5%)
  starting transfers between devices  10.5 us (4%)
  local copies, waits for them, and re-layouts  10 us (3%)
    psum x1, waiting for transfers between devices, body(): lax.psum(batch_sums.astype(jnp.bfloat16), 'dp').astype(jnp.float32)  76.7 us
    psum x1, blocking collectives, body(): lax.psum(batch_counts.astype(jnp.bfloat16), 'dp').astype(jnp.float32)  74.6 us
    dot_general x8, matrix products, one_block(): lax.dot_general(selector, grouped_rows, (((0,), (0,)), ((), ())), preferr...  35.6 us
    dot_general x8, matrix products, one_block(): jnp.dot(selector, tile_rows, preferred_element_type=jnp.float32)  28.7 us
    all_to_all x1, waiting for transfers between devices, body(): lax.all_to_all(latent, 'group', split_axis=1, concat_axis=0, tiled=True)  10.8 us
    reduce_sum x8, other arithmetic, one_block(): counts = jnp.sum(selector, axis=0, dtype=jnp.float32)  7.75 us
  transfers between devices with their start and end apart: 4, of which 3 were waited for; matrix products, arithmetic and copies ran while one was open for 3% of the time, Pallas kernels for 0%

commit v1 on v0

v1 whole, which is shorter than its diff:
```python
import functools

import jax
import jax.numpy as jnp
from jax import lax
from jax.experimental import pallas as pl
from jax.experimental.pallas import tpu as pltpu
from jax.sharding import PartitionSpec as P

ema_decay = 0.9

F32 = jnp.float32
BF16 = jnp.bfloat16
I32 = jnp.int32

LANES = 128
PARTS = 16
BLOCK = 192
CAP = 184
SHARE = 512

VMEM = pl.BlockSpec(memory_space=pltpu.VMEM)


def one_hot(condition):
    return jnp.where(condition, 1.0, 0.0).astype(BF16)


def iota(shape, axis):
    return lax.broadcasted_iota(I32, shape, axis)


def id_columns(ids_ref):
    rows = [ids_ref[0:1, c * LANES:(c + 1) * LANES] for c in range(PARTS)]
    return jnp.concatenate(rows, axis=0).T


def pick_kernel(ids_ref, book_ref, out_ref):
    columns = id_columns(ids_ref)
    lanes = iota((LANES, 1024), 1)
    step = 4
    for first in range(0, PARTS, step):
        ids = jnp.concatenate(
            [columns[:, c:c + 1] for c in range(first, first + step)], axis=0
        )
        low, top = ids & 1023, ids >> 10
        selector = jnp.concatenate(
            [one_hot(low[k * LANES:(k + 1) * LANES] == lanes) for k in range(step)], axis=0
        )
        picked = jnp.zeros((step * LANES, LANES), F32)
        for pair in range(4):
            begin = pair * 2048
            tile = jnp.concatenate(
                [book_ref[begin:begin + 1024, :], book_ref[begin + 1024:begin + 2048, :]], axis=1
            )
            both = jnp.dot(selector, tile, preferred_element_type=F32)
            picked = jnp.where(top == 2 * pair, both[:, :LANES], picked)
            picked = jnp.where(top == 2 * pair + 1, both[:, LANES:], picked)
        picked = picked.astype(BF16)
        for k in range(step):
            out_ref[first + k, LANES:, :] = picked[k * LANES:(k + 1) * LANES]


def encode_kernel(frames_ref, halo_ref, clips_ref, weight_ref, base_ref, out_ref):
    del base_ref
    frames = frames_ref[...]
    row, col = iota((LANES, 256), 0), iota((LANES, 256), 1)
    even = jnp.dot(one_hot(col == 2 * row), frames, preferred_element_type=F32)
    odd = jnp.dot(one_hot(col == 2 * row + 1), frames, preferred_element_type=F32)
    earlier = jnp.dot(one_hot(col == 2 * row - 1), frames, preferred_element_type=F32)
    earlier = jnp.where(row == 0, halo_ref[...].astype(F32), earlier)
    hits = jnp.where(iota((LANES, 8), 0) == clips_ref[...], 1.0, 0.0)
    starts = jnp.max(hits, axis=1, keepdims=True)
    earlier = jnp.where(starts > 0.0, 0.0, earlier)
    stacked = jnp.concatenate([earlier, even, odd], axis=1).astype(BF16)
    for pair in range(PARTS // 2):
        wide = jnp.dot(
            stacked, weight_ref[:, pair * 256:(pair + 1) * 256], preferred_element_type=F32
        ).astype(BF16)
        out_ref[2 * pair, :LANES, :] = wide[:, :LANES]
        out_ref[2 * pair + 1, :LANES, :] = wide[:, LANES:]


def route_kernel(round_ref, ids_ref, owned_ref, out_ref, total_ref):
    passed = round_ref[0, 0] * CAP
    dest_rows, tables = [], []
    sub16 = iota((PARTS, LANES), 0)
    for c in range(PARTS):
        dest = ids_ref[0:1, c * LANES:(c + 1) * LANES] >> 9
        dest_rows.append(dest)
        tables.append(jnp.where(sub16 == dest, 1.0, 0.0))
    upper = one_hot(iota((LANES, LANES), 0) <= iota((LANES, LANES), 1))
    cumulative = jnp.dot(
        jnp.concatenate(tables, axis=0).astype(BF16), upper, preferred_element_type=F32
    )
    offset = jnp.zeros((PARTS, 1), F32)
    place_rows = []
    for c in range(PARTS):
        inside = cumulative[c * PARTS:(c + 1) * PARTS]
        rank = jnp.sum(tables[c] * (inside + (offset - 1.0)), axis=0, keepdims=True)
        rank = rank.astype(I32) - passed
        kept = (rank >= 0) & (rank < CAP)
        place_rows.append(jnp.where(kept, (dest_rows[c] & 3) * BLOCK + rank, -1))
        offset = offset + inside[:, LANES - 1:]
    most = jnp.max(offset, axis=0, keepdims=True)
    need = jnp.ones((1, 1), F32)
    for k in range(1, 2048 // CAP + 1):
        need = need + jnp.where(most > float(k * CAP), 1.0, 0.0)

    columns = id_columns(ids_ref)
    lane = iota((LANES, LANES), 1)
    rows = iota((4 * BLOCK, LANES), 0)
    for pair in range(PARTS // 2):
        wides, selectors = [], []
        for c in (2 * pair, 2 * pair + 1):
            ids = columns[:, c:c + 1]
            quarter = ids >> 11
            code = ids & (SHARE - 1)
            latent = owned_ref[c, :LANES, :]
            zero = jnp.zeros_like(latent)
            pieces = [jnp.where(quarter == q, latent, zero) for q in range(4)]
            mark = jnp.where((lane & 1) == 1, code & 15, (code >> 4) + 1)
            mark = jnp.where((lane >> 3) == quarter, mark, 0)
            pieces.append(mark.astype(F32).astype(BF16))
            wides.append(jnp.concatenate(pieces, axis=1))
            selectors.append(one_hot(rows == place_rows[c]))
        part = jnp.dot(
            jnp.concatenate(selectors, axis=1), jnp.concatenate(wides, axis=0), preferred_element_type=F32
        )
        if pair == 0:
            total_ref[...] = part
        else:
            total_ref[...] += part

    row8 = iota((8, LANES), 0)
    for j in range(4):
        begin = j * BLOCK
        marks = total_ref[begin:begin + BLOCK, 512:640]
        first = marks[:LANES].T
        second = jnp.concatenate([marks[LANES:], jnp.zeros((2 * LANES - BLOCK, LANES), F32)], axis=0).T
        for q in range(4):
            meta = jnp.where(
                row8 < 2,
                first[8 * q:8 * q + 8],
                jnp.where(row8 < 4, second[8 * q:8 * q + 8], need),
            )
            data = total_ref[begin:begin + CAP, q * LANES:(q + 1) * LANES]
            out_ref[4 * q + j] = jnp.concatenate([data, meta], axis=0).astype(BF16)


def update_kernel(
    message_ref, held_ref, ema_sums_ref, ema_counts_ref, book_ref, counts_ref, kept_ref, need_ref
):
    codes = iota((SHARE, LANES), 0).astype(F32)
    ones = jnp.ones((2 * LANES, LANES), BF16)
    kept_ref[...] = held_ref[...]
    need = jnp.zeros((1, 1), F32)
    tails = []
    selectors, datas = [], []

    def flush():
        data = jnp.concatenate(datas, axis=0)
        kept_ref[...] += jnp.dot(
            jnp.concatenate(selectors, axis=1),
            jnp.concatenate([data, ones], axis=1),
            preferred_element_type=F32,
        )
        selectors.clear()
        datas.clear()

    for s in range(PARTS):
        meta = message_ref[s, BLOCK - 16:, :].astype(F32)[8:]
        code = (meta[0:1] - 1.0) * 16.0 + meta[1:2]
        need = jnp.maximum(need, meta[4:5, 0:1])
        tails.append((meta[2:3], meta[3:4]))
        selectors.append(one_hot(codes == code))
        datas.append(message_ref[s, :LANES, :])
        if len(datas) == 2:
            flush()
    for s in range(0, PARTS, 2):
        (high0, low0), (high1, low1) = tails[s], tails[s + 1]
        shift = 2 * LANES - BLOCK
        high = high0 + pltpu.roll(jnp.broadcast_to(high1, (8, LANES)), shift, 1)[0:1]
        low = low0 + pltpu.roll(jnp.broadcast_to(low1, (8, LANES)), shift, 1)[0:1]
        selectors.append(one_hot(codes == (high - 1.0) * 16.0 + low))
        datas.append(
            jnp.concatenate([message_ref[s, LANES:, :], message_ref[s + 1, LANES:, :]], axis=0)
        )
        if len(datas) == 2:
            flush()
    need_ref[0, 0] = jnp.max(need).astype(I32)
    diagonal = iota((LANES, LANES), 0) == iota((LANES, LANES), 1)
    for k in range(SHARE // LANES):
        begin = k * LANES
        old = jnp.broadcast_to(ema_counts_ref[0:1, begin:begin + LANES], (LANES, LANES)).T
        sums, counts = kept_ref[begin:begin + LANES, :LANES], kept_ref[begin:begin + LANES, LANES:]
        new_counts = ema_decay * old + (1.0 - ema_decay) * counts
        book_ref[begin:begin + LANES, :] = (
            ema_decay * ema_sums_ref[begin:begin + LANES, :] + (1.0 - ema_decay) * sums
        ) / new_counts
        counts_ref[0:1, begin:begin + LANES] = jnp.sum(
            jnp.where(diagonal, new_counts, 0.0), axis=0, keepdims=True
        )


def decode_kernel(got_ref, sent_ref, weight_ref, out_ref, error_ref):
    picked = jnp.concatenate([got_ref[g, LANES:, :] for g in range(PARTS)], axis=1)
    decoded = jnp.dot(picked, weight_ref[...], preferred_element_type=F32).astype(BF16)
    halves = jnp.concatenate([decoded[:, :256], decoded[:, 256:]], axis=0)
    row, col = iota((256, 256), 0), iota((256, 256), 1)
    source = (row >> 1) + (row & 1) * LANES
    out_ref[...] = jnp.dot(one_hot(col == source), halves, preferred_element_type=F32).astype(BF16)
    for c in range(PARTS):
        diff = got_ref[c, :LANES, :].astype(F32) - sent_ref[c, LANES:, :].astype(F32)
        error = jnp.sum((diff * diff).T, axis=0, keepdims=True) * (1.0 / LANES)
        error_ref[0:1, c * LANES:(c + 1) * LANES] = error


def call(kernel, out_shape, count, flops, size, scalars=0, scalar_out=False, scratch=(), aliases=None):
    in_specs = [pl.BlockSpec(memory_space=pltpu.SMEM)] * scalars + [VMEM] * (count - scalars)
    out_specs = jax.tree.map(lambda _: VMEM, out_shape)
    if scalar_out:
        out_specs = out_specs[:-1] + (pl.BlockSpec(memory_space=pltpu.SMEM),)
    return pl.pallas_call(
        kernel,
        out_shape=out_shape,
        in_specs=in_specs,
        out_specs=out_specs,
        scratch_shapes=list(scratch),
        input_output_aliases=aliases or {},
        cost_estimate=pl.CostEstimate(flops=flops, bytes_accessed=size, transcendentals=0),
        compiler_params=pltpu.CompilerParams(vmem_limit_bytes=40 << 20),
    )


def passed_along(shard, axis, by):
    size = lax.axis_size(axis)
    pairs = [(i, i + by) for i in range(size) if 0 <= i + by < size]
    return lax.ppermute(shard, axis, pairs)


def body(
    motion_frames, enc_weight, code_ids, clip_offsets, codebook, ema_sums, ema_counts, dec_weight
):
    shape = jax.ShapeDtypeStruct
    halo = passed_along(motion_frames[-1:], ("dp", "group"), 1)
    buffer = shape((PARTS, 2 * LANES, LANES), BF16)
    picked = call(pick_kernel, buffer, 2, 4 << 30, 4 << 20)(code_ids, codebook[0])
    sent = call(encode_kernel, buffer, 5, 400 << 20, 4 << 20, aliases={4: 0})(
        motion_frames, halo, clip_offsets, enc_weight, picked
    )
    got = lax.all_to_all(sent, "group", split_axis=0, concat_axis=0)

    def one_round(index, held):
        message = call(
            route_kernel, shape((PARTS, BLOCK, LANES), BF16), 3, 2 << 30, 2 << 20, scalars=1,
            scratch=[pltpu.VMEM((4 * BLOCK, 5 * LANES), F32)],
        )(index.reshape(1, 1), code_ids, got)
        arrived = lax.all_to_all(message, "dp", split_axis=0, concat_axis=0)
        return call(
            update_kernel,
            (
                shape((SHARE, LANES), F32),
                shape((1, SHARE), F32),
                shape((SHARE, 2 * LANES), F32),
                shape((1, 1), I32),
            ),
            4, 800 << 20, 2 << 20, scalar_out=True,
        )(arrived, held, ema_sums[0], ema_counts)

    decoded, commit_error = call(
        decode_kernel,
        (shape((256, 256), BF16), shape((1, PARTS * LANES), F32)),
        3, 300 << 20, 4 << 20,
    )(got, sent, dec_weight)

    first = one_round(jnp.zeros((), I32), jnp.zeros((SHARE, 2 * LANES), F32))

    def more(state):
        return state[0] < state[4][0, 0]

    def again(state):
        index, _, _, held, _ = state
        return (index + 1, *one_round(index, held))

    _, new_codebook, new_counts, _, _ = lax.while_loop(more, again, (jnp.ones((), I32), *first))
    return (decoded, commit_error, new_codebook[None], new_counts)


def solution(mesh):
    return jax.shard_map(
        body,
        mesh=mesh,
        in_specs=(
            P(("dp", "group"), None),
            P(),
            P("group", "dp"),
            P(("dp", "group"), None),
            P("group", None, None),
            P("group", "dp", None),
            P("group", "dp"),
            P(),
        ),
        out_specs=(
            P(("dp", "group"), None),
            P("group", "dp"),
            P("group", "dp", None),
            P("group", "dp"),
        ),
        check_vma=False,
    )
```

time: 290 us -> 76.5 us (0.26)
  waiting for transfers between devices: 92.3 us -> 19.3 us
  matrix products: 67.2 us -> 0 us
  blocking collectives: 74.6 us -> 22.9 us
  other arithmetic: 18.5 us -> 0 us
  Pallas kernels: 0 us -> 15.4 us
  between operations: 14.2 us -> 0.93 us
  local copies, waits for them, and re-layouts: 10 us -> 4.23 us
    psum x1 -> x0, waiting for transfers between devices: 76.7 us -> none  [body(): lax.psum(batch_sums.astype(jnp.bfloat16), 'dp').astype(jnp.float32)]
    psum x1 -> x0, blocking collectives: 74.6 us -> none  [body(): lax.psum(batch_counts.astype(jnp.bfloat16), 'dp').astype(jnp.float32)]
    dot_general x18 -> x0, matrix products: 67.2 us -> none  [the longest x8 35.6 us: one_block(): lax.dot_general(selector, grouped_rows, (((0,), (0,)), ((), ())), preferr...]
    all_to_all x0 -> x1, blocking collectives: none -> 22.9 us  [body(): got = lax.all_to_all(sent, 'group', split_axis=0, concat_axis=0)]
    pallas_call x0 -> x5, Pallas kernels: none -> 15.4 us  [the longest x1 5.7 us: body(): call(pick_kernel, buffer, 2, 4 << 30, 4 << 20)(code_ids, codebook[0])]
    reduce_sum x9 -> x0, other arithmetic: 10.2 us -> none  [the longest x8 7.75 us: one_block(): counts = jnp.sum(selector, axis=0, dtype=jnp.float32)]
    all_to_all x2 -> x1, waiting for transfers between devices: 10.8 us -> 19.3 us  [one_round(): arrived = lax.all_to_all(message, 'dp', split_axis=0, concat_axis=0)]
    add x9 -> x0, other arithmetic: 5.21 us -> none  [the longest x8 5.2 us: one_block(): selector = (indices[:, None] == first + columns).astype(jnp.bfloat16)]
  transfers between devices with their start and end apart: 4 -> 2, of which waited for: 3 -> 1; matrix products, arithmetic and copies ran while one was open for 3% -> 0% of each run, Pallas kernels for 0% -> 11%
where the time goes in v1:
time: 76.5 us; the launch traced here: 76.1 us
  blocking collectives  22.9 us (30%)
  waiting for transfers between devices  19.3 us (25%)
  Pallas kernels  15.4 us (20%)
  starting transfers between devices  12.6 us (16%)
  local copies, waits for them, and re-layouts  4.23 us (6%)
  between operations  0.93 us (1%)
  loops' own time  0.81 us (1%)
    all_to_all x1, blocking collectives, body(): got = lax.all_to_all(sent, 'group', split_axis=0, concat_axis=0)  22.9 us
    all_to_all x1, waiting for transfers between devices, one_round(): arrived = lax.all_to_all(message, 'dp', split_axis=0, concat_axis=0)  19.3 us
    all_to_all x1, starting transfers between devices, one_round(): arrived = lax.all_to_all(message, 'dp', split_axis=0, concat_axis=0)  10.7 us
    pallas_call x1, Pallas kernels, body(): call(pick_kernel, buffer, 2, 4 << 30, 4 << 20)(code_ids, codebook[0])  5.7 us
    pallas_call x1, Pallas kernels, one_round(): call(route_kernel, shape((PARTS, BLOCK, LANES), BF16), 3, 2 << 30, 2 << 2...  3.51 us
    unnamed x22, local copies, waits for them, and re-layouts  3.5 us
    pallas_call x1, Pallas kernels, one_round(): call(update_kernel, (shape((SHARE, LANES), F32), shape((1, SHARE), F32),...  2.84 us
    pallas_call x1, Pallas kernels, body(): call(decode_kernel, (shape((256, 256), BF16), shape((1, PARTS * LANES), F...  2.59 us
  transfers between devices with their start and end apart: 2, of which 1 were waited for; matrix products, arithmetic and copies ran while one was open for 0% of the time, Pallas kernels for 11%

profile of v1, /device:TPU:32, one launch (start us, length us, event | category | flops | bytes accessed | tf_op | source)
XLA Modules:
  0.0 76.1 jit_solution(5273447819488186567)
XLA Ops:
  0.6 0.7 slice.3
  1.3 1.9 %collective-permute-start = (bf16[1,256]{1,0:T(2,128)(2,1)S(1)}, bf16[1,256]{1,0:T(2,128)(2,1)S(1)}, u32[]{:S(2)}, u32[]{:S(2)}) collective-permute-start(bf16[1,256]{1,0:T(2,128)(2,1)S(1)} %slice.3), channel_id=1, source_target_pairs={{0,1},{1,2},{2,3},{3,4},{4,5},{5,6},{6,7},{7,8},{8,9},{9,10},{10,1... | collective-permute-start | bytes 1544 | tf_op jit(solution)/shard_map/ppermute | solution.py:239
  3.2 0.0 copy-start.5
  3.3 1.6 %copy-done.5 = bf16[1,8192,128]{2,1,0:T(8,128)(2,1)S(1)} copy-done((bf16[1,8192,128]{2,1,0:T(8,128)(2,1)S(1)}, bf16[1,8192,128]{2,1,0:T(8,128)(2,1)}, u32[]{:S(2)}) %copy-start.5) | copy-done | bytes 2097176
  4.8 5.7 %shard_map.111.base_ref = bf16[16,256,128]{2,1,0:T(8,128)(2,1)S(1)} custom-call(s32[1,2048]{1,0:T(1,128)} %ids_ref.3, bf16[8192,128]{1,0:T(8,128)(2,1)S(1)} %bitcast.11), custom_call_target="tpu_custom_call" | custom-call | flops 4294967296 | bytes 4194304 | tf_op jit(solution)/shard_map/pallas_call | solution.py:248
  10.5 0.0 collective-permute-done.halo_ref
  10.6 0.0 copy-done
  10.6 0.0 copy-done.3
  10.6 0.0 copy-done.4
  10.6 0.8 %shard_map.112.sent_ref = bf16[16,256,128]{2,1,0:T(8,128)(2,1)S(1)} custom-call(bf16[256,256]{1,0:T(8,128)(2,1)S(1)} %copy-done.3, bf16[1,256]{1,0:T(2,128)(2,1)S(1)} %collective-permute-done.halo_ref, s32[1,8]{1,0:T(1,128)S(1)} %copy-done.4, bf16[768,2048]{1,0:T(8,128)(2,1)S(1)} %copy-done, ...), custom_call_target="tpu_custom_call", output_to_operand_aliasing={{}: (4, {})} | custom-call | flops 419430400 | bytes 4194304 | tf_op jit(solution)/shard_map/pallas_call | solution.py:249
  11.4 0.0 copy-start.9
  11.4 22.9 %all_to_all.16.got_ref.owned_ref = bf16[16,256,128]{2,1,0:T(8,128)(2,1)S(1)} all-to-all(bf16[16,256,128]{2,1,0:T(8,128)(2,1)S(1)} %shard_map.112.sent_ref), channel_id=1, replica_groups=mesh['dp'=16,'group'=16] {'group'}, dimensions={0} | all-to-all | bytes 2097152 | tf_op jit(solution)/shard_map/all_to_all | solution.py:252
  34.2 1.0 %copy-done.6 = bf16[16,256,128]{2,1,0:T(8,128)(2,1)} copy-done((bf16[16,256,128]{2,1,0:T(8,128)(2,1)}, bf16[16,256,128]{2,1,0:T(8,128)(2,1)S(1)}, u32[]{:S(2)}) %copy-start.6) | copy-done | bytes 1048600
  35.2 0.0 copy-done.9
  35.2 3.5 %shard_map.114 = bf16[16,192,128]{2,1,0:T(8,128)(2,1)S(1)} custom-call(s32[1,1]{1,0:T(1,128)} %constant.2.clone.1.round_ref, s32[1,2048]{1,0:T(1,128)S(1)} %copy-done.9, bf16[16,256,128]{2,1,0:T(8,128)(2,1)S(1)} %all_to_all.16.got_ref.owned_ref), custom_call_target="tpu_custom_call" | custom-call | flops 2147483648 | bytes 2097152 | tf_op jit(solution)/shard_map/pallas_call | solution.py:255
  38.8 0.9 %copy-done.2 = bf16[16,192,128]{2,1,0:T(8,128)(2,1)} copy-done((bf16[16,192,128]{2,1,0:T(8,128)(2,1)}, bf16[16,192,128]{2,1,0:T(8,128)(2,1)S(1)}, u32[]{:S(2)}) %copy-start.2) | copy-done | bytes 786456
  39.6 10.7 %all-to-all-start.2 = ((bf16[16,192,128]{2,1,0:T(8,128)(2,1)}), bf16[16,192,128]{2,1,0:T(8,128)(2,1)}, u32[]{:S(2)}, u32[]{:S(2)}) async-start(bf16[16,192,128]{2,1,0:T(8,128)(2,1)} %copy-done.2), calls=%async_computation.2 | async-start | bytes 1572864 | tf_op jit(solution)/shard_map/all_to_all | solution.py:259
  50.3 0.0 copy-done.1
  50.3 0.0 copy-start.8
  50.3 0.0 copy-start.10
  50.3 2.6 %shard_map.113 = (bf16[256,256]{1,0:T(8,128)(2,1)}, f32[1,2048]{1,0:T(1,128)}) custom-call(bf16[16,256,128]{2,1,0:T(8,128)(2,1)} %copy-done.6, bf16[16,256,128]{2,1,0:T(8,128)(2,1)S(1)} %shard_map.112.sent_ref, bf16[2048,512]{1,0:T(8,128)(2,1)S(1)} %copy-done.1), custom_call_target="tpu_custom_call" | custom-call | flops 314572800 | bytes 4194304 | tf_op jit(solution)/shard_map/pallas_call | solution.py:271
  52.9 19.3 %all-to-all-done.2.message_ref = bf16[16,192,128]{2,1,0:T(8,128)(2,1)} async-done(((bf16[16,192,128]{2,1,0:T(8,128)(2,1)}), bf16[16,192,128]{2,1,0:T(8,128)(2,1)}, u32[]{:S(2)}, u32[]{:S(2)}) %all-to-all-start.2) | async-done | bytes 786464 | tf_op jit(solution)/shard_map/all_to_all | solution.py:259
  72.2 2.8 %shard_map.115 = (f32[512,128]{1,0:T(8,128)}, f32[1,512]{1,0:T(1,128)}, f32[512,256]{1,0:T(8,128)S(1)}, s32[1,1]{1,0:T(1,128)}) custom-call(bf16[16,192,128]{2,1,0:T(8,128)(2,1)} %all-to-all-done.2.message_ref, f32[512,256]{1,0:T(8,128)S(1)} %broadcast_in_dim.6.held_ref, f32[512,128]{1,0:T(8,128)S(1)} %bitcast.12, f32[1,512]{1,0:T(1,128)S(1)} %copy-done.10), custom_call_target="tpu_custom_call" | custom-call | flops 838860800 | bytes 2097152 | tf_op jit(solution)/shard_map/pallas_call | solution.py:260
  75.1 0.8 %while.16 = (s32[]{:T(128)}, f32[512,128]{1,0:T(8,128)}, f32[1,512]{1,0:T(1,128)}, f32[512,256]{1,0:T(8,128)S(1)}, s32[1,1]{1,0:T(1,128)}, /*index=5*/s32[1,2048...) while((s32[]{:T(128)}, f32[512,128]{1,0:T(8,128)}, ...), condition=%wide.region_1.0_spmd, body=%wide.region_0.0_spmd.sunk | while | flops 2986344448 | bytes 7602309 | solution.py:286
  (11 shorter events, 0.1 us)
Async XLA Ops:
  1.3 9.2 %collective-permute-start = (bf16[1,256]{1,0:T(2,128)(2,1)S(1)}, bf16[1,256]{1,0:T(2,128)(2,1)S(1)}, u32[]{:S(2)}, u32[]{:S(2)}) collective-permute-start(bf16[1,256]{1,0:T(2,128)(2,1)S(1)} %slice.3), channel_id=1, source_target_pairs={{0,1},{1,2},{2,3},{3,4},{4,5},{5,6},{6,7},{7,8},{8,9},{9,10},{10,1... | collective-permute-start | bytes 1544 | tf_op jit(solution)/shard_map/ppermute | solution.py:239
  3.2 1.6 %copy-start.5 = (bf16[1,8192,128]{2,1,0:T(8,128)(2,1)S(1)}, bf16[1,8192,128]{2,1,0:T(8,128)(2,1)}, u32[]{:S(2)}) copy-start(bf16[1,8192,128]{2,1,0:T(8,128)(2,1)} %param.14) | copy-start | bytes 6291460
  4.8 5.7 %copy-start = (bf16[768,2048]{1,0:T(8,128)(2,1)S(1)}, bf16[768,2048]{1,0:T(8,128)(2,1)}, u32[]{:S(2)}) copy-start(bf16[768,2048]{1,0:T(8,128)(2,1)} %weight_ref.2) | copy-start | bytes 9437188
  4.8 5.7 %copy-start.3 = (bf16[256,256]{1,0:T(8,128)(2,1)S(1)}, bf16[256,256]{1,0:T(8,128)(2,1)}, u32[]{:S(2)}) copy-start(bf16[256,256]{1,0:T(8,128)(2,1)} %frames_ref.1) | copy-start | bytes 393220
  4.8 5.7 %copy-start.4 = (s32[1,8]{1,0:T(1,128)S(1)}, s32[1,8]{1,0:T(1,128)}, u32[]{:S(2)}) copy-start(s32[1,8]{1,0:T(1,128)} %clips_ref.1) | copy-start | bytes 100
  11.4 23.9 %copy-start.9 = (s32[1,2048]{1,0:T(1,128)S(1)}, s32[1,2048]{1,0:T(1,128)}, u32[]{:S(2)}) copy-start(s32[1,2048]{1,0:T(1,128)} %ids_ref.3) | copy-start | bytes 24580
  34.2 1.0 %copy-start.6 = (bf16[16,256,128]{2,1,0:T(8,128)(2,1)}, bf16[16,256,128]{2,1,0:T(8,128)(2,1)S(1)}, u32[]{:S(2)}) copy-start(bf16[16,256,128]{2,1,0:T(8,128)(2,1)S(1)} %all_to_all.16.got_ref.owned_ref) | copy-start | bytes 3145732
  35.2 15.1 %copy-start.1 = (bf16[2048,512]{1,0:T(8,128)(2,1)S(1)}, bf16[2048,512]{1,0:T(8,128)(2,1)}, u32[]{:S(2)}) copy-start(bf16[2048,512]{1,0:T(8,128)(2,1)} %weight_ref.3) | copy-start | bytes 6291460
  38.7 0.9 %copy-start.2 = (bf16[16,192,128]{2,1,0:T(8,128)(2,1)}, bf16[16,192,128]{2,1,0:T(8,128)(2,1)S(1)}, u32[]{:S(2)}) copy-start(bf16[16,192,128]{2,1,0:T(8,128)(2,1)S(1)} %shard_map.114) | copy-start | bytes 2359300
  39.6 32.5 %all-to-all-start.2 = ((bf16[16,192,128]{2,1,0:T(8,128)(2,1)}), bf16[16,192,128]{2,1,0:T(8,128)(2,1)}, u32[]{:S(2)}, u32[]{:S(2)}) async-start(bf16[16,192,128]{2,1,0:T(8,128)(2,1)} %copy-done.2), calls=%async_computation.2 | async-start | bytes 1572864 | tf_op jit(solution)/shard_map/all_to_all | solution.py:259
  50.3 21.9 %copy-start.8 = (f32[1,512,128]{2,1,0:T(8,128)S(1)}, f32[1,512,128]{2,1,0:T(8,128)}, u32[]{:S(2)}) copy-start(f32[1,512,128]{2,1,0:T(8,128)} %param.15) | copy-start | bytes 786436
  50.3 21.9 %copy-start.10 = (f32[1,512]{1,0:T(1,128)S(1)}, f32[1,512]{1,0:T(1,128)}, u32[]{:S(2)}) copy-start(f32[1,512]{1,0:T(1,128)} %ema_counts_ref.1) | copy-start | bytes 6148
  52.9 22.2 %copy-start.7 = (bf16[16,256,128]{2,1,0:T(8,128)(2,1)S(1)}, bf16[16,256,128]{2,1,0:T(8,128)(2,1)}, u32[]{:S(2)}) copy-start(bf16[16,256,128]{2,1,0:T(8,128)(2,1)} %copy-done.6) | copy-start | bytes 3145732

commit v2 on v1

--- a/solution.py
+++ b/solution.py
@@ -20,6 +20,7 @@
 SHARE = 512
 
 VMEM = pl.BlockSpec(memory_space=pltpu.VMEM)
+IN_HBM = pl.BlockSpec(memory_space=pltpu.HBM)
 
 
 def one_hot(condition):
@@ -35,8 +36,18 @@
     return jnp.concatenate(rows, axis=0).T
 
 
-def pick_kernel(ids_ref, book_ref, out_ref):
-    columns = id_columns(ids_ref)
+def relative_blocks(place_ref):
+    x, y, core = place_ref[0], place_ref[1], place_ref[2]
+    return [
+        ((x ^ dx) * 4 + ((y + dy) & 3)) * 2 + (core ^ dc)
+        for dx in range(2) for dc in range(2) for dy in range(4)
+    ]
+
+
+def pick_kernel(place_ref, ids_ref, book_ref, near_ref, far_ref, beside_ref):
+    blocks = relative_blocks(place_ref)
+    rows = [ids_ref[0:1, pl.ds(pl.multiple_of(b * LANES, LANES), LANES)] for b in blocks]
+    columns = jnp.concatenate(rows, axis=0).T
     lanes = iota((LANES, 1024), 1)
     step = 4
     for first in range(0, PARTS, step):
@@ -58,30 +69,70 @@
             picked = jnp.where(top == 2 * pair + 1, both[:, LANES:], picked)
         picked = picked.astype(BF16)
         for k in range(step):
-            out_ref[first + k, LANES:, :] = picked[k * LANES:(k + 1) * LANES]
-
-
-def encode_kernel(frames_ref, halo_ref, clips_ref, weight_ref, base_ref, out_ref):
-    del base_ref
+            out_ref = (near_ref, far_ref, beside_ref)[min(first // 4, 2)]
+            out_ref[(first + k) % (4 if first < 8 else 8)] = picked[k * LANES:(k + 1) * LANES]
+
+
+def encode_kernel(
+    frames_ref, clips_ref, weight_hbm, out_ref, head_ref, first_ref, weight_ref, stage_ref, in_sems, sems
+):
+    def strip(pair):
+        columns = pl.ds(pair * 256, 256)
+        return pltpu.make_async_copy(
+            weight_hbm.at[:, columns], weight_ref.at[:, columns], in_sems.at[pair]
+        )
+
+    for pair in range(PARTS // 2):
+        strip(pair).start()
     frames = frames_ref[...]
     row, col = iota((LANES, 256), 0), iota((LANES, 256), 1)
     even = jnp.dot(one_hot(col == 2 * row), frames, preferred_element_type=F32)
     odd = jnp.dot(one_hot(col == 2 * row + 1), frames, preferred_element_type=F32)
     earlier = jnp.dot(one_hot(col == 2 * row - 1), frames, preferred_element_type=F32)
-    earlier = jnp.where(row == 0, halo_ref[...].astype(F32), earlier)
     hits = jnp.where(iota((LANES, 8), 0) == clips_ref[...], 1.0, 0.0)
     starts = jnp.max(hits, axis=1, keepdims=True)
     earlier = jnp.where(starts > 0.0, 0.0, earlier)
     stacked = jnp.concatenate([earlier, even, odd], axis=1).astype(BF16)
     for pair in range(PARTS // 2):
+        strip(pair).wait()
         wide = jnp.dot(
             stacked, weight_ref[:, pair * 256:(pair + 1) * 256], preferred_element_type=F32
-        ).astype(BF16)
-        out_ref[2 * pair, :LANES, :] = wide[:, :LANES]
-        out_ref[2 * pair + 1, :LANES, :] = wide[:, LANES:]
-
-
-def route_kernel(round_ref, ids_ref, owned_ref, out_ref, total_ref):
+        )
+        first_ref[:, pair * 256:(pair + 1) * 256] = wide[:1]
+        wide = wide.astype(BF16)
+        for g, block in ((2 * pair, wide[:, :LANES]), (2 * pair + 1, wide[:, LANES:])):
+            stage_ref[g] = block
+            head_ref[g] = block[:16]
+            pltpu.make_async_copy(stage_ref.at[g], out_ref.at[g], sems.at[g]).start()
+    for g in range(PARTS):
+        pltpu.make_async_copy(stage_ref.at[g], out_ref.at[g], sems.at[g]).wait()
+
+
+def halo_kernel(
+    halo_ref, clips_ref, head_ref, first_ref, weight_hbm, sent_ref, out_ref, weight_ref, stage_ref, in_sem, sem
+):
+    del sent_ref
+    loaded = pltpu.make_async_copy(weight_hbm.at[pl.ds(0, 256), :], weight_ref, in_sem)
+    loaded.start()
+    starts = jnp.max(jnp.where(clips_ref[...] == 0, 1.0, 0.0), axis=1, keepdims=True)
+    halo = jnp.where(starts > 0.0, 0.0, halo_ref[...].astype(F32))
+    halo = jnp.broadcast_to(halo, (16, 256)).astype(BF16)
+    loaded.wait()
+    added = jnp.dot(halo, weight_ref[...], preferred_element_type=F32)
+    whole = (added + first_ref[...]).astype(BF16)
+    row = iota((16, LANES), 0)
+    for g in range(PARTS):
+        stage_ref[g] = jnp.where(row == 0, whole[:, g * LANES:(g + 1) * LANES], head_ref[g])
+    copy = pltpu.make_async_copy(stage_ref, out_ref.at[:, pl.ds(0, 16), :], sem)
+    copy.start()
+    copy.wait()
+
+
+def route_kernel(
+    round_ref, ids_ref, got_ref, out_ref, total_ref, owned_ref, stage_ref, sems, got_sem
+):
+    loaded = pltpu.make_async_copy(got_ref, owned_ref, got_sem)
+    loaded.start()
     passed = round_ref[0, 0] * CAP
     dest_rows, tables = [], []
     sub16 = iota((PARTS, LANES), 0)
@@ -110,13 +161,14 @@
     columns = id_columns(ids_ref)
     lane = iota((LANES, LANES), 1)
     rows = iota((4 * BLOCK, LANES), 0)
+    loaded.wait()
     for pair in range(PARTS // 2):
         wides, selectors = [], []
         for c in (2 * pair, 2 * pair + 1):
             ids = columns[:, c:c + 1]
             quarter = ids >> 11
             code = ids & (SHARE - 1)
-            latent = owned_ref[c, :LANES, :]
+            latent = owned_ref[c]
             zero = jnp.zeros_like(latent)
             pieces = [jnp.where(quarter == q, latent, zero) for q in range(4)]
             mark = jnp.where((lane & 1) == 1, code & 15, (code >> 4) + 1)
@@ -145,7 +197,11 @@
                 jnp.where(row8 < 4, second[8 * q:8 * q + 8], need),
             )
             data = total_ref[begin:begin + CAP, q * LANES:(q + 1) * LANES]
-            out_ref[4 * q + j] = jnp.concatenate([data, meta], axis=0).astype(BF16)
+            to = 4 * q + j
+            stage_ref[to] = jnp.concatenate([data, meta], axis=0).astype(BF16)
+            pltpu.make_async_copy(stage_ref.at[to], out_ref.at[to], sems.at[to]).start()
+    for to in range(PARTS):
+        pltpu.make_async_copy(stage_ref.at[to], out_ref.at[to], sems.at[to]).wait()
 
 
 def update_kernel(
@@ -203,33 +259,51 @@
         )
 
 
-def decode_kernel(got_ref, sent_ref, weight_ref, out_ref, error_ref):
-    picked = jnp.concatenate([got_ref[g, LANES:, :] for g in range(PARTS)], axis=1)
-    decoded = jnp.dot(picked, weight_ref[...], preferred_element_type=F32).astype(BF16)
+def gather_kernel(near_ref, far_ref, beside_ref, across_ref, *out_refs):
+    for k, ref in enumerate((near_ref, far_ref, beside_ref, across_ref)):
+        for dy in range(1, 4):
+            out_refs[dy - 1][k] = ref[dy]
+
+
+def decode_kernel(
+    place_ref, near_ref, far_ref, beside_ref, across_ref, y1_ref, y2_ref, y3_ref, weight_ref, out_ref
+):
+    groups = relative_blocks(place_ref)
+    slabs, weights = [], []
+    for dy in range(4):
+        for k, ref in enumerate((near_ref, far_ref, beside_ref, across_ref)):
+            group = groups[4 * k + (4 - dy) % 4]
+            slabs.append(ref[0] if dy == 0 else (y1_ref, y2_ref, y3_ref)[dy - 1][k])
+            weights.append(weight_ref[pl.ds(pl.multiple_of(group * LANES, LANES), LANES), :])
+    decoded = jnp.dot(
+        jnp.concatenate(slabs, axis=1), jnp.concatenate(weights, axis=0), preferred_element_type=F32
+    ).astype(BF16)
     halves = jnp.concatenate([decoded[:, :256], decoded[:, 256:]], axis=0)
     row, col = iota((256, 256), 0), iota((256, 256), 1)
     source = (row >> 1) + (row & 1) * LANES
     out_ref[...] = jnp.dot(one_hot(col == source), halves, preferred_element_type=F32).astype(BF16)
-    for c in range(PARTS):
-        diff = got_ref[c, :LANES, :].astype(F32) - sent_ref[c, LANES:, :].astype(F32)
+
+
+def error_kernel(place_ref, got_ref, near_ref, far_ref, beside_ref, error_ref):
+    for k, block in enumerate(relative_blocks(place_ref)):
+        picked = (near_ref, far_ref)[k // 4][k % 4] if k < 8 else beside_ref[k - 8]
+        diff = got_ref[block].astype(F32) - picked.astype(F32)
         error = jnp.sum((diff * diff).T, axis=0, keepdims=True) * (1.0 / LANES)
-        error_ref[0:1, c * LANES:(c + 1) * LANES] = error
-
-
-def call(kernel, out_shape, count, flops, size, scalars=0, scalar_out=False, scratch=(), aliases=None):
+        error_ref[0:1, pl.ds(pl.multiple_of(block * LANES, LANES), LANES)] = error
+
+
+def call(kernel, out_shape, count, flops, size, scalars=0, hbm_in=0, out_specs=None, scratch=(), aliases=None, limit=40):
     in_specs = [pl.BlockSpec(memory_space=pltpu.SMEM)] * scalars + [VMEM] * (count - scalars)
-    out_specs = jax.tree.map(lambda _: VMEM, out_shape)
-    if scalar_out:
-        out_specs = out_specs[:-1] + (pl.BlockSpec(memory_space=pltpu.SMEM),)
+    in_specs[count - hbm_in:] = [IN_HBM] * hbm_in
     return pl.pallas_call(
         kernel,
         out_shape=out_shape,
         in_specs=in_specs,
-        out_specs=out_specs,
+        out_specs=out_specs or jax.tree.map(lambda _: VMEM, out_shape),
         scratch_shapes=list(scratch),
         input_output_aliases=aliases or {},
         cost_estimate=pl.CostEstimate(flops=flops, bytes_accessed=size, transcendentals=0),
-        compiler_params=pltpu.CompilerParams(vmem_limit_bytes=40 << 20),
+        compiler_params=pltpu.CompilerParams(vmem_limit_bytes=limit << 20),
     )
 
 
@@ -239,23 +313,70 @@
     return lax.ppermute(shard, axis, pairs)
 
 
+def moved(shard, dx, dy, dc):
+    pairs = [
+        ((x * 4 + y) * 2 + c, ((x ^ dx) * 4 + (y + dy) % 4) * 2 + (c ^ dc))
+        for x in range(2) for y in range(4) for c in range(2)
+    ]
+    return lax.ppermute(shard, "group", pairs)
+
+
 def body(
     motion_frames, enc_weight, code_ids, clip_offsets, codebook, ema_sums, ema_counts, dec_weight
 ):
     shape = jax.ShapeDtypeStruct
+    me = lax.axis_index("group").astype(I32)
+    place = jnp.stack([me >> 3, (me >> 1) & 3, me & 1])
     halo = passed_along(motion_frames[-1:], ("dp", "group"), 1)
-    buffer = shape((PARTS, 2 * LANES, LANES), BF16)
-    picked = call(pick_kernel, buffer, 2, 4 << 30, 4 << 20)(code_ids, codebook[0])
-    sent = call(encode_kernel, buffer, 5, 400 << 20, 4 << 20, aliases={4: 0})(
-        motion_frames, halo, clip_offsets, enc_weight, picked
+    blocks = shape((PARTS, LANES, LANES), BF16)
+    four, eight = shape((4, LANES, LANES), BF16), shape((8, LANES, LANES), BF16)
+    started, head, row = call(
+        encode_kernel,
+        (blocks, shape((PARTS, 16, LANES), BF16), shape((1, PARTS * LANES), F32)),
+        3, 400 << 20, 4 << 20, hbm_in=1, limit=60,
+        out_specs=(IN_HBM, VMEM, VMEM),
+        scratch=[
+            pltpu.VMEM(enc_weight.shape, BF16),
+            pltpu.VMEM(blocks.shape, BF16),
+            pltpu.SemaphoreType.DMA((PARTS // 2,)),
+            pltpu.SemaphoreType.DMA((PARTS,)),
+        ],
+    )(motion_frames, clip_offsets, enc_weight)
+    sent = call(
+        halo_kernel, blocks, 6, 20 << 20, 1 << 20, hbm_in=2, limit=60, out_specs=IN_HBM, aliases={5: 0},
+        scratch=[
+            pltpu.VMEM((256, enc_weight.shape[1]), BF16),
+            pltpu.VMEM((PARTS, 16, LANES), BF16),
+            pltpu.SemaphoreType.DMA,
+            pltpu.SemaphoreType.DMA,
+        ],
+    )(halo, clip_offsets, head, row, enc_weight, started)
+    sent, late_ids = lax.optimization_barrier((sent, code_ids))
+    near, far, beside = call(pick_kernel, (four, four, eight), 3, 4 << 30, 4 << 20, scalars=1)(
+        place, late_ids, codebook[0]
     )
     got = lax.all_to_all(sent, "group", split_axis=0, concat_axis=0)
-
-    def one_round(index, held):
-        message = call(
-            route_kernel, shape((PARTS, BLOCK, LANES), BF16), 3, 2 << 30, 2 << 20, scalars=1,
-            scratch=[pltpu.VMEM((4 * BLOCK, 5 * LANES), F32)],
+    commit_error = call(
+        error_kernel, shape((1, PARTS * LANES), F32), 5, 1 << 20, 1 << 20, scalars=1
+    )(place, got, near, far, beside)
+
+    from_x = moved(beside, 1, 0, 0)
+    from_core = moved(far, 0, 0, 1)
+
+    def route(index):
+        message = shape((PARTS, BLOCK, LANES), BF16)
+        return call(
+            route_kernel, message, 3, 2 << 30, 2 << 20, scalars=1, hbm_in=1, out_specs=IN_HBM, limit=60,
+            scratch=[
+                pltpu.VMEM((4 * BLOCK, 5 * LANES), F32),
+                pltpu.VMEM(blocks.shape, BF16),
+                pltpu.VMEM(message.shape, BF16),
+                pltpu.SemaphoreType.DMA((PARTS,)),
+                pltpu.SemaphoreType.DMA,
+            ],
         )(index.reshape(1, 1), code_ids, got)
+
+    def one_round(message, held):
         arrived = lax.all_to_all(message, "dp", split_axis=0, concat_axis=0)
         return call(
             update_kernel,
@@ -265,23 +386,26 @@
                 shape((SHARE, 2 * LANES), F32),
                 shape((1, 1), I32),
             ),
-            4, 800 << 20, 2 << 20, scalar_out=True,
+            4, 800 << 20, 2 << 20,
+            out_specs=(VMEM, VMEM, VMEM, pl.BlockSpec(memory_space=pltpu.SMEM)),
         )(arrived, held, ema_sums[0], ema_counts)
 
-    decoded, commit_error = call(
-        decode_kernel,
-        (shape((256, 256), BF16), shape((1, PARTS * LANES), F32)),
-        3, 300 << 20, 4 << 20,
-    )(got, sent, dec_weight)
-
-    first = one_round(jnp.zeros((), I32), jnp.zeros((SHARE, 2 * LANES), F32))
+    message, from_x, from_core = lax.optimization_barrier((route(jnp.zeros((), I32)), from_x, from_core))
+    across = moved(from_x[4:], 0, 0, 1)
+    columns = call(gather_kernel, (four,) * 3, 4, 1 << 20, 1 << 20)(near, from_core, from_x, across)
+    columns = [moved(columns[dy - 1], 0, dy, 0) for dy in range(1, 4)]
+    decoded = call(decode_kernel, shape((256, 256), BF16), 9, 300 << 20, 4 << 20, scalars=1)(
+        place, near, from_core, from_x, across, *columns, dec_weight
+    )
+
+    first = one_round(message, jnp.zeros((SHARE, 2 * LANES), F32))
 
     def more(state):
         return state[0] < state[4][0, 0]
 
     def again(state):
         index, _, _, held, _ = state
-        return (index + 1, *one_round(index, held))
+        return (index + 1, *one_round(route(index), held))
 
     _, new_codebook, new_counts, _, _ = lax.while_loop(more, again, (jnp.ones((), I32), *first))
     return (decoded, commit_error, new_codebook[None], new_counts)

time: 76.5 us -> 71.2 us (0.931)
  blocking collectives: 22.9 us -> 0 us
  starting transfers between devices: 12.6 us -> 25.3 us
  Pallas kernels: 15.4 us -> 26.4 us
  waiting for transfers between devices: 19.3 us -> 14 us
  local copies, waits for them, and re-layouts: 4.23 us -> 3.19 us
    all_to_all x1 -> x0, blocking collectives: 22.9 us -> none  [body(): got = lax.all_to_all(sent, 'group', split_axis=0, concat_axis=0)]
    all_to_all x1, waiting for transfers between devices: 19.3 us -> 6.69 us  [one_round(): arrived = lax.all_to_all(message, 'dp', split_axis=0, concat_axis=0)]
    pallas_call x4 -> x7, Pallas kernels: 12.6 us -> 23.7 us  [the longest x1 5.44 us: body(): call(pick_kernel, (four, four, eight), 3, 4 << 30, 4 << 20, scalars=1)]
    ppermute x0 -> x6, starting transfers between devices: none -> 6.55 us  [moved(): return lax.ppermute(shard, 'group', pairs)]
    all_to_all x0 -> x1, starting transfers between devices: none -> 6.07 us  [body(): got = lax.all_to_all(sent, 'group', split_axis=0, concat_axis=0)]
    ppermute x0 -> x6, waiting for transfers between devices: none -> 3.49 us  [moved(): return lax.ppermute(shard, 'group', pairs)]
    all_to_all x0 -> x1, waiting for transfers between devices: none -> 3.3 us  [body(): got = lax.all_to_all(sent, 'group', split_axis=0, concat_axis=0)]
    unnamed x22 -> x24, local copies, waits for them, and re-layouts: 3.5 us -> 2.45 us
  transfers between devices with their start and end apart: 2 -> 9, of which waited for: 1 -> 6; matrix products, arithmetic and copies ran while one was open for 0% -> 0% of each run, Pallas kernels for 11% -> 29%
where the time goes in v2:
time: 71.2 us; the launch traced here: 70.7 us
  Pallas kernels  26.4 us (37%)
  starting transfers between devices  25.3 us (36%)
  waiting for transfers between devices  14 us (20%)
  local copies, waits for them, and re-layouts  3.19 us (4%)
  between operations  0.97 us (1%)
    all_to_all x1, starting transfers between devices, one_round(): arrived = lax.all_to_all(message, 'dp', split_axis=0, concat_axis=0)  10.8 us
    all_to_all x1, waiting for transfers between devices, one_round(): arrived = lax.all_to_all(message, 'dp', split_axis=0, concat_axis=0)  6.69 us
    ppermute x6, starting transfers between devices, moved(): return lax.ppermute(shard, 'group', pairs)  6.55 us
    all_to_all x1, starting transfers between devices, body(): got = lax.all_to_all(sent, 'group', split_axis=0, concat_axis=0)  6.07 us
    pallas_call x1, Pallas kernels, body(): call(pick_kernel, (four, four, eight), 3, 4 << 30, 4 << 20, scalars=1)  5.44 us
    pallas_call x1, Pallas kernels, body(): call(encode_kernel, (blocks, shape((PARTS, 16, LANES), BF16), shape((1, P...  5.42 us
    pallas_call x1, Pallas kernels, route(): call(route_kernel, message, 3, 2 << 30, 2 << 20, scalars=1, hbm_in=1, out...  4.53 us
    ppermute x6, waiting for transfers between devices, moved(): return lax.ppermute(shard, 'group', pairs)  3.49 us
  transfers between devices with their start and end apart: 9, of which 6 were waited for; matrix products, arithmetic and copies ran while one was open for 0% of the time, Pallas kernels for 29%

profile of v2, /device:TPU:32, one launch (start us, length us, event | category | flops | bytes accessed | tf_op | source)
XLA Modules:
  0.0 70.7 jit_solution(9268636355269399260)
XLA Ops:
  0.6 0.7 slice.6
  1.3 1.9 %collective-permute-start = (bf16[1,256]{1,0:T(2,128)(2,1)S(1)}, bf16[1,256]{1,0:T(2,128)(2,1)S(1)}, u32[]{:S(2)}, u32[]{:S(2)}) collective-permute-start(bf16[1,256]{1,0:T(2,128)(2,1)S(1)} %slice.6), channel_id=1, source_target_pairs={{0,1},{1,2},{2,3},{3,4},{4,5},{5,6},{6,7},{7,8},{8,9},{9,10},{10,1... | collective-permute-start | bytes 1544 | tf_op jit(solution)/shard_map/ppermute | solution.py:313
  3.2 5.4 %shard_map.111 = (bf16[16,128,128]{2,1,0:T(8,128)(2,1)}, bf16[16,16,128]{2,1,0:T(8,128)(2,1)}, f32[1,2048]{1,0:T(1,128)}) custom-call(bf16[256,256]{1,0:T(8,128)(2,1)} %frames_ref.1, s32[1,8]{1,0:T(1,128)} %clips_ref.3, bf16[768,2048]{1,0:T(8,128)(2,1)} %weight_hbm.3), custom_call_target="tpu_custom_call" | custom-call | flops 419430400 | bytes 4194304 | tf_op jit(solution)/shard_map/pallas_call | solution.py:333
  9.2 0.6 copy-done.8
  9.8 3.2 %shard_map.112 = bf16[16,128,128]{2,1,0:T(8,128)(2,1)} custom-call(bf16[1,256]{1,0:T(2,128)(2,1)} %copy-done.8, s32[1,8]{1,0:T(1,128)} %clips_ref.3, bf16[16,16,128]{2,1,0:T(8,128)(2,1)} %get-tuple-element.72.head_ref, f32[1,2048]{1,0:T(1,128)} %get-tuple-element.73.first_ref, bf16[768,2048]{1,0:T(8,128)(2,1)} %weight_hbm.3, ...), custom_call_target="tpu_custom_call", output_to_operand_aliasing={{}: (5, {})} | custom-call | flops 20971520 | bytes 1048576 | tf_op jit(solution)/shard_map/pallas_call | solution.py:345
  13.0 6.1 %all-to-all-start.1 = ((bf16[16,128,128]{2,1,0:T(8,128)(2,1)}), bf16[16,128,128]{2,1,0:T(8,128)(2,1)S(1)}, u32[]{:S(2)}, u32[]{:S(2)}) async-start(bf16[16,128,128]{2,1,0:T(8,128)(2,1)} %shard_map.112), calls=%async_computation.1 | async-start | bytes 1048576 | tf_op jit(solution)/shard_map/all_to_all | solution.py:358
  19.1 5.4 %shard_map.113 = (bf16[4,128,128]{2,1,0:T(8,128)(2,1)S(1)}, bf16[4,128,128]{2,1,0:T(8,128)(2,1)S(1)}, bf16[8,128,128]{2,1,0:T(8,128)(2,1)S(1)}) custom-call(s32[3]{0:T(128)S(1)} %pad_add_fusion.place_ref, s32[1,2048]{1,0:T(1,128)S(1)} %copy-done.10, bf16[8192,128]{1,0:T(8,128)(2,1)S(1)} %bitcast.14), custom_call_target="tpu_custom_call" | custom-call | flops 4294967296 | bytes 4194304 | tf_op jit(solution)/shard_map/pallas_call | solution.py:355
  24.6 2.0 %collective-permute-start.1 = (bf16[8,128,128]{2,1,0:T(8,128)(2,1)S(1)}, bf16[8,128,128]{2,1,0:T(8,128)(2,1)S(1)}, u32[]{:S(2)}, u32[]{:S(2)}) collective-permute-start(bf16[8,128,128]{2,1,0:T(8,128)(2,1)S(1)} %get-tuple-element.78.beside_ref), channel_id=1, source_target_pairs={{0,8},{1,9},{2,10},{3,11},{4,12},{5,13},{6,14},{7,15},{8,0},{9,1},... | collective-permute-start | bytes 786440 | tf_op jit(solution)/shard_map/ppermute | solution.py:321
  26.6 3.3 %all-to-all-done.1.got_ref = bf16[16,128,128]{2,1,0:T(8,128)(2,1)S(1)} async-done(((bf16[16,128,128]{2,1,0:T(8,128)(2,1)}), bf16[16,128,128]{2,1,0:T(8,128)(2,1)S(1)}, u32[]{:S(2)}, u32[]{:S(2)}) %all-to-all-start.1) | async-done | bytes 524320 | tf_op jit(solution)/shard_map/all_to_all | solution.py:358
  29.9 4.5 %shard_map.114 = bf16[16,192,128]{2,1,0:T(8,128)(2,1)} custom-call(s32[1,1]{1,0:T(1,128)} %constant.4.clone.1.round_ref, s32[1,2048]{1,0:T(1,128)S(1)} %copy-done.10, bf16[16,128,128]{2,1,0:T(8,128)(2,1)S(1)} %all-to-all-done.1.got_ref), custom_call_target="tpu_custom_call" | custom-call | flops 2147483648 | bytes 2097152 | tf_op jit(solution)/shard_map/pallas_call | solution.py:368
  34.5 10.8 %all-to-all-start.2 = ((bf16[16,192,128]{2,1,0:T(8,128)(2,1)}), bf16[16,192,128]{2,1,0:T(8,128)(2,1)S(1)}, u32[]{:S(2)}, u32[]{:S(2)}) async-start(bf16[16,192,128]{2,1,0:T(8,128)(2,1)} %shard_map.114), calls=%async_computation.2 | async-start | bytes 1572864 | tf_op jit(solution)/shard_map/all_to_all | solution.py:380
  45.4 1.3 %collective-permute-done.3.across_ref = bf16[4,128,128]{2,1,0:T(8,128)(2,1)S(1)} collective-permute-done((bf16[4,128,128]{2,1,0:T(8,128)(2,1)S(1)}, bf16[4,128,128]{2,1,0:T(8,128)(2,1)S(1)}, u32[]{:S(2)}, u32[]{:S(2)}) %collective-permute-start.3) | collective-permute-done | bytes 131104 | tf_op jit(solution)/shard_map/ppermute | solution.py:321
  46.8 0.8 %shard_map.115 = (bf16[4,128,128]{2,1,0:T(8,128)(2,1)}, bf16[4,128,128]{2,1,0:T(8,128)(2,1)}, bf16[4,128,128]{2,1,0:T(8,128)(2,1)}) custom-call(bf16[4,128,128]{2,1,0:T(8,128)(2,1)S(1)} %get-tuple-element.76.near_ref, bf16[4,128,128]{2,1,0:T(8,128)(2,1)S(1)} %collective-permute-done.2.far_ref, bf16[8,128,128]{2,1,0:T(8,128)(2,1)S(1)} %collective-permute-done.1.beside_ref, ...), custom_call_target="tpu_custom_call" | custom-call | flops 1048576 | bytes 1048576 | tf_op jit(solution)/shard_map/pallas_call | solution.py:395
  47.9 2.7 %collective-permute-start.5 = (bf16[4,128,128]{2,1,0:T(8,128)(2,1)}, bf16[4,128,128]{2,1,0:T(8,128)(2,1)}, u32[]{:S(2)}, u32[]{:S(2)}) collective-permute-start(bf16[4,128,128]{2,1,0:T(8,128)(2,1)} %get-tuple-element.83), channel_id=1, source_target_pairs={{0,4},{1,5},{2,6},{3,7},{4,0},{5,1},{6,2},{7,3},{8,12},{9,13},{10,... | collective-permute-start | bytes 393224 | tf_op jit(solution)/shard_map/ppermute | solution.py:321
  50.5 1.5 %collective-permute-start.6 = (bf16[4,128,128]{2,1,0:T(8,128)(2,1)}, bf16[4,128,128]{2,1,0:T(8,128)(2,1)}, u32[]{:S(2)}, u32[]{:S(2)}) collective-permute-start(bf16[4,128,128]{2,1,0:T(8,128)(2,1)} %get-tuple-element.84), channel_id=1, source_target_pairs={{0,6},{1,7},{2,0},{3,1},{4,2},{5,3},{6,4},{7,5},{8,14},{9,15},{10,... | collective-permute-start | bytes 393224 | tf_op jit(solution)/shard_map/ppermute | solution.py:321
  52.0 0.9 %copy-done.2 = bf16[8,128,128]{2,1,0:T(8,128)(2,1)S(1)} copy-done((bf16[8,128,128]{2,1,0:T(8,128)(2,1)S(1)}, bf16[8,128,128]{2,1,0:T(8,128)(2,1)}, u32[]{:S(2)}) %copy-start.2) | copy-done | bytes 262168
  53.0 0.9 %copy-done.4 = bf16[4,128,128]{2,1,0:T(8,128)(2,1)S(1)} copy-done((bf16[4,128,128]{2,1,0:T(8,128)(2,1)S(1)}, bf16[4,128,128]{2,1,0:T(8,128)(2,1)}, u32[]{:S(2)}) %copy-start.4) | copy-done | bytes 131096
  53.9 2.0 %shard_map.117 = f32[1,2048]{1,0:T(1,128)} custom-call(s32[3]{0:T(128)S(1)} %pad_add_fusion.place_ref, bf16[16,128,128]{2,1,0:T(8,128)(2,1)} %copy-done.6, bf16[4,128,128]{2,1,0:T(8,128)(2,1)S(1)} %get-tuple-element.76.near_ref, bf16[4,128,128]{2,1,0:T(8,128)(2,1)S(1)} %copy-done.4, bf16[8,128,128]{2,1,0:T(8,128)(2,1)S(1)} %copy-done.2), custom_call_target="tpu_custom_call" | custom-call | flops 1048576 | bytes 1048576 | tf_op jit(solution)/shard_map/pallas_call | solution.py:359
  55.9 1.6 %collective-permute-done.4.y1_ref = bf16[4,128,128]{2,1,0:T(8,128)(2,1)} collective-permute-done((bf16[4,128,128]{2,1,0:T(8,128)(2,1)}, bf16[4,128,128]{2,1,0:T(8,128)(2,1)}, u32[]{:S(2)}, u32[]{:S(2)}) %collective-permute-start.4) | collective-permute-done | bytes 131104 | tf_op jit(solution)/shard_map/ppermute | solution.py:321
  57.4 0.6 collective-permute-done.6.y3_ref
  58.0 2.4 %shard_map.116 = bf16[256,256]{1,0:T(8,128)(2,1)} custom-call(s32[3]{0:T(128)S(1)} %pad_add_fusion.place_ref, bf16[4,128,128]{2,1,0:T(8,128)(2,1)S(1)} %get-tuple-element.76.near_ref, bf16[4,128,128]{2,1,0:T(8,128)(2,1)S(1)} %collective-permute-done.2.far_ref, bf16[8,128,128]{2,1,0:T(8,128)(2,1)S(1)} %collective-permute-done.1.beside_ref, ...), custom_call_target="tpu_custom_call" | custom-call | flops 314572800 | bytes 4194304 | tf_op jit(solution)/shard_map/pallas_call | solution.py:397
  60.4 6.7 %all-to-all-done.2.message_ref = bf16[16,192,128]{2,1,0:T(8,128)(2,1)S(1)} async-done(((bf16[16,192,128]{2,1,0:T(8,128)(2,1)}), bf16[16,192,128]{2,1,0:T(8,128)(2,1)S(1)}, u32[]{:S(2)}, u32[]{:S(2)}) %all-to-all-start.2) | async-done | bytes 786464 | tf_op jit(solution)/shard_map/all_to_all | solution.py:380
  67.1 2.7 %shard_map.118 = (f32[512,128]{1,0:T(8,128)}, f32[1,512]{1,0:T(1,128)}, f32[512,256]{1,0:T(8,128)S(1)}, s32[1,1]{1,0:T(1,128)}) custom-call(bf16[16,192,128]{2,1,0:T(8,128)(2,1)S(1)} %all-to-all-done.2.message_ref, f32[512,256]{1,0:T(8,128)S(1)} %broadcast_in_dim.6.held_ref, f32[512,128]{1,0:T(8,128)} %bitcast.15, f32[1,512]{1,0:T(1,128)S(1)} %copy-done.11), custom_call_target="tpu_custom_call" | custom-call | flops 838860800 | bytes 2097152 | tf_op jit(solution)/shard_map/pallas_call | solution.py:381
  69.8 0.7 while.16
  (31 shorter events, 1.1 us)
Async XLA Ops:
  1.3 7.9 %collective-permute-start = (bf16[1,256]{1,0:T(2,128)(2,1)S(1)}, bf16[1,256]{1,0:T(2,128)(2,1)S(1)}, u32[]{:S(2)}, u32[]{:S(2)}) collective-permute-start(bf16[1,256]{1,0:T(2,128)(2,1)S(1)} %slice.6), channel_id=1, source_target_pairs={{0,1},{1,2},{2,3},{3,4},{4,5},{5,6},{6,7},{7,8},{8,9},{9,10},{10,1... | collective-permute-start | bytes 1544 | tf_op jit(solution)/shard_map/ppermute | solution.py:313
  9.2 0.6 copy-start.8
  9.8 9.4 %copy-start.5 = (bf16[1,8192,128]{2,1,0:T(8,128)(2,1)S(1)}, bf16[1,8192,128]{2,1,0:T(8,128)(2,1)}, u32[]{:S(2)}) copy-start(bf16[1,8192,128]{2,1,0:T(8,128)(2,1)} %param.14) | copy-start | bytes 6291460
  9.8 9.4 %copy-start.10 = (s32[1,2048]{1,0:T(1,128)S(1)}, s32[1,2048]{1,0:T(1,128)}, u32[]{:S(2)}) copy-start(s32[1,2048]{1,0:T(1,128)} %ids_ref.2) | copy-start | bytes 24580
  13.0 16.9 %all-to-all-start.1 = ((bf16[16,128,128]{2,1,0:T(8,128)(2,1)}), bf16[16,128,128]{2,1,0:T(8,128)(2,1)S(1)}, u32[]{:S(2)}, u32[]{:S(2)}) async-start(bf16[16,128,128]{2,1,0:T(8,128)(2,1)} %shard_map.112), calls=%async_computation.1 | async-start | bytes 1048576 | tf_op jit(solution)/shard_map/all_to_all | solution.py:358
  24.6 9.9 %copy-start.1 = (bf16[8,128,128]{2,1,0:T(8,128)(2,1)}, bf16[8,128,128]{2,1,0:T(8,128)(2,1)S(1)}, u32[]{:S(2)}) copy-start(bf16[8,128,128]{2,1,0:T(8,128)(2,1)S(1)} %get-tuple-element.78.beside_ref) | copy-start | bytes 786436
  24.6 9.9 %copy-start.3 = (bf16[4,128,128]{2,1,0:T(8,128)(2,1)}, bf16[4,128,128]{2,1,0:T(8,128)(2,1)S(1)}, u32[]{:S(2)}) copy-start(bf16[4,128,128]{2,1,0:T(8,128)(2,1)S(1)} %get-tuple-element.79.far_ref) | copy-start | bytes 393220
  24.6 9.9 %collective-permute-start.1 = (bf16[8,128,128]{2,1,0:T(8,128)(2,1)S(1)}, bf16[8,128,128]{2,1,0:T(8,128)(2,1)S(1)}, u32[]{:S(2)}, u32[]{:S(2)}) collective-permute-start(bf16[8,128,128]{2,1,0:T(8,128)(2,1)S(1)} %get-tuple-element.78.beside_ref), channel_id=1, source_target_pairs={{0,8},{1,9},{2,10},{3,11},{4,12},{5,13},{6,14},{7,15},{8,0},{9,1},... | collective-permute-start | bytes 786440 | tf_op jit(solution)/shard_map/ppermute | solution.py:321
  26.6 7.9 %collective-permute-start.2 = (bf16[4,128,128]{2,1,0:T(8,128)(2,1)S(1)}, bf16[4,128,128]{2,1,0:T(8,128)(2,1)S(1)}, u32[]{:S(2)}, u32[]{:S(2)}) collective-permute-start(bf16[4,128,128]{2,1,0:T(8,128)(2,1)S(1)} %get-tuple-element.79.far_ref), channel_id=1, source_target_pairs={{0,1},{1,0},{2,3},{3,2},{4,5},{5,4},{6,7},{7,6},{8,9},{9,8},{10,11... | collective-permute-start | bytes 393224 | tf_op jit(solution)/shard_map/ppermute | solution.py:321
  29.9 4.6 %copy-start.6 = (bf16[16,128,128]{2,1,0:T(8,128)(2,1)}, bf16[16,128,128]{2,1,0:T(8,128)(2,1)S(1)}, u32[]{:S(2)}) copy-start(bf16[16,128,128]{2,1,0:T(8,128)(2,1)S(1)} %all-to-all-done.1.got_ref) | copy-start | bytes 1572868
  34.5 23.5 %copy-start = (bf16[2048,512]{1,0:T(8,128)(2,1)S(1)}, bf16[2048,512]{1,0:T(8,128)(2,1)}, u32[]{:S(2)}) copy-start(bf16[2048,512]{1,0:T(8,128)(2,1)} %weight_ref.1) | copy-start | bytes 6291460
  34.5 32.6 %all-to-all-start.2 = ((bf16[16,192,128]{2,1,0:T(8,128)(2,1)}), bf16[16,192,128]{2,1,0:T(8,128)(2,1)S(1)}, u32[]{:S(2)}, u32[]{:S(2)}) async-start(bf16[16,192,128]{2,1,0:T(8,128)(2,1)} %shard_map.114), calls=%async_computation.2 | async-start | bytes 1572864 | tf_op jit(solution)/shard_map/all_to_all | solution.py:380
  45.3 1.4 %collective-permute-start.3 = (bf16[4,128,128]{2,1,0:T(8,128)(2,1)S(1)}, bf16[4,128,128]{2,1,0:T(8,128)(2,1)S(1)}, u32[]{:S(2)}, u32[]{:S(2)}) collective-permute-start(bf16[4,128,128]{2,1,0:T(8,128)(2,1)S(1)} %slice.7), channel_id=1, source_target_pairs={{0,1},{1,0},{2,3},{3,2},{4,5},{5,4},{6,7},{7,6},{8,9},{9,8},{10,11... | collective-permute-start | bytes 393224 | tf_op jit(solution)/shard_map/ppermute | solution.py:321
  47.6 9.9 %collective-permute-start.4 = (bf16[4,128,128]{2,1,0:T(8,128)(2,1)}, bf16[4,128,128]{2,1,0:T(8,128)(2,1)}, u32[]{:S(2)}, u32[]{:S(2)}) collective-permute-start(bf16[4,128,128]{2,1,0:T(8,128)(2,1)} %get-tuple-element.82), channel_id=1, source_target_pairs={{0,2},{1,3},{2,4},{3,5},{4,6},{5,7},{6,0},{7,1},{8,10},{9,11},{10,... | collective-permute-start | bytes 393224 | tf_op jit(solution)/shard_map/ppermute | solution.py:321
  47.9 9.6 %collective-permute-start.5 = (bf16[4,128,128]{2,1,0:T(8,128)(2,1)}, bf16[4,128,128]{2,1,0:T(8,128)(2,1)}, u32[]{:S(2)}, u32[]{:S(2)}) collective-permute-start(bf16[4,128,128]{2,1,0:T(8,128)(2,1)} %get-tuple-element.83), channel_id=1, source_target_pairs={{0,4},{1,5},{2,6},{3,7},{4,0},{5,1},{6,2},{7,3},{8,12},{9,13},{10,... | collective-permute-start | bytes 393224 | tf_op jit(solution)/shard_map/ppermute | solution.py:321
  50.5 7.5 %collective-permute-start.6 = (bf16[4,128,128]{2,1,0:T(8,128)(2,1)}, bf16[4,128,128]{2,1,0:T(8,128)(2,1)}, u32[]{:S(2)}, u32[]{:S(2)}) collective-permute-start(bf16[4,128,128]{2,1,0:T(8,128)(2,1)} %get-tuple-element.84), channel_id=1, source_target_pairs={{0,6},{1,7},{2,0},{3,1},{4,2},{5,3},{6,4},{7,5},{8,14},{9,15},{10,... | collective-permute-start | bytes 393224 | tf_op jit(solution)/shard_map/ppermute | solution.py:321
  52.0 0.9 %copy-start.2 = (bf16[8,128,128]{2,1,0:T(8,128)(2,1)S(1)}, bf16[8,128,128]{2,1,0:T(8,128)(2,1)}, u32[]{:S(2)}) copy-start(bf16[8,128,128]{2,1,0:T(8,128)(2,1)} %copy-done.1) | copy-start | bytes 786436
  53.0 0.9 %copy-start.4 = (bf16[4,128,128]{2,1,0:T(8,128)(2,1)S(1)}, bf16[4,128,128]{2,1,0:T(8,128)(2,1)}, u32[]{:S(2)}) copy-start(bf16[4,128,128]{2,1,0:T(8,128)(2,1)} %copy-done.3) | copy-start | bytes 393220
  55.9 11.3 %copy-start.11 = (f32[1,512]{1,0:T(1,128)S(1)}, f32[1,512]{1,0:T(1,128)}, u32[]{:S(2)}) copy-start(f32[1,512]{1,0:T(1,128)} %ema_counts_ref.1) | copy-start | bytes 6148
  60.4 9.4 %copy-start.7 = (bf16[16,128,128]{2,1,0:T(8,128)(2,1)S(1)}, bf16[16,128,128]{2,1,0:T(8,128)(2,1)}, u32[]{:S(2)}) copy-start(bf16[16,128,128]{2,1,0:T(8,128)(2,1)} %copy-done.6) | copy-start | bytes 1572868
  60.4 9.4 %copy-start.9 = (f32[1,512,128]{2,1,0:T(8,128)S(1)}, f32[1,512,128]{2,1,0:T(8,128)}, u32[]{:S(2)}) copy-start(f32[1,512,128]{2,1,0:T(8,128)} %param.15) | copy-start | bytes 786436

commit v3 on v2

v3 whole, which is shorter than its diff:
```python
import jax
import jax.numpy as jnp
from jax import lax
from jax.experimental import pallas as pl
from jax.experimental.pallas import tpu as pltpu
from jax.sharding import PartitionSpec as P

ema_decay = 0.9

F32 = jnp.float32
BF16 = jnp.bfloat16
I32 = jnp.int32

LANES = 128
PARTS = 16
BLOCK = 192
CAP = 184
SHARE = 512
NEED = 56
TALL = 144

VMEM = pl.BlockSpec(memory_space=pltpu.VMEM)
IN_HBM = pl.BlockSpec(memory_space=pltpu.HBM)


def one_hot(condition):
    return jnp.where(condition, 1.0, 0.0).astype(BF16)


def iota(shape, axis):
    return lax.broadcasted_iota(I32, shape, axis)


def id_columns(ids_ref):
    rows = [ids_ref[0:1, c * LANES:(c + 1) * LANES] for c in range(PARTS)]
    return jnp.concatenate(rows, axis=0).T


def relative_blocks(place_ref):
    x, y, core = place_ref[0], place_ref[1], place_ref[2]
    return [
        ((x ^ dx) * 4 + ((y + dy) & 3)) * 2 + (core ^ dc)
        for dx in range(2) for dc in range(2) for dy in range(4)
    ]


def pick_kernel(place_ref, ids_ref, book_ref, near_ref, far_ref, beside_ref):
    blocks = relative_blocks(place_ref)
    rows = [ids_ref[0:1, pl.ds(pl.multiple_of(b * LANES, LANES), LANES)] for b in blocks]
    columns = jnp.concatenate(rows, axis=0).T
    lanes = iota((LANES, 1024), 1)
    step = 4
    for first in range(0, PARTS, step):
        ids = jnp.concatenate(
            [columns[:, c:c + 1] for c in range(first, first + step)], axis=0
        )
        low, top = ids & 1023, ids >> 10
        selector = jnp.concatenate(
            [one_hot(low[k * LANES:(k + 1) * LANES] == lanes) for k in range(step)], axis=0
        )
        picked = jnp.zeros((step * LANES, LANES), F32)
        for pair in range(4):
            begin = pair * 2048
            tile = jnp.concatenate(
                [book_ref[begin:begin + 1024, :], book_ref[begin + 1024:begin + 2048, :]], axis=1
            )
            both = jnp.dot(selector, tile, preferred_element_type=F32)
            picked = jnp.where(top == 2 * pair, both[:, :LANES], picked)
            picked = jnp.where(top == 2 * pair + 1, both[:, LANES:], picked)
        picked = picked.astype(BF16)
        for k in range(step):
            out_ref = (near_ref, far_ref, beside_ref)[min(first // 4, 2)]
            out_ref[(first + k) % (4 if first < 8 else 8)] = picked[k * LANES:(k + 1) * LANES]


def split3(values):
    first = values.astype(BF16).astype(F32)
    second = (values - first).astype(BF16).astype(F32)
    return first, second, values - first - second


def stacked_rows(rows, shape):
    row, table = iota(shape, 0), jnp.zeros(shape, F32)
    for k, values in enumerate(rows):
        table = jnp.where(row == k, values, table)
    return table


def encode_kernel(
    frames_hbm, clips_hbm, weight_hbm, out_ref, frames_ref, clips_ref, weight_ref, stage_ref, in_sems, sems
):
    loads = [
        pltpu.make_async_copy(frames_hbm, frames_ref, in_sems.at[6]),
        pltpu.make_async_copy(clips_hbm, clips_ref, in_sems.at[7]),
    ]
    for k in range(6):
        rows = pl.ds(k * LANES, LANES)
        loads.append(
            pltpu.make_async_copy(weight_hbm.at[rows, :], weight_ref.at[rows, :], in_sems.at[k])
        )
    for load in loads:
        load.start()
    loads[0].wait()
    loads[1].wait()
    frames = frames_ref[...]
    row, col = iota((LANES, 256), 0), iota((LANES, 256), 1)
    even = jnp.dot(one_hot(col == 2 * row), frames, preferred_element_type=F32)
    odd = jnp.dot(one_hot(col == 2 * row + 1), frames, preferred_element_type=F32)
    earlier = jnp.dot(one_hot(col == 2 * row - 1), frames, preferred_element_type=F32)
    hits = jnp.where(iota((LANES, 8), 0) == clips_ref[...], 1.0, 0.0)
    starts = jnp.max(hits, axis=1, keepdims=True)
    earlier = jnp.where(starts > 0.0, 0.0, earlier)
    stacked = jnp.concatenate([earlier, even, odd], axis=1).astype(BF16)
    last = odd[LANES - 1:]
    for load in loads[2:]:
        load.wait()
    for pair in range(PARTS // 2):
        wide = jnp.dot(
            stacked, weight_ref[:, pair * 256:(pair + 1) * 256], preferred_element_type=F32
        )
        for g, block in ((2 * pair, wide[:, :LANES]), (2 * pair + 1, wide[:, LANES:])):
            extra = [last[:, :LANES], last[:, LANES:], *split3(block[:1]), starts[:1]]
            stage_ref[g, :LANES, :] = block.astype(BF16)
            stage_ref[g, LANES:, :] = stacked_rows(extra, (16, LANES)).astype(BF16)
            pltpu.make_async_copy(stage_ref.at[g], out_ref.at[g], sems.at[g]).start()
    for g in range(PARTS):
        pltpu.make_async_copy(stage_ref.at[g], out_ref.at[g], sems.at[g]).wait()


def finished_rows(lasts, parts, flags, weight):
    halo = jnp.concatenate(
        [jnp.concatenate(half, axis=0) for half in lasts], axis=1
    ).astype(BF16)
    added = jnp.dot(halo, weight, preferred_element_type=F32)
    added = jnp.where(jnp.concatenate(flags, axis=0) > 0.0, 0.0, added)
    return (added + jnp.concatenate(parts, axis=0)).astype(BF16).astype(F32)


def select_kernel(round_ref, ids_ref, place_ref, meta_ref):
    passed = round_ref[0, 0] * CAP
    dest_rows, tables = [], []
    sub16 = iota((PARTS, LANES), 0)
    for c in range(PARTS):
        dest = ids_ref[0:1, c * LANES:(c + 1) * LANES] >> 9
        dest_rows.append(dest)
        table = jnp.where(sub16 == dest, 1.0, 0.0)
        if c == 0:
            table = jnp.where(iota((PARTS, LANES), 1) == 0, 0.0, table)
        tables.append(table)
    upper = one_hot(iota((LANES, LANES), 0) <= iota((LANES, LANES), 1))
    cumulative = jnp.dot(
        jnp.concatenate(tables, axis=0).astype(BF16), upper, preferred_element_type=F32
    )
    offset = jnp.zeros((PARTS, 1), F32)
    rows = iota((4 * BLOCK, LANES), 0)
    selectors = []
    for c in range(PARTS):
        inside = cumulative[c * PARTS:(c + 1) * PARTS]
        rank = jnp.sum(tables[c] * (inside + (offset - 1.0)), axis=0, keepdims=True)
        rank = rank.astype(I32) - passed
        kept = (rank >= 0) & (rank < CAP)
        if c == 0:
            kept = kept & (iota((1, LANES), 1) > 0)
        place = jnp.where(kept, (dest_rows[c] & 3) * BLOCK + rank, -1)
        place_ref[:, c * LANES:(c + 1) * LANES] = place
        selectors.append(one_hot(rows == place))
        offset = offset + inside[:, LANES - 1:]
    most = jnp.max(offset, axis=0, keepdims=True)
    need = jnp.ones((1, 1), F32)
    for k in range(1, 2048 // CAP + 1):
        need = need + jnp.where(most > float(k * CAP), 1.0, 0.0)

    columns = id_columns(ids_ref)
    lane = iota((LANES, LANES), 1)
    pieces = []
    for c in range(PARTS):
        ids = columns[:, c:c + 1]
        code = ids & (SHARE - 1)
        mark = jnp.where((lane & 1) == 1, code & 15, (code >> 4) + 1)
        pieces.append(jnp.where((lane >> 3) == (ids >> 11), mark, 0).astype(F32).astype(BF16))
    marks = jnp.dot(
        jnp.concatenate(selectors, axis=1), jnp.concatenate(pieces, axis=0), preferred_element_type=F32
    )
    lane8, row8 = iota((8, LANES), 1), iota((8, LANES), 0)
    ids = jnp.broadcast_to(columns[0:1, 0:1], (8, LANES))
    code = ids & (SHARE - 1)
    late = jnp.where(lane8 == NEED + 1, (code >> 4) + 1, jnp.where(lane8 == NEED + 2, code & 15, 0))
    late = jnp.where(round_ref[0, 0] == 0, late, 0).astype(F32)
    for j in range(4):
        block = marks[j * BLOCK:(j + 1) * BLOCK]
        first = block[:LANES].T
        second = jnp.concatenate([block[LANES:], pltpu.roll(block[LANES:], 1, 1)], axis=0).T
        for q in range(4):
            special = jnp.where((ids >> 9) == 4 * q + j, late, 0.0)
            special = jnp.where(lane8 == NEED, need, special)
            tail = second[8 * q:8 * q + 8] + special
            meta_ref[4 * q + j] = jnp.where(
                row8 < 2, first[8 * q:8 * q + 8], jnp.where(row8 == 2, tail, 0.0)
            )


def route_kernel(
    spot_ref, place_ref, ids_ref, meta_ref, weight_hbm, got_ref,
    out_ref, firsts_ref, owned_ref, weight_ref, stage_ref, sems, got_sem, weight_sem,
):
    loaded = pltpu.make_async_copy(got_ref, owned_ref, got_sem)
    loaded.start()
    group = (spot_ref[0] * 4 + spot_ref[1]) * 2 + spot_ref[2]
    mine = pl.ds(pl.multiple_of(group * LANES, LANES), LANES)
    weight_load = pltpu.make_async_copy(weight_hbm.at[pl.ds(0, 256), mine], weight_ref, weight_sem)
    weight_load.start()
    columns = id_columns(ids_ref)
    rows = iota((4 * BLOCK, LANES), 0)
    selector = jnp.concatenate(
        [one_hot(rows == place_ref[:, c * LANES:(c + 1) * LANES]) for c in range(PARTS)], axis=1
    )
    weight_load.wait()
    loaded.wait()
    extras = [owned_ref[c, LANES:, :].astype(F32) for c in range(PARTS)]
    before = [jnp.zeros((16, LANES), F32)] + extras[:-1]
    firsts = finished_rows(
        [[extra[k:k + 1] for extra in before] for k in range(2)],
        [extra[2:3] + extra[3:4] + extra[4:5] for extra in extras],
        [extra[5:6, 0:1] for extra in extras],
        weight_ref[...],
    )
    firsts_ref[...] = firsts
    row16 = iota((16, LANES), 0)
    for c in range(1, PARTS):
        head = owned_ref[c, :16, :].astype(F32)
        owned_ref[c, :16, :] = jnp.where(row16 == 0, firsts[c:c + 1], head).astype(BF16)
    here = extras[0]
    late = stacked_rows(
        [0.0, 0.0, 0.0, extras[-1][0:1], extras[-1][1:2], here[2:3], here[3:4], here[4:5]], (8, LANES)
    )
    flag = (iota((8, LANES), 0) == 2) & (iota((8, LANES), 1) == NEED + 3)
    late = jnp.where(flag, here[5:6, 0:1], late)
    for half in range(2):
        wides = []
        for c in range(PARTS):
            quarter = columns[:, c:c + 1] >> 11
            latent = owned_ref[c, :LANES, :]
            wides.append(jnp.concatenate(
                [latent * one_hot(jnp.broadcast_to(quarter, (LANES, LANES)) == q) for q in (2 * half, 2 * half + 1)], axis=1
            ))
        total = jnp.dot(selector, jnp.concatenate(wides, axis=0), preferred_element_type=F32)
        for q in range(2):
            for j in range(4):
                to = 8 * half + 4 * q + j
                data = total[j * BLOCK:j * BLOCK + CAP, q * LANES:(q + 1) * LANES]
                stage_ref[to] = jnp.concatenate([data, meta_ref[to] + late], axis=0).astype(BF16)
                pltpu.make_async_copy(stage_ref.at[to], out_ref.at[to], sems.at[to]).start()
    for to in range(PARTS):
        pltpu.make_async_copy(stage_ref.at[to], out_ref.at[to], sems.at[to]).wait()


def update_kernel(
    spot_ref, message_ref, held_ref, ema_counts_ref, error_ref, picked_ref, weight_hbm, ema_sums_hbm,
    book_ref, counts_ref, kept_ref, error_out_ref, need_ref, ema_sums_ref, weight_ref, sems,
):
    group = (spot_ref[0] * 4 + spot_ref[1]) * 2 + spot_ref[2]
    mine = pl.ds(pl.multiple_of(group * LANES, LANES), LANES)
    weight_load = pltpu.make_async_copy(weight_hbm.at[pl.ds(0, 256), mine], weight_ref, sems.at[0])
    weight_load.start()
    sums_load = pltpu.make_async_copy(ema_sums_hbm, ema_sums_ref, sems.at[1])
    sums_load.start()
    codes = iota((SHARE, LANES), 0).astype(F32)
    ones = jnp.ones((8 * LANES, LANES), BF16)
    kept_ref[...] = held_ref[...]
    need = jnp.zeros((1, 1), F32)
    lane = iota((1, LANES), 1)
    metas, selectors, datas = [], [], []

    def flush():
        data = jnp.concatenate(datas, axis=0)
        kept_ref[...] += jnp.dot(
            jnp.concatenate(selectors, axis=1),
            jnp.concatenate([data, ones[:data.shape[0]]], axis=1),
            preferred_element_type=F32,
        )
        selectors.clear()
        datas.clear()

    for s in range(PARTS):
        meta = message_ref[s, BLOCK - 16:, :].astype(F32)[8:]
        metas.append(meta)
        need = jnp.maximum(need, meta[2:3, NEED:NEED + 1])
        selectors.append(one_hot(codes == (meta[0:1] - 1.0) * 16.0 + meta[1:2]))
        datas.append(message_ref[s, :LANES, :])
        if len(datas) == 8:
            flush()
    for s in range(0, PARTS, 2):
        tails = [meta[2:3] for meta in metas[s:s + 2]]
        turned = [pltpu.roll(jnp.broadcast_to(tail, (8, LANES)), 64, 1)[0:1] for tail in tails]
        high = jnp.where(lane < 64, tails[0], turned[1])
        low = jnp.where(lane < 64, turned[0], tails[1])
        high = jnp.where((lane & 63) < NEED, high, 0.0)
        selectors.append(one_hot(codes == (high - 1.0) * 16.0 + low))
        datas.append(
            jnp.concatenate([message_ref[s, LANES:, :], message_ref[s + 1, LANES:, :]], axis=0)
        )
        if len(datas) == 8:
            flush()

    weight_load.wait()
    before = [jnp.zeros((8, LANES), F32)] + metas[:-1]
    firsts = finished_rows(
        [[meta[k:k + 1] for meta in before] for k in (3, 4)],
        [meta[5:6] + meta[6:7] + meta[7:8] for meta in metas],
        [meta[2:3, NEED + 3:NEED + 4] for meta in metas],
        weight_ref[...],
    )
    wanted = jnp.full((1, LANES), -16.0, F32)
    for s in range(PARTS):
        high, low = metas[s][2:3, NEED + 1:NEED + 2], metas[s][2:3, NEED + 2:NEED + 3]
        wanted = jnp.where(lane == s, (high - 1.0) * 16.0 + low, wanted)
    selectors.append(one_hot(codes == wanted))
    datas.append(
        jnp.concatenate([firsts, jnp.zeros((LANES - PARTS, LANES), F32)], axis=0).astype(BF16)
    )
    flush()
    own = jnp.where(iota((PARTS, LANES), 0) == spot_ref[3], firsts, 0.0)
    diff = jnp.sum(own, axis=0, keepdims=True) - picked_ref[0:1]
    error = jnp.sum(diff * diff, axis=1, keepdims=True) * (1.0 / LANES)
    error_out_ref[...] = error_ref[...]
    error_out_ref[0:1, :LANES] = jnp.where(lane == 0, error, error_ref[0:1, :LANES])
    sums_load.wait()
    need_ref[0, 0] = jnp.max(need).astype(I32)
    diagonal = iota((LANES, LANES), 0) == iota((LANES, LANES), 1)
    for k in range(SHARE // LANES):
        begin = k * LANES
        old = jnp.broadcast_to(ema_counts_ref[0:1, begin:begin + LANES], (LANES, LANES)).T
        sums, counts = kept_ref[begin:begin + LANES, :LANES], kept_ref[begin:begin + LANES, LANES:]
        new_counts = ema_decay * old + (1.0 - ema_decay) * counts
        book_ref[begin:begin + LANES, :] = (
            ema_decay * ema_sums_ref[begin:begin + LANES, :] + (1.0 - ema_decay) * sums
        ) / new_counts
        counts_ref[0:1, begin:begin + LANES] = jnp.sum(
            jnp.where(diagonal, new_counts, 0.0), axis=0, keepdims=True
        )


def gather_kernel(near_ref, far_ref, beside_ref, across_ref, *out_refs):
    for k, ref in enumerate((near_ref, far_ref, beside_ref, across_ref)):
        for dy in range(1, 4):
            out_refs[dy - 1][k] = ref[dy]


def decode_kernel(
    place_ref, near_ref, far_ref, beside_ref, across_ref, y1_ref, y2_ref, y3_ref, weight_ref, out_ref
):
    groups = relative_blocks(place_ref)
    slabs, weights = [], []
    for dy in range(4):
        for k, ref in enumerate((near_ref, far_ref, beside_ref, across_ref)):
            group = groups[4 * k + (4 - dy) % 4]
            slabs.append(ref[0] if dy == 0 else (y1_ref, y2_ref, y3_ref)[dy - 1][k])
            weights.append(weight_ref[pl.ds(pl.multiple_of(group * LANES, LANES), LANES), :])
    decoded = jnp.dot(
        jnp.concatenate(slabs, axis=1), jnp.concatenate(weights, axis=0), preferred_element_type=F32
    ).astype(BF16)
    halves = jnp.concatenate([decoded[:, :256], decoded[:, 256:]], axis=0)
    row, col = iota((256, 256), 0), iota((256, 256), 1)
    source = (row >> 1) + (row & 1) * LANES
    out_ref[...] = jnp.dot(one_hot(col == source), halves, preferred_element_type=F32).astype(BF16)


def error_kernel(place_ref, firsts_ref, got_ref, near_ref, far_ref, beside_ref, error_ref, picked_ref):
    row = iota((LANES, LANES), 0)
    first = jnp.zeros((1, LANES), F32)
    for k, block in enumerate(relative_blocks(place_ref)):
        picked = (near_ref, far_ref)[k // 4][k % 4] if k < 8 else beside_ref[k - 8]
        picked = picked.astype(F32)
        first = jnp.where(block == 0, picked[0:1], first)
        latent = got_ref[block, :LANES, :].astype(F32)
        diff = jnp.where(row == 0, firsts_ref[pl.ds(block, 1), :], latent) - picked
        error = jnp.sum((diff * diff).T, axis=0, keepdims=True) * (1.0 / LANES)
        error_ref[0:1, pl.ds(pl.multiple_of(block * LANES, LANES), LANES)] = error
    picked_ref[...] = jnp.broadcast_to(first, (8, LANES))


def call(kernel, out_shape, count, flops, size, scalars=0, hbm_in=0, out_specs=None, scratch=(), aliases=None, limit=40):
    in_specs = [pl.BlockSpec(memory_space=pltpu.SMEM)] * scalars + [VMEM] * (count - scalars)
    in_specs[count - hbm_in:] = [IN_HBM] * hbm_in
    return pl.pallas_call(
        kernel,
        out_shape=out_shape,
        in_specs=in_specs,
        out_specs=out_specs or jax.tree.map(lambda _: VMEM, out_shape),
        scratch_shapes=list(scratch),
        input_output_aliases=aliases or {},
        cost_estimate=pl.CostEstimate(flops=flops, bytes_accessed=size, transcendentals=0),
        compiler_params=pltpu.CompilerParams(vmem_limit_bytes=limit << 20),
    )


def moved(shard, dx, dy, dc):
    pairs = [
        ((x * 4 + y) * 2 + c, ((x ^ dx) * 4 + (y + dy) % 4) * 2 + (c ^ dc))
        for x in range(2) for y in range(4) for c in range(2)
    ]
    return lax.ppermute(shard, "group", pairs)


def body(
    motion_frames, enc_weight, code_ids, clip_offsets, codebook, ema_sums, ema_counts, dec_weight
):
    shape = jax.ShapeDtypeStruct
    me = lax.axis_index("group").astype(I32)
    place = jnp.stack([me >> 3, (me >> 1) & 3, me & 1, lax.axis_index("dp").astype(I32)])
    blocks = shape((PARTS, TALL, LANES), BF16)
    four, eight = shape((4, LANES, LANES), BF16), shape((8, LANES, LANES), BF16)
    sent = call(
        encode_kernel, blocks, 3, 400 << 20, 4 << 20, hbm_in=3, limit=60, out_specs=IN_HBM,
        scratch=[
            pltpu.VMEM(motion_frames.shape, BF16),
            pltpu.VMEM(clip_offsets.shape, I32),
            pltpu.VMEM(enc_weight.shape, BF16),
            pltpu.VMEM(blocks.shape, BF16),
            pltpu.SemaphoreType.DMA((8,)),
            pltpu.SemaphoreType.DMA((PARTS,)),
        ],
    )(motion_frames, clip_offsets, enc_weight)
    sent, late_ids = lax.optimization_barrier((sent, code_ids))
    near, far, beside = call(pick_kernel, (four, four, eight), 3, 4 << 30, 4 << 20, scalars=1)(
        place, late_ids, codebook[0]
    )
    got = lax.all_to_all(sent, "group", split_axis=0, concat_axis=0)
    from_x = moved(beside, 1, 0, 0)
    from_core = moved(far, 0, 0, 1)

    def route(index):
        frame_places, meta = call(
            select_kernel,
            (shape((1, PARTS * LANES), I32), shape((PARTS, 8, LANES), F32)),
            2, 500 << 20, 1 << 20, scalars=1,
        )(index.reshape(1, 1), code_ids)
        message = shape((PARTS, BLOCK, LANES), BF16)
        return call(
            route_kernel, (message, shape((PARTS, LANES), F32)), 6, 2 << 30, 2 << 20, scalars=1, hbm_in=2,
            out_specs=(IN_HBM, VMEM), limit=60,
            scratch=[
                pltpu.VMEM(blocks.shape, BF16),
                pltpu.VMEM((256, LANES), BF16),
                pltpu.VMEM(message.shape, BF16),
                pltpu.SemaphoreType.DMA((PARTS,)),
                pltpu.SemaphoreType.DMA,
                pltpu.SemaphoreType.DMA,
            ],
        )(place, frame_places, code_ids, meta, enc_weight, got)

    def one_round(message, held):
        arrived = lax.all_to_all(message, "dp", split_axis=0, concat_axis=0)
        return call(
            update_kernel,
            (
                shape((SHARE, LANES), F32),
                shape((1, SHARE), F32),
                shape((SHARE, 2 * LANES), F32),
                shape((1, PARTS * LANES), F32),
                shape((1, 1), I32),
            ),
            8, 800 << 20, 2 << 20, scalars=1, hbm_in=2,
            out_specs=(VMEM, VMEM, VMEM, VMEM, pl.BlockSpec(memory_space=pltpu.SMEM)),
            scratch=[
                pltpu.VMEM((SHARE, LANES), F32),
                pltpu.VMEM((256, LANES), BF16),
                pltpu.SemaphoreType.DMA((2,)),
            ],
        )(place, arrived, held, ema_counts, error, first_picked, enc_weight, ema_sums[0])

    message, firsts = route(jnp.zeros((), I32))
    error, first_picked = call(
        error_kernel, (shape((1, PARTS * LANES), F32), shape((8, LANES), F32)), 6, 1 << 20, 1 << 20, scalars=1
    )(place, firsts, got, near, far, beside)
    message, from_x, from_core = lax.optimization_barrier((message, from_x, from_core))
    across = moved(from_x[4:], 0, 0, 1)
    columns = call(gather_kernel, (four,) * 3, 4, 1 << 20, 1 << 20)(near, from_core, from_x, across)
    columns = [moved(columns[dy - 1], 0, dy, 0) for dy in range(1, 4)]
    decoded = call(decode_kernel, shape((256, 256), BF16), 9, 300 << 20, 4 << 20, scalars=1)(
        place, near, from_core, from_x, across, *columns, dec_weight
    )

    first = one_round(message, jnp.zeros((SHARE, 2 * LANES), F32))

    def more(state):
        return state[0] < state[5][0, 0]

    def again(state):
        index, held = state[0], state[3]
        return (index + 1, *one_round(route(index)[0], held))

    _, new_codebook, new_counts, _, commit_error, _ = lax.while_loop(
        more, again, (jnp.ones((), I32), *first)
    )
    return (decoded, commit_error, new_codebook[None], new_counts)


def solution(mesh):
    return jax.shard_map(
        body,
        mesh=mesh,
        in_specs=(
            P(("dp", "group"), None),
            P(),
            P("group", "dp"),
            P(("dp", "group"), None),
            P("group", None, None),
            P("group", "dp", None),
            P("group", "dp"),
            P(),
        ),
        out_specs=(
            P(("dp", "group"), None),
            P("group", "dp"),
            P("group", "dp", None),
            P("group", "dp"),
        ),
        check_vma=False,
    )
```

time: 71.2 us -> 64.9 us (0.912)
  starting transfers between devices: 25.3 us -> 22.4 us
  Pallas kernels: 26.4 us -> 24.3 us
  waiting for transfers between devices: 14 us -> 12.2 us
    pallas_call x4, Pallas kernels: 15.1 us -> 12.8 us  [the longest x1 5.56 us: route(): call(route_kernel, (message, shape((PARTS, LANES), F32)), 6, 2 << 30, 2 <...]
    ppermute x1 -> x0, starting transfers between devices: 1.91 us -> none  [passed_along(): return lax.ppermute(shard, axis, pairs)]
    all_to_all x1, waiting for transfers between devices: 3.3 us -> 1.76 us  [body(): got = lax.all_to_all(sent, 'group', split_axis=0, concat_axis=0)]
    unnamed x24 -> x32, local copies, waits for them, and re-layouts: 2.45 us -> 3.14 us
  transfers between devices with their start and end apart: 9 -> 8, of which waited for: 6 -> 5; matrix products, arithmetic and copies ran while one was open for 0% -> 0% of each run, Pallas kernels for 29% -> 28%
where the time goes in v3:
time: 64.9 us; the launch traced here: 63.8 us
  Pallas kernels  24.3 us (37%)
  starting transfers between devices  22.4 us (35%)
  waiting for transfers between devices  12.2 us (19%)
  local copies, waits for them, and re-layouts  3.19 us (5%)
  between operations  1.03 us (2%)
    all_to_all x1, starting transfers between devices, one_round(): arrived = lax.all_to_all(message, 'dp', split_axis=0, concat_axis=0)  10.9 us
    all_to_all x1, waiting for transfers between devices, one_round(): arrived = lax.all_to_all(message, 'dp', split_axis=0, concat_axis=0)  6.24 us
    ppermute x6, starting transfers between devices, moved(): return lax.ppermute(shard, 'group', pairs)  5.91 us
    pallas_call x1, Pallas kernels, route(): call(route_kernel, (message, shape((PARTS, LANES), F32)), 6, 2 << 30, 2 <...  5.56 us
    all_to_all x1, starting transfers between devices, body(): got = lax.all_to_all(sent, 'group', split_axis=0, concat_axis=0)  5.56 us
    pallas_call x1, Pallas kernels, body(): call(pick_kernel, (four, four, eight), 3, 4 << 30, 4 << 20, scalars=1)  5.3 us
    ppermute x6, waiting for transfers between devices, moved(): return lax.ppermute(shard, 'group', pairs)  4.16 us
    pallas_call x1, Pallas kernels, body(): call(encode_kernel, blocks, 3, 400 << 20, 4 << 20, hbm_in=3, limit=60, ou...  3.51 us
  transfers between devices with their start and end apart: 8, of which 5 were waited for; matrix products, arithmetic and copies ran while one was open for 0% of the time, Pallas kernels for 28%

profile of v3, /device:TPU:32, one launch (start us, length us, event | category | flops | bytes accessed | tf_op | source)
XLA Modules:
  0.0 63.8 jit_solution(16876543375590185319)
XLA Ops:
  0.7 3.5 %shard_map.111 = bf16[16,144,128]{2,1,0:T(8,128)(2,1)} custom-call(bf16[256,256]{1,0:T(8,128)(2,1)} %frames_hbm.1, s32[1,8]{1,0:T(1,128)} %clips_hbm.1, bf16[768,2048]{1,0:T(8,128)(2,1)} %weight_hbm.5), custom_call_target="tpu_custom_call" | custom-call | flops 419430400 | bytes 4194304 | tf_op jit(solution)/shard_map/pallas_call | solution.py:413
  4.2 5.6 %all-to-all-start.1 = ((bf16[16,144,128]{2,1,0:T(8,128)(2,1)}), bf16[16,144,128]{2,1,0:T(8,128)(2,1)}, u32[]{:S(2)}, u32[]{:S(2)}) async-start(bf16[16,144,128]{2,1,0:T(8,128)(2,1)} %shard_map.111), calls=%async_computation.1 | async-start | bytes 1179648 | tf_op jit(solution)/shard_map/all_to_all | solution.py:428
  9.8 5.3 %shard_map.112 = (bf16[4,128,128]{2,1,0:T(8,128)(2,1)S(1)}, bf16[4,128,128]{2,1,0:T(8,128)(2,1)S(1)}, bf16[8,128,128]{2,1,0:T(8,128)(2,1)S(1)}) custom-call(s32[4]{0:T(128)S(1)} %pad_add_fusion.place_ref.spot_ref, s32[1,2048]{1,0:T(1,128)S(1)} %copy-done.16, bf16[8192,128]{1,0:T(8,128)(2,1)S(1)} %bitcast.15), custom_call_target="tpu_custom_call" | custom-call | flops 4294967296 | bytes 4194304 | tf_op jit(solution)/shard_map/pallas_call | solution.py:425
  15.2 2.0 %collective-permute-start = (bf16[8,128,128]{2,1,0:T(8,128)(2,1)S(1)}, bf16[8,128,128]{2,1,0:T(8,128)(2,1)S(1)}, u32[]{:S(2)}, u32[]{:S(2)}) collective-permute-start(bf16[8,128,128]{2,1,0:T(8,128)(2,1)S(1)} %get-tuple-element.111.beside_ref), channel_id=1, source_target_pairs={{0,8},{1,9},{2,10},{3,11},{4,12},{5,13},{6,14},{7,15},{8,0},{9,1},... | collective-permute-start | bytes 786440 | tf_op jit(solution)/shard_map/ppermute | solution.py:402
  17.1 1.7 %shard_map.113 = (s32[1,2048]{1,0:T(1,128)S(1)}, f32[16,8,128]{2,1,0:T(8,128)S(1)}) custom-call(s32[1,1]{1,0:T(1,128)} %constant.15.clone.1.round_ref, s32[1,2048]{1,0:T(1,128)S(1)} %copy-done.16), custom_call_target="tpu_custom_call" | custom-call | flops 524288000 | bytes 1048576 | tf_op jit(solution)/shard_map/pallas_call | solution.py:433
  18.9 0.6 copy-done.7
  19.5 0.6 copy-done.9
  20.1 1.8 %all-to-all-done.1.got_ref = bf16[16,144,128]{2,1,0:T(8,128)(2,1)} async-done(((bf16[16,144,128]{2,1,0:T(8,128)(2,1)}), bf16[16,144,128]{2,1,0:T(8,128)(2,1)}, u32[]{:S(2)}, u32[]{:S(2)}) %all-to-all-start.1) | async-done | bytes 589856 | tf_op jit(solution)/shard_map/all_to_all | solution.py:428
  21.9 5.6 %shard_map.114 = (bf16[16,192,128]{2,1,0:T(8,128)(2,1)}, f32[16,128]{1,0:T(8,128)}) custom-call(s32[4]{0:T(128)S(1)} %pad_add_fusion.place_ref.spot_ref, s32[1,2048]{1,0:T(1,128)} %copy-done.9, s32[1,2048]{1,0:T(1,128)S(1)} %copy-done.16, f32[16,8,128]{2,1,0:T(8,128)} %copy-done.7, bf16[768,2048]{1,0:T(8,128)(2,1)} %weight_hbm.5, ...), custom_call_target="tpu_custom_call" | custom-call | flops 2147483648 | bytes 2097152 | tf_op jit(solution)/shard_map/pallas_call | solution.py:439
  27.5 10.9 %all-to-all-start.2 = ((bf16[16,192,128]{2,1,0:T(8,128)(2,1)}), bf16[16,192,128]{2,1,0:T(8,128)(2,1)S(1)}, u32[]{:S(2)}, u32[]{:S(2)}) async-start(bf16[16,192,128]{2,1,0:T(8,128)(2,1)} %get-tuple-element.118), calls=%async_computation.2 | async-start | bytes 1572864 | tf_op jit(solution)/shard_map/all_to_all | solution.py:453
  38.4 0.1 collective-permute-start.2
  38.5 1.3 %collective-permute-done.2.across_ref = bf16[4,128,128]{2,1,0:T(8,128)(2,1)S(1)} collective-permute-done((bf16[4,128,128]{2,1,0:T(8,128)(2,1)S(1)}, bf16[4,128,128]{2,1,0:T(8,128)(2,1)S(1)}, u32[]{:S(2)}, u32[]{:S(2)}) %collective-permute-start.2) | collective-permute-done | bytes 131104 | tf_op jit(solution)/shard_map/ppermute | solution.py:402
  39.9 0.8 %shard_map.115 = (bf16[4,128,128]{2,1,0:T(8,128)(2,1)}, bf16[4,128,128]{2,1,0:T(8,128)(2,1)}, bf16[4,128,128]{2,1,0:T(8,128)(2,1)}) custom-call(bf16[4,128,128]{2,1,0:T(8,128)(2,1)S(1)} %get-tuple-element.106.near_ref, bf16[4,128,128]{2,1,0:T(8,128)(2,1)S(1)} %collective-permute-done.1.far_ref, bf16[8,128,128]{2,1,0:T(8,128)(2,1)S(1)} %collective-permute-done.beside_ref, ...), custom_call_target="tpu_custom_call" | custom-call | flops 1048576 | bytes 1048576 | tf_op jit(solution)/shard_map/pallas_call | solution.py:478
  40.6 2.4 %collective-permute-start.4 = (bf16[4,128,128]{2,1,0:T(8,128)(2,1)}, bf16[4,128,128]{2,1,0:T(8,128)(2,1)}, u32[]{:S(2)}, u32[]{:S(2)}) collective-permute-start(bf16[4,128,128]{2,1,0:T(8,128)(2,1)} %get-tuple-element.116), channel_id=1, source_target_pairs={{0,4},{1,5},{2,6},{3,7},{4,0},{5,1},{6,2},{7,3},{8,12},{9,13},{10,... | collective-permute-start | bytes 393224 | tf_op jit(solution)/shard_map/ppermute | solution.py:402
  43.0 1.5 %collective-permute-start.5 = (bf16[4,128,128]{2,1,0:T(8,128)(2,1)}, bf16[4,128,128]{2,1,0:T(8,128)(2,1)}, u32[]{:S(2)}, u32[]{:S(2)}) collective-permute-start(bf16[4,128,128]{2,1,0:T(8,128)(2,1)} %get-tuple-element.117), channel_id=1, source_target_pairs={{0,6},{1,7},{2,0},{3,1},{4,2},{5,3},{6,4},{7,5},{8,14},{9,15},{10,... | collective-permute-start | bytes 393224 | tf_op jit(solution)/shard_map/ppermute | solution.py:402
  44.5 0.9 %copy-done.2 = bf16[8,128,128]{2,1,0:T(8,128)(2,1)S(1)} copy-done((bf16[8,128,128]{2,1,0:T(8,128)(2,1)S(1)}, bf16[8,128,128]{2,1,0:T(8,128)(2,1)}, u32[]{:S(2)}) %copy-start.2) | copy-done | bytes 262168
  45.4 0.9 %copy-done.4 = bf16[4,128,128]{2,1,0:T(8,128)(2,1)S(1)} copy-done((bf16[4,128,128]{2,1,0:T(8,128)(2,1)S(1)}, bf16[4,128,128]{2,1,0:T(8,128)(2,1)}, u32[]{:S(2)}) %copy-start.4) | copy-done | bytes 131096
  46.3 1.9 %shard_map.117 = (f32[1,2048]{1,0:T(1,128)S(1)}, f32[8,128]{1,0:T(8,128)}) custom-call(s32[4]{0:T(128)} %copy-done.14, f32[16,128]{1,0:T(8,128)S(1)} %copy-done.5, bf16[16,144,128]{2,1,0:T(8,128)(2,1)} %all-to-all-done.1.got_ref, bf16[4,128,128]{2,1,0:T(8,128)(2,1)S(1)} %get-tuple-element.106.near_ref, bf16[4,128,128]{2,1,0:T(8,128)(2,1)S(1)} %copy-done.4, ...), custom_call_target="tpu_custom_call" | custom-call | flops 1048576 | bytes 1048576 | tf_op jit(solution)/shard_map/pallas_call | solution.py:473
  48.3 2.2 %collective-permute-done.3.y1_ref = bf16[4,128,128]{2,1,0:T(8,128)(2,1)} collective-permute-done((bf16[4,128,128]{2,1,0:T(8,128)(2,1)}, bf16[4,128,128]{2,1,0:T(8,128)(2,1)}, u32[]{:S(2)}, u32[]{:S(2)}) %collective-permute-start.3) | collective-permute-done | bytes 131104 | tf_op jit(solution)/shard_map/ppermute | solution.py:402
  50.5 0.6 collective-permute-done.5.y3_ref
  51.1 2.4 %shard_map.116 = bf16[256,256]{1,0:T(8,128)(2,1)} custom-call(s32[4]{0:T(128)} %copy-done.14, bf16[4,128,128]{2,1,0:T(8,128)(2,1)S(1)} %get-tuple-element.106.near_ref, bf16[4,128,128]{2,1,0:T(8,128)(2,1)S(1)} %collective-permute-done.1.far_ref, bf16[8,128,128]{2,1,0:T(8,128)(2,1)S(1)} %collective-permute-done.beside_ref, ...), custom_call_target="tpu_custom_call" | custom-call | flops 314572800 | bytes 4194304 | tf_op jit(solution)/shard_map/pallas_call | solution.py:480
  53.5 6.2 %all-to-all-done.2.message_ref = bf16[16,192,128]{2,1,0:T(8,128)(2,1)S(1)} async-done(((bf16[16,192,128]{2,1,0:T(8,128)(2,1)}), bf16[16,192,128]{2,1,0:T(8,128)(2,1)S(1)}, u32[]{:S(2)}, u32[]{:S(2)}) %all-to-all-start.2) | async-done | bytes 786464 | tf_op jit(solution)/shard_map/all_to_all | solution.py:453
  59.8 3.1 %shard_map.118 = (f32[512,128]{1,0:T(8,128)}, f32[1,512]{1,0:T(1,128)}, f32[512,256]{1,0:T(8,128)S(1)}, f32[1,2048]{1,0:T(1,128)}, s32[1,1]{1,0:T(1,128)}) custom-call(s32[4]{0:T(128)} %copy-done.14, bf16[16,192,128]{2,1,0:T(8,128)(2,1)S(1)} %all-to-all-done.2.message_ref, f32[512,256]{1,0:T(8,128)S(1)} %broadcast_in_dim.6.held_ref, ...), custom_call_target="tpu_custom_call" | custom-call | flops 838860800 | bytes 2097152 | tf_op jit(solution)/shard_map/pallas_call | solution.py:454
  63.0 0.6 while.18
  (36 shorter events, 0.2 us)
Async XLA Ops:
  0.6 9.2 %copy-start.6 = (bf16[1,8192,128]{2,1,0:T(8,128)(2,1)S(1)}, bf16[1,8192,128]{2,1,0:T(8,128)(2,1)}, u32[]{:S(2)}) copy-start(bf16[1,8192,128]{2,1,0:T(8,128)(2,1)} %param.14) | copy-start | bytes 6291460
  0.6 9.2 %copy-start.16 = (s32[1,2048]{1,0:T(1,128)S(1)}, s32[1,2048]{1,0:T(1,128)}, u32[]{:S(2)}) copy-start(s32[1,2048]{1,0:T(1,128)} %ids_ref.4) | copy-start | bytes 24580
  4.2 17.7 %all-to-all-start.1 = ((bf16[16,144,128]{2,1,0:T(8,128)(2,1)}), bf16[16,144,128]{2,1,0:T(8,128)(2,1)}, u32[]{:S(2)}, u32[]{:S(2)}) async-start(bf16[16,144,128]{2,1,0:T(8,128)(2,1)} %shard_map.111), calls=%async_computation.1 | async-start | bytes 1179648 | tf_op jit(solution)/shard_map/all_to_all | solution.py:428
  9.8 12.1 %copy-start.14 = (s32[4]{0:T(128)}, s32[4]{0:T(128)S(1)}, u32[]{:S(2)}) copy-start(s32[4]{0:T(128)S(1)} %pad_add_fusion.place_ref.spot_ref) | copy-start | bytes 52
  15.2 12.3 %copy-start.1 = (bf16[8,128,128]{2,1,0:T(8,128)(2,1)}, bf16[8,128,128]{2,1,0:T(8,128)(2,1)S(1)}, u32[]{:S(2)}) copy-start(bf16[8,128,128]{2,1,0:T(8,128)(2,1)S(1)} %get-tuple-element.111.beside_ref) | copy-start | bytes 786436
  15.2 12.3 %copy-start.3 = (bf16[4,128,128]{2,1,0:T(8,128)(2,1)}, bf16[4,128,128]{2,1,0:T(8,128)(2,1)S(1)}, u32[]{:S(2)}) copy-start(bf16[4,128,128]{2,1,0:T(8,128)(2,1)S(1)} %get-tuple-element.112.far_ref) | copy-start | bytes 393220
  15.2 12.3 %collective-permute-start = (bf16[8,128,128]{2,1,0:T(8,128)(2,1)S(1)}, bf16[8,128,128]{2,1,0:T(8,128)(2,1)S(1)}, u32[]{:S(2)}, u32[]{:S(2)}) collective-permute-start(bf16[8,128,128]{2,1,0:T(8,128)(2,1)S(1)} %get-tuple-element.111.beside_ref), channel_id=1, source_target_pairs={{0,8},{1,9},{2,10},{3,11},{4,12},{5,13},{6,14},{7,15},{8,0},{9,1},... | collective-permute-start | bytes 786440 | tf_op jit(solution)/shard_map/ppermute | solution.py:402
  17.1 10.4 %collective-permute-start.1 = (bf16[4,128,128]{2,1,0:T(8,128)(2,1)S(1)}, bf16[4,128,128]{2,1,0:T(8,128)(2,1)S(1)}, u32[]{:S(2)}, u32[]{:S(2)}) collective-permute-start(bf16[4,128,128]{2,1,0:T(8,128)(2,1)S(1)} %get-tuple-element.112.far_ref), channel_id=1, source_target_pairs={{0,1},{1,0},{2,3},{3,2},{4,5},{5,4},{6,7},{7,6},{8,9},{9,8},{10,11... | collective-permute-start | bytes 393224 | tf_op jit(solution)/shard_map/ppermute | solution.py:402
  18.9 0.6 %copy-start.7 = (f32[16,8,128]{2,1,0:T(8,128)}, f32[16,8,128]{2,1,0:T(8,128)S(1)}, u32[]{:S(2)}) copy-start(f32[16,8,128]{2,1,0:T(8,128)S(1)} %get-tuple-element.108.meta_ref) | copy-start | bytes 196612
  19.5 0.6 copy-start.9
  27.5 17.0 %copy-start.5 = (f32[16,128]{1,0:T(8,128)S(1)}, f32[16,128]{1,0:T(8,128)}, u32[]{:S(2)}) copy-start(f32[16,128]{1,0:T(8,128)} %get-tuple-element.119.firsts_ref) | copy-start | bytes 24580
  27.5 23.6 %copy-start = (bf16[2048,512]{1,0:T(8,128)(2,1)S(1)}, bf16[2048,512]{1,0:T(8,128)(2,1)}, u32[]{:S(2)}) copy-start(bf16[2048,512]{1,0:T(8,128)(2,1)} %weight_ref.1) | copy-start | bytes 6291460
  27.5 32.2 %all-to-all-start.2 = ((bf16[16,192,128]{2,1,0:T(8,128)(2,1)}), bf16[16,192,128]{2,1,0:T(8,128)(2,1)S(1)}, u32[]{:S(2)}, u32[]{:S(2)}) async-start(bf16[16,192,128]{2,1,0:T(8,128)(2,1)} %get-tuple-element.118), calls=%async_computation.2 | async-start | bytes 1572864 | tf_op jit(solution)/shard_map/all_to_all | solution.py:453
  38.4 1.4 %collective-permute-start.2 = (bf16[4,128,128]{2,1,0:T(8,128)(2,1)S(1)}, bf16[4,128,128]{2,1,0:T(8,128)(2,1)S(1)}, u32[]{:S(2)}, u32[]{:S(2)}) collective-permute-start(bf16[4,128,128]{2,1,0:T(8,128)(2,1)S(1)} %slice.3), channel_id=1, source_target_pairs={{0,1},{1,0},{2,3},{3,2},{4,5},{5,4},{6,7},{7,6},{8,9},{9,8},{10,11... | collective-permute-start | bytes 393224 | tf_op jit(solution)/shard_map/ppermute | solution.py:402
  40.6 9.9 %collective-permute-start.3 = (bf16[4,128,128]{2,1,0:T(8,128)(2,1)}, bf16[4,128,128]{2,1,0:T(8,128)(2,1)}, u32[]{:S(2)}, u32[]{:S(2)}) collective-permute-start(bf16[4,128,128]{2,1,0:T(8,128)(2,1)} %get-tuple-element.115), channel_id=1, source_target_pairs={{0,2},{1,3},{2,4},{3,5},{4,6},{5,7},{6,0},{7,1},{8,10},{9,11},{10,... | collective-permute-start | bytes 393224 | tf_op jit(solution)/shard_map/ppermute | solution.py:402
  40.6 9.9 %collective-permute-start.4 = (bf16[4,128,128]{2,1,0:T(8,128)(2,1)}, bf16[4,128,128]{2,1,0:T(8,128)(2,1)}, u32[]{:S(2)}, u32[]{:S(2)}) collective-permute-start(bf16[4,128,128]{2,1,0:T(8,128)(2,1)} %get-tuple-element.116), channel_id=1, source_target_pairs={{0,4},{1,5},{2,6},{3,7},{4,0},{5,1},{6,2},{7,3},{8,12},{9,13},{10,... | collective-permute-start | bytes 393224 | tf_op jit(solution)/shard_map/ppermute | solution.py:402
  43.0 8.1 %collective-permute-start.5 = (bf16[4,128,128]{2,1,0:T(8,128)(2,1)}, bf16[4,128,128]{2,1,0:T(8,128)(2,1)}, u32[]{:S(2)}, u32[]{:S(2)}) collective-permute-start(bf16[4,128,128]{2,1,0:T(8,128)(2,1)} %get-tuple-element.117), channel_id=1, source_target_pairs={{0,6},{1,7},{2,0},{3,1},{4,2},{5,3},{6,4},{7,5},{8,14},{9,15},{10,... | collective-permute-start | bytes 393224 | tf_op jit(solution)/shard_map/ppermute | solution.py:402
  44.5 1.0 %copy-start.2 = (bf16[8,128,128]{2,1,0:T(8,128)(2,1)S(1)}, bf16[8,128,128]{2,1,0:T(8,128)(2,1)}, u32[]{:S(2)}) copy-start(bf16[8,128,128]{2,1,0:T(8,128)(2,1)} %copy-done.1) | copy-start | bytes 786436
  45.4 0.9 %copy-start.4 = (bf16[4,128,128]{2,1,0:T(8,128)(2,1)S(1)}, bf16[4,128,128]{2,1,0:T(8,128)(2,1)}, u32[]{:S(2)}) copy-start(bf16[4,128,128]{2,1,0:T(8,128)(2,1)} %copy-done.3) | copy-start | bytes 393220
  48.3 11.5 %copy-start.12 = (f32[8,128]{1,0:T(8,128)S(1)}, f32[8,128]{1,0:T(8,128)}, u32[]{:S(2)}) copy-start(f32[8,128]{1,0:T(8,128)} %get-tuple-element.265.picked_ref) | copy-start | bytes 12292
  48.3 11.5 %copy-start.13 = (f32[1,512]{1,0:T(1,128)S(1)}, f32[1,512]{1,0:T(1,128)}, u32[]{:S(2)}) copy-start(f32[1,512]{1,0:T(1,128)} %ema_counts_ref.1) | copy-start | bytes 6148
  59.8 3.2 %copy-start.11 = (f32[1,512,128]{2,1,0:T(8,128)S(1)}, f32[1,512,128]{2,1,0:T(8,128)}, u32[]{:S(2)}) copy-start(f32[1,512,128]{2,1,0:T(8,128)} %param.15) | copy-start | bytes 786436
  59.8 3.2 %copy-start.15 = (s32[4]{0:T(128)S(1)}, s32[4]{0:T(128)}, u32[]{:S(2)}) copy-start(s32[4]{0:T(128)} %copy-done.14) | copy-start | bytes 52
  59.8 3.2 %copy-start.17 = (s32[1,2048]{1,0:T(1,128)S(1)}, s32[1,2048]{1,0:T(1,128)}, u32[]{:S(2)}) copy-start(s32[1,2048]{1,0:T(1,128)} %ids_ref.4) | copy-start | bytes 24580

commit v4 on v3

--- a/solution.py
+++ b/solution.py
@@ -87,7 +87,7 @@
 
 
 def encode_kernel(
-    frames_hbm, clips_hbm, weight_hbm, out_ref, frames_ref, clips_ref, weight_ref, stage_ref, in_sems, sems
+    frames_hbm, clips_hbm, weight_hbm, out_ref, frames_ref, clips_ref, weight_ref, part_ref, stage_ref, in_sems, sems
 ):
     loads = [
         pltpu.make_async_copy(frames_hbm, frames_ref, in_sems.at[6]),
@@ -112,11 +112,19 @@
     earlier = jnp.where(starts > 0.0, 0.0, earlier)
     stacked = jnp.concatenate([earlier, even, odd], axis=1).astype(BF16)
     last = odd[LANES - 1:]
-    for load in loads[2:]:
+    for load in loads[2:6]:
         load.wait()
     for pair in range(PARTS // 2):
-        wide = jnp.dot(
-            stacked, weight_ref[:, pair * 256:(pair + 1) * 256], preferred_element_type=F32
+        strip = pl.ds(pair * 256, 256)
+        part_ref[:, strip] = jnp.dot(
+            stacked[:, :512], weight_ref[:512, strip], preferred_element_type=F32
+        )
+    for load in loads[6:]:
+        load.wait()
+    for pair in range(PARTS // 2):
+        strip = pl.ds(pair * 256, 256)
+        wide = part_ref[:, strip] + jnp.dot(
+            stacked[:, 512:], weight_ref[512:, strip], preferred_element_type=F32
         )
         for g, block in ((2 * pair, wide[:, :LANES]), (2 * pair + 1, wide[:, LANES:])):
             extra = [last[:, :LANES], last[:, LANES:], *split3(block[:1]), starts[:1]]
@@ -201,22 +209,23 @@
 
 def route_kernel(
     spot_ref, place_ref, ids_ref, meta_ref, weight_hbm, got_ref,
-    out_ref, firsts_ref, owned_ref, weight_ref, stage_ref, sems, got_sem, weight_sem,
+    out_ref, firsts_ref, owned_ref, extra_ref, weight_ref, in_sems,
 ):
-    loaded = pltpu.make_async_copy(got_ref, owned_ref, got_sem)
-    loaded.start()
     group = (spot_ref[0] * 4 + spot_ref[1]) * 2 + spot_ref[2]
     mine = pl.ds(pl.multiple_of(group * LANES, LANES), LANES)
-    weight_load = pltpu.make_async_copy(weight_hbm.at[pl.ds(0, 256), mine], weight_ref, weight_sem)
-    weight_load.start()
+    extra_load = pltpu.make_async_copy(got_ref.at[:, pl.ds(LANES, 16), :], extra_ref, in_sems.at[0])
+    weight_load = pltpu.make_async_copy(weight_hbm.at[pl.ds(0, 256), mine], weight_ref, in_sems.at[1])
+    loaded = pltpu.make_async_copy(got_ref.at[:, pl.ds(0, LANES), :], owned_ref, in_sems.at[2])
+    for load in (extra_load, weight_load, loaded):
+        load.start()
     columns = id_columns(ids_ref)
     rows = iota((4 * BLOCK, LANES), 0)
     selector = jnp.concatenate(
         [one_hot(rows == place_ref[:, c * LANES:(c + 1) * LANES]) for c in range(PARTS)], axis=1
     )
+    extra_load.wait()
     weight_load.wait()
-    loaded.wait()
-    extras = [owned_ref[c, LANES:, :].astype(F32) for c in range(PARTS)]
+    extras = [extra_ref[c].astype(F32) for c in range(PARTS)]
     before = [jnp.zeros((16, LANES), F32)] + extras[:-1]
     firsts = finished_rows(
         [[extra[k:k + 1] for extra in before] for k in range(2)],
@@ -224,6 +233,7 @@
         [extra[5:6, 0:1] for extra in extras],
         weight_ref[...],
     )
+    loaded.wait()
     firsts_ref[...] = firsts
     row16 = iota((16, LANES), 0)
     for c in range(1, PARTS):
@@ -239,7 +249,7 @@
         wides = []
         for c in range(PARTS):
             quarter = columns[:, c:c + 1] >> 11
-            latent = owned_ref[c, :LANES, :]
+            latent = owned_ref[c]
             wides.append(jnp.concatenate(
                 [latent * one_hot(jnp.broadcast_to(quarter, (LANES, LANES)) == q) for q in (2 * half, 2 * half + 1)], axis=1
             ))
@@ -248,10 +258,7 @@
             for j in range(4):
                 to = 8 * half + 4 * q + j
                 data = total[j * BLOCK:j * BLOCK + CAP, q * LANES:(q + 1) * LANES]
-                stage_ref[to] = jnp.concatenate([data, meta_ref[to] + late], axis=0).astype(BF16)
-                pltpu.make_async_copy(stage_ref.at[to], out_ref.at[to], sems.at[to]).start()
-    for to in range(PARTS):
-        pltpu.make_async_copy(stage_ref.at[to], out_ref.at[to], sems.at[to]).wait()
+                out_ref[to] = jnp.concatenate([data, meta_ref[to] + late], axis=0).astype(BF16)
 
 
 def update_kernel(
@@ -416,6 +423,7 @@
             pltpu.VMEM(motion_frames.shape, BF16),
             pltpu.VMEM(clip_offsets.shape, I32),
             pltpu.VMEM(enc_weight.shape, BF16),
+            pltpu.VMEM((LANES, enc_weight.shape[1]), F32),
             pltpu.VMEM(blocks.shape, BF16),
             pltpu.SemaphoreType.DMA((8,)),
             pltpu.SemaphoreType.DMA((PARTS,)),
@@ -438,14 +446,11 @@
         message = shape((PARTS, BLOCK, LANES), BF16)
         return call(
             route_kernel, (message, shape((PARTS, LANES), F32)), 6, 2 << 30, 2 << 20, scalars=1, hbm_in=2,
-            out_specs=(IN_HBM, VMEM), limit=60,
             scratch=[
-                pltpu.VMEM(blocks.shape, BF16),
+                pltpu.VMEM((PARTS, LANES, LANES), BF16),
+                pltpu.VMEM((PARTS, 16, LANES), BF16),
                 pltpu.VMEM((256, LANES), BF16),
-                pltpu.VMEM(message.shape, BF16),
-                pltpu.SemaphoreType.DMA((PARTS,)),
-                pltpu.SemaphoreType.DMA,
-                pltpu.SemaphoreType.DMA,
+                pltpu.SemaphoreType.DMA((3,)),
             ],
         )(place, frame_places, code_ids, meta, enc_weight, got)
 

time: 64.9 us -> 63.2 us (0.974)
  Pallas kernels: 24.3 us -> 22.3 us
  waiting for transfers between devices: 12.2 us -> 13.5 us
    pallas_call x1, Pallas kernels: 5.56 us -> 3.65 us  [route(): call(route_kernel, (message, shape((PARTS, LANES), F32)), 6, 2 << 30, 2 <...]
    all_to_all x1, waiting for transfers between devices: 1.76 us -> 3 us  [body(): got = lax.all_to_all(sent, 'group', split_axis=0, concat_axis=0)]
    unnamed x32 -> x28, local copies, waits for them, and re-layouts: 3.14 us -> 2.79 us
  transfers between devices with their start and end apart: 8 -> 8, of which waited for: 5 -> 5; matrix products, arithmetic and copies ran while one was open for 0% -> 0% of each run, Pallas kernels for 28% -> 25%
where the time goes in v4:
time: 63.2 us; the launch traced here: 62.7 us
  Pallas kernels  22.3 us (35%)
  starting transfers between devices  22.3 us (35%)
  waiting for transfers between devices  13.5 us (21%)
  local copies, waits for them, and re-layouts  2.84 us (4%)
  between operations  1 us (2%)
  loops' own time  0.68 us (1%)
    all_to_all x1, starting transfers between devices, one_round(): arrived = lax.all_to_all(message, 'dp', split_axis=0, concat_axis=0)  10.9 us
    all_to_all x1, waiting for transfers between devices, one_round(): arrived = lax.all_to_all(message, 'dp', split_axis=0, concat_axis=0)  6.21 us
    ppermute x6, starting transfers between devices, moved(): return lax.ppermute(shard, 'group', pairs)  5.82 us
    all_to_all x1, starting transfers between devices, body(): got = lax.all_to_all(sent, 'group', split_axis=0, concat_axis=0)  5.56 us
    pallas_call x1, Pallas kernels, body(): call(pick_kernel, (four, four, eight), 3, 4 << 30, 4 << 20, scalars=1)  5.3 us
    ppermute x6, waiting for transfers between devices, moved(): return lax.ppermute(shard, 'group', pairs)  4.28 us
    pallas_call x1, Pallas kernels, route(): call(route_kernel, (message, shape((PARTS, LANES), F32)), 6, 2 << 30, 2 <...  3.65 us
    pallas_call x1, Pallas kernels, body(): call(encode_kernel, blocks, 3, 400 << 20, 4 << 20, hbm_in=3, limit=60, ou...  3.4 us
  transfers between devices with their start and end apart: 8, of which 5 were waited for; matrix products, arithmetic and copies ran while one was open for 0% of the time, Pallas kernels for 25%

profile of v4, /device:TPU:32, one launch (start us, length us, event | category | flops | bytes accessed | tf_op | source)
XLA Modules:
  0.0 62.7 jit_solution(13412923277977381231)
XLA Ops:
  0.7 3.4 %shard_map.111 = bf16[16,144,128]{2,1,0:T(8,128)(2,1)} custom-call(bf16[256,256]{1,0:T(8,128)(2,1)} %frames_hbm.1, s32[1,8]{1,0:T(1,128)} %clips_hbm.1, bf16[768,2048]{1,0:T(8,128)(2,1)} %weight_hbm.5), custom_call_target="tpu_custom_call" | custom-call | flops 419430400 | bytes 4194304 | tf_op jit(solution)/shard_map/pallas_call | solution.py:420
  4.1 5.6 %all-to-all-start.1 = ((bf16[16,144,128]{2,1,0:T(8,128)(2,1)}), bf16[16,144,128]{2,1,0:T(8,128)(2,1)}, u32[]{:S(2)}, u32[]{:S(2)}) async-start(bf16[16,144,128]{2,1,0:T(8,128)(2,1)} %shard_map.111), calls=%async_computation.1 | async-start | bytes 1179648 | tf_op jit(solution)/shard_map/all_to_all | solution.py:436
  9.6 0.1 pad_add_fusion.place_ref.spot_ref
  9.7 5.3 %shard_map.112 = (bf16[4,128,128]{2,1,0:T(8,128)(2,1)S(1)}, bf16[4,128,128]{2,1,0:T(8,128)(2,1)S(1)}, bf16[8,128,128]{2,1,0:T(8,128)(2,1)S(1)}) custom-call(s32[4]{0:T(128)S(1)} %pad_add_fusion.place_ref.spot_ref, s32[1,2048]{1,0:T(1,128)S(1)} %copy-done.12, bf16[8192,128]{1,0:T(8,128)(2,1)S(1)} %bitcast.15), custom_call_target="tpu_custom_call" | custom-call | flops 4294967296 | bytes 4194304 | tf_op jit(solution)/shard_map/pallas_call | solution.py:433
  15.1 2.0 %collective-permute-start = (bf16[8,128,128]{2,1,0:T(8,128)(2,1)S(1)}, bf16[8,128,128]{2,1,0:T(8,128)(2,1)S(1)}, u32[]{:S(2)}, u32[]{:S(2)}) collective-permute-start(bf16[8,128,128]{2,1,0:T(8,128)(2,1)S(1)} %get-tuple-element.111.beside_ref), channel_id=1, source_target_pairs={{0,8},{1,9},{2,10},{3,11},{4,12},{5,13},{6,14},{7,15},{8,0},{9,1},... | collective-permute-start | bytes 786440 | tf_op jit(solution)/shard_map/ppermute | solution.py:409
  17.0 1.7 %shard_map.113 = (s32[1,2048]{1,0:T(1,128)S(1)}, f32[16,8,128]{2,1,0:T(8,128)S(1)}) custom-call(s32[1,1]{1,0:T(1,128)} %constant.15.clone.1.round_ref, s32[1,2048]{1,0:T(1,128)S(1)} %copy-done.12), custom_call_target="tpu_custom_call" | custom-call | flops 524288000 | bytes 1048576 | tf_op jit(solution)/shard_map/pallas_call | solution.py:441
  18.8 3.0 %all-to-all-done.1.got_ref = bf16[16,144,128]{2,1,0:T(8,128)(2,1)} async-done(((bf16[16,144,128]{2,1,0:T(8,128)(2,1)}), bf16[16,144,128]{2,1,0:T(8,128)(2,1)}, u32[]{:S(2)}, u32[]{:S(2)}) %all-to-all-start.1) | async-done | bytes 589856 | tf_op jit(solution)/shard_map/all_to_all | solution.py:436
  21.8 3.6 %shard_map.114 = (bf16[16,192,128]{2,1,0:T(8,128)(2,1)S(1)}, f32[16,128]{1,0:T(8,128)S(1)}) custom-call(s32[4]{0:T(128)S(1)} %pad_add_fusion.place_ref.spot_ref, s32[1,2048]{1,0:T(1,128)S(1)} %get-tuple-element.107.place_ref, s32[1,2048]{1,0:T(1,128)S(1)} %copy-done.12, f32[16,8,128]{2,1,0:T(8,128)S(1)} %get-tuple-element.108.meta_ref, ...), custom_call_target="tpu_custom_call" | custom-call | flops 2147483648 | bytes 2097152 | tf_op jit(solution)/shard_map/pallas_call | solution.py:447
  25.5 0.9 %copy-done.1 = bf16[16,192,128]{2,1,0:T(8,128)(2,1)} copy-done((bf16[16,192,128]{2,1,0:T(8,128)(2,1)}, bf16[16,192,128]{2,1,0:T(8,128)(2,1)S(1)}, u32[]{:S(2)}) %copy-start.1) | copy-done | bytes 786456
  26.4 10.9 %all-to-all-start.2 = ((bf16[16,192,128]{2,1,0:T(8,128)(2,1)}), bf16[16,192,128]{2,1,0:T(8,128)(2,1)S(1)}, u32[]{:S(2)}, u32[]{:S(2)}) async-start(bf16[16,192,128]{2,1,0:T(8,128)(2,1)} %copy-done.1), calls=%async_computation.2 | async-start | bytes 1572864 | tf_op jit(solution)/shard_map/all_to_all | solution.py:458
  37.3 0.1 collective-permute-start.2
  37.4 1.3 %collective-permute-done.2.across_ref = bf16[4,128,128]{2,1,0:T(8,128)(2,1)S(1)} collective-permute-done((bf16[4,128,128]{2,1,0:T(8,128)(2,1)S(1)}, bf16[4,128,128]{2,1,0:T(8,128)(2,1)S(1)}, u32[]{:S(2)}, u32[]{:S(2)}) %collective-permute-start.2) | collective-permute-done | bytes 131104 | tf_op jit(solution)/shard_map/ppermute | solution.py:409
  38.7 0.8 %shard_map.115 = (bf16[4,128,128]{2,1,0:T(8,128)(2,1)}, bf16[4,128,128]{2,1,0:T(8,128)(2,1)}, bf16[4,128,128]{2,1,0:T(8,128)(2,1)}) custom-call(bf16[4,128,128]{2,1,0:T(8,128)(2,1)S(1)} %get-tuple-element.106.near_ref, bf16[4,128,128]{2,1,0:T(8,128)(2,1)S(1)} %collective-permute-done.1.far_ref, bf16[8,128,128]{2,1,0:T(8,128)(2,1)S(1)} %collective-permute-done.beside_ref, ...), custom_call_target="tpu_custom_call" | custom-call | flops 1048576 | bytes 1048576 | tf_op jit(solution)/shard_map/pallas_call | solution.py:483
  39.5 2.5 %collective-permute-start.4 = (bf16[4,128,128]{2,1,0:T(8,128)(2,1)}, bf16[4,128,128]{2,1,0:T(8,128)(2,1)}, u32[]{:S(2)}, u32[]{:S(2)}) collective-permute-start(bf16[4,128,128]{2,1,0:T(8,128)(2,1)} %get-tuple-element.116), channel_id=1, source_target_pairs={{0,4},{1,5},{2,6},{3,7},{4,0},{5,1},{6,2},{7,3},{8,12},{9,13},{10,... | collective-permute-start | bytes 393224 | tf_op jit(solution)/shard_map/ppermute | solution.py:409
  41.9 1.3 %collective-permute-start.5 = (bf16[4,128,128]{2,1,0:T(8,128)(2,1)}, bf16[4,128,128]{2,1,0:T(8,128)(2,1)}, u32[]{:S(2)}, u32[]{:S(2)}) collective-permute-start(bf16[4,128,128]{2,1,0:T(8,128)(2,1)} %get-tuple-element.117), channel_id=1, source_target_pairs={{0,6},{1,7},{2,0},{3,1},{4,2},{5,3},{6,4},{7,5},{8,14},{9,15},{10,... | collective-permute-start | bytes 393224 | tf_op jit(solution)/shard_map/ppermute | solution.py:409
  43.2 0.9 %copy-done.3 = bf16[8,128,128]{2,1,0:T(8,128)(2,1)S(1)} copy-done((bf16[8,128,128]{2,1,0:T(8,128)(2,1)S(1)}, bf16[8,128,128]{2,1,0:T(8,128)(2,1)}, u32[]{:S(2)}) %copy-start.3) | copy-done | bytes 262168
  44.2 0.9 %copy-done.5 = bf16[4,128,128]{2,1,0:T(8,128)(2,1)S(1)} copy-done((bf16[4,128,128]{2,1,0:T(8,128)(2,1)S(1)}, bf16[4,128,128]{2,1,0:T(8,128)(2,1)}, u32[]{:S(2)}) %copy-start.5) | copy-done | bytes 131096
  45.1 1.9 %shard_map.117 = (f32[1,2048]{1,0:T(1,128)S(1)}, f32[8,128]{1,0:T(8,128)}) custom-call(s32[4]{0:T(128)} %copy-done.10, f32[16,128]{1,0:T(8,128)S(1)} %get-tuple-element.119.firsts_ref, bf16[16,144,128]{2,1,0:T(8,128)(2,1)} %all-to-all-done.1.got_ref, bf16[4,128,128]{2,1,0:T(8,128)(2,1)S(1)} %get-tuple-element.106.near_ref, ...), custom_call_target="tpu_custom_call" | custom-call | flops 1048576 | bytes 1048576 | tf_op jit(solution)/shard_map/pallas_call | solution.py:478
  47.0 2.3 %collective-permute-done.3.y1_ref = bf16[4,128,128]{2,1,0:T(8,128)(2,1)} collective-permute-done((bf16[4,128,128]{2,1,0:T(8,128)(2,1)}, bf16[4,128,128]{2,1,0:T(8,128)(2,1)}, u32[]{:S(2)}, u32[]{:S(2)}) %collective-permute-start.3) | collective-permute-done | bytes 131104 | tf_op jit(solution)/shard_map/ppermute | solution.py:409
  49.4 0.6 collective-permute-done.5.y3_ref
  50.0 2.4 %shard_map.116 = bf16[256,256]{1,0:T(8,128)(2,1)} custom-call(s32[4]{0:T(128)} %copy-done.10, bf16[4,128,128]{2,1,0:T(8,128)(2,1)S(1)} %get-tuple-element.106.near_ref, bf16[4,128,128]{2,1,0:T(8,128)(2,1)S(1)} %collective-permute-done.1.far_ref, bf16[8,128,128]{2,1,0:T(8,128)(2,1)S(1)} %collective-permute-done.beside_ref, ...), custom_call_target="tpu_custom_call" | custom-call | flops 314572800 | bytes 4194304 | tf_op jit(solution)/shard_map/pallas_call | solution.py:485
  52.3 6.2 %all-to-all-done.2.message_ref = bf16[16,192,128]{2,1,0:T(8,128)(2,1)S(1)} async-done(((bf16[16,192,128]{2,1,0:T(8,128)(2,1)}), bf16[16,192,128]{2,1,0:T(8,128)(2,1)S(1)}, u32[]{:S(2)}, u32[]{:S(2)}) %all-to-all-start.2) | async-done | bytes 786464 | tf_op jit(solution)/shard_map/all_to_all | solution.py:458
  58.6 3.1 %shard_map.118 = (f32[512,128]{1,0:T(8,128)}, f32[1,512]{1,0:T(1,128)}, f32[512,256]{1,0:T(8,128)S(1)}, f32[1,2048]{1,0:T(1,128)}, s32[1,1]{1,0:T(1,128)}) custom-call(s32[4]{0:T(128)} %copy-done.10, bf16[16,192,128]{2,1,0:T(8,128)(2,1)S(1)} %all-to-all-done.2.message_ref, f32[512,256]{1,0:T(8,128)S(1)} %broadcast_in_dim.6.held_ref, f32[1,512]{1,0:T(1,128)S(1)} %copy-done.9, ...), custom_call_target="tpu_custom_call" | custom-call | flops 838860800 | bytes 2097152 | tf_op jit(solution)/shard_map/pallas_call | solution.py:459
  61.8 0.7 %while.18 = (s32[]{:T(128)}, f32[512,128]{1,0:T(8,128)}, f32[1,512]{1,0:T(1,128)}, f32[512,256]{1,0:T(8,128)S(1)}, f32[1,2048]{1,0:T(1,128)}, /*index=5*/s32[1,1...) while((s32[]{:T(128)}, f32[512,128]{1,0:T(8,128)}, ...), condition=%wide.region_1.0_spmd, body=%wide.region_0.0_spmd.sunk | while | flops 3510632448 | bytes 8650925 | solution.py:498
  (32 shorter events, 0.1 us)
Async XLA Ops:
  0.6 9.1 %copy-start.6 = (bf16[1,8192,128]{2,1,0:T(8,128)(2,1)S(1)}, bf16[1,8192,128]{2,1,0:T(8,128)(2,1)}, u32[]{:S(2)}) copy-start(bf16[1,8192,128]{2,1,0:T(8,128)(2,1)} %param.14) | copy-start | bytes 6291460
  0.6 9.1 %copy-start.12 = (s32[1,2048]{1,0:T(1,128)S(1)}, s32[1,2048]{1,0:T(1,128)}, u32[]{:S(2)}) copy-start(s32[1,2048]{1,0:T(1,128)} %ids_ref.4) | copy-start | bytes 24580
  4.1 17.7 %all-to-all-start.1 = ((bf16[16,144,128]{2,1,0:T(8,128)(2,1)}), bf16[16,144,128]{2,1,0:T(8,128)(2,1)}, u32[]{:S(2)}, u32[]{:S(2)}) async-start(bf16[16,144,128]{2,1,0:T(8,128)(2,1)} %shard_map.111), calls=%async_computation.1 | async-start | bytes 1179648 | tf_op jit(solution)/shard_map/all_to_all | solution.py:436
  9.7 12.1 %copy-start.10 = (s32[4]{0:T(128)}, s32[4]{0:T(128)S(1)}, u32[]{:S(2)}) copy-start(s32[4]{0:T(128)S(1)} %pad_add_fusion.place_ref.spot_ref) | copy-start | bytes 52
  15.0 10.4 %copy-start.2 = (bf16[8,128,128]{2,1,0:T(8,128)(2,1)}, bf16[8,128,128]{2,1,0:T(8,128)(2,1)S(1)}, u32[]{:S(2)}) copy-start(bf16[8,128,128]{2,1,0:T(8,128)(2,1)S(1)} %get-tuple-element.111.beside_ref) | copy-start | bytes 786436
  15.0 10.4 %copy-start.4 = (bf16[4,128,128]{2,1,0:T(8,128)(2,1)}, bf16[4,128,128]{2,1,0:T(8,128)(2,1)S(1)}, u32[]{:S(2)}) copy-start(bf16[4,128,128]{2,1,0:T(8,128)(2,1)S(1)} %get-tuple-element.112.far_ref) | copy-start | bytes 393220
  15.1 11.3 %collective-permute-start = (bf16[8,128,128]{2,1,0:T(8,128)(2,1)S(1)}, bf16[8,128,128]{2,1,0:T(8,128)(2,1)S(1)}, u32[]{:S(2)}, u32[]{:S(2)}) collective-permute-start(bf16[8,128,128]{2,1,0:T(8,128)(2,1)S(1)} %get-tuple-element.111.beside_ref), channel_id=1, source_target_pairs={{0,8},{1,9},{2,10},{3,11},{4,12},{5,13},{6,14},{7,15},{8,0},{9,1},... | collective-permute-start | bytes 786440 | tf_op jit(solution)/shard_map/ppermute | solution.py:409
  17.0 9.3 %collective-permute-start.1 = (bf16[4,128,128]{2,1,0:T(8,128)(2,1)S(1)}, bf16[4,128,128]{2,1,0:T(8,128)(2,1)S(1)}, u32[]{:S(2)}, u32[]{:S(2)}) collective-permute-start(bf16[4,128,128]{2,1,0:T(8,128)(2,1)S(1)} %get-tuple-element.112.far_ref), channel_id=1, source_target_pairs={{0,1},{1,0},{2,3},{3,2},{4,5},{5,4},{6,7},{7,6},{8,9},{9,8},{10,11... | collective-permute-start | bytes 393224 | tf_op jit(solution)/shard_map/ppermute | solution.py:409
  25.5 0.9 %copy-start.1 = (bf16[16,192,128]{2,1,0:T(8,128)(2,1)}, bf16[16,192,128]{2,1,0:T(8,128)(2,1)S(1)}, u32[]{:S(2)}) copy-start(bf16[16,192,128]{2,1,0:T(8,128)(2,1)S(1)} %get-tuple-element.118) | copy-start | bytes 2359300
  26.3 23.6 %copy-start = (bf16[2048,512]{1,0:T(8,128)(2,1)S(1)}, bf16[2048,512]{1,0:T(8,128)(2,1)}, u32[]{:S(2)}) copy-start(bf16[2048,512]{1,0:T(8,128)(2,1)} %weight_ref.1) | copy-start | bytes 6291460
  26.4 32.2 %all-to-all-start.2 = ((bf16[16,192,128]{2,1,0:T(8,128)(2,1)}), bf16[16,192,128]{2,1,0:T(8,128)(2,1)S(1)}, u32[]{:S(2)}, u32[]{:S(2)}) async-start(bf16[16,192,128]{2,1,0:T(8,128)(2,1)} %copy-done.1), calls=%async_computation.2 | async-start | bytes 1572864 | tf_op jit(solution)/shard_map/all_to_all | solution.py:458
  37.3 1.4 %collective-permute-start.2 = (bf16[4,128,128]{2,1,0:T(8,128)(2,1)S(1)}, bf16[4,128,128]{2,1,0:T(8,128)(2,1)S(1)}, u32[]{:S(2)}, u32[]{:S(2)}) collective-permute-start(bf16[4,128,128]{2,1,0:T(8,128)(2,1)S(1)} %slice.3), channel_id=1, source_target_pairs={{0,1},{1,0},{2,3},{3,2},{4,5},{5,4},{6,7},{7,6},{8,9},{9,8},{10,11... | collective-permute-start | bytes 393224 | tf_op jit(solution)/shard_map/ppermute | solution.py:409
  39.5 9.9 %collective-permute-start.3 = (bf16[4,128,128]{2,1,0:T(8,128)(2,1)}, bf16[4,128,128]{2,1,0:T(8,128)(2,1)}, u32[]{:S(2)}, u32[]{:S(2)}) collective-permute-start(bf16[4,128,128]{2,1,0:T(8,128)(2,1)} %get-tuple-element.115), channel_id=1, source_target_pairs={{0,2},{1,3},{2,4},{3,5},{4,6},{5,7},{6,0},{7,1},{8,10},{9,11},{10,... | collective-permute-start | bytes 393224 | tf_op jit(solution)/shard_map/ppermute | solution.py:409
  39.5 9.9 %collective-permute-start.4 = (bf16[4,128,128]{2,1,0:T(8,128)(2,1)}, bf16[4,128,128]{2,1,0:T(8,128)(2,1)}, u32[]{:S(2)}, u32[]{:S(2)}) collective-permute-start(bf16[4,128,128]{2,1,0:T(8,128)(2,1)} %get-tuple-element.116), channel_id=1, source_target_pairs={{0,4},{1,5},{2,6},{3,7},{4,0},{5,1},{6,2},{7,3},{8,12},{9,13},{10,... | collective-permute-start | bytes 393224 | tf_op jit(solution)/shard_map/ppermute | solution.py:409
  41.9 8.0 %collective-permute-start.5 = (bf16[4,128,128]{2,1,0:T(8,128)(2,1)}, bf16[4,128,128]{2,1,0:T(8,128)(2,1)}, u32[]{:S(2)}, u32[]{:S(2)}) collective-permute-start(bf16[4,128,128]{2,1,0:T(8,128)(2,1)} %get-tuple-element.117), channel_id=1, source_target_pairs={{0,6},{1,7},{2,0},{3,1},{4,2},{5,3},{6,4},{7,5},{8,14},{9,15},{10,... | collective-permute-start | bytes 393224 | tf_op jit(solution)/shard_map/ppermute | solution.py:409
  43.2 0.9 %copy-start.3 = (bf16[8,128,128]{2,1,0:T(8,128)(2,1)S(1)}, bf16[8,128,128]{2,1,0:T(8,128)(2,1)}, u32[]{:S(2)}) copy-start(bf16[8,128,128]{2,1,0:T(8,128)(2,1)} %copy-done.2) | copy-start | bytes 786436
  44.2 0.9 %copy-start.5 = (bf16[4,128,128]{2,1,0:T(8,128)(2,1)S(1)}, bf16[4,128,128]{2,1,0:T(8,128)(2,1)}, u32[]{:S(2)}) copy-start(bf16[4,128,128]{2,1,0:T(8,128)(2,1)} %copy-done.4) | copy-start | bytes 393220
  47.0 11.6 %copy-start.8 = (f32[8,128]{1,0:T(8,128)S(1)}, f32[8,128]{1,0:T(8,128)}, u32[]{:S(2)}) copy-start(f32[8,128]{1,0:T(8,128)} %get-tuple-element.265.picked_ref) | copy-start | bytes 12292
  47.0 11.6 %copy-start.9 = (f32[1,512]{1,0:T(1,128)S(1)}, f32[1,512]{1,0:T(1,128)}, u32[]{:S(2)}) copy-start(f32[1,512]{1,0:T(1,128)} %ema_counts_ref.1) | copy-start | bytes 6148
  58.6 3.2 %copy-start.7 = (f32[1,512,128]{2,1,0:T(8,128)S(1)}, f32[1,512,128]{2,1,0:T(8,128)}, u32[]{:S(2)}) copy-start(f32[1,512,128]{2,1,0:T(8,128)} %param.15) | copy-start | bytes 786436
  58.6 3.2 %copy-start.11 = (s32[4]{0:T(128)S(1)}, s32[4]{0:T(128)}, u32[]{:S(2)}) copy-start(s32[4]{0:T(128)} %copy-done.10) | copy-start | bytes 52
  58.6 3.2 %copy-start.13 = (s32[1,2048]{1,0:T(1,128)S(1)}, s32[1,2048]{1,0:T(1,128)}, u32[]{:S(2)}) copy-start(s32[1,2048]{1,0:T(1,128)} %ids_ref.4) | copy-start | bytes 24580

commit v5 on v4

--- a/solution.py
+++ b/solution.py
@@ -1,3 +1,5 @@
+import functools
+
 import jax
 import jax.numpy as jnp
 from jax import lax
@@ -262,7 +264,7 @@
 
 
 def update_kernel(
-    spot_ref, message_ref, held_ref, ema_counts_ref, error_ref, picked_ref, weight_hbm, ema_sums_hbm,
+    fresh, spot_ref, message_ref, held_ref, ema_counts_ref, error_ref, picked_ref, weight_hbm, ema_sums_hbm,
     book_ref, counts_ref, kept_ref, error_out_ref, need_ref, ema_sums_ref, weight_ref, sems,
 ):
     group = (spot_ref[0] * 4 + spot_ref[1]) * 2 + spot_ref[2]
@@ -273,18 +275,24 @@
     sums_load.start()
     codes = iota((SHARE, LANES), 0).astype(F32)
     ones = jnp.ones((8 * LANES, LANES), BF16)
-    kept_ref[...] = held_ref[...]
+    if not fresh:
+        kept_ref[...] = held_ref[...]
     need = jnp.zeros((1, 1), F32)
     lane = iota((1, LANES), 1)
-    metas, selectors, datas = [], [], []
+    metas, selectors, datas, begun = [], [], [], []
 
     def flush():
         data = jnp.concatenate(datas, axis=0)
-        kept_ref[...] += jnp.dot(
+        product = jnp.dot(
             jnp.concatenate(selectors, axis=1),
             jnp.concatenate([data, ones[:data.shape[0]]], axis=1),
             preferred_element_type=F32,
         )
+        if fresh and not begun:
+            kept_ref[...] = product
+        else:
+            kept_ref[...] += product
+        begun.append(True)
         selectors.clear()
         datas.clear()
 
@@ -454,10 +462,10 @@
             ],
         )(place, frame_places, code_ids, meta, enc_weight, got)
 
-    def one_round(message, held):
+    def one_round(message, held, fresh=False):
         arrived = lax.all_to_all(message, "dp", split_axis=0, concat_axis=0)
         return call(
-            update_kernel,
+            functools.partial(update_kernel, fresh),
             (
                 shape((SHARE, LANES), F32),
                 shape((1, SHARE), F32),
@@ -486,7 +494,7 @@
         place, near, from_core, from_x, across, *columns, dec_weight
     )
 
-    first = one_round(message, jnp.zeros((SHARE, 2 * LANES), F32))
+    first = one_round(message, jnp.zeros((SHARE, 2 * LANES), F32), True)
 
     def more(state):
         return state[0] < state[5][0, 0]

time: 63.2 us -> 63.8 us (level)
  no operation moved by 1% of the time
where the time goes in v5:
time: 63.8 us; the launch traced here: 63.2 us
  Pallas kernels  22.9 us (36%)
  starting transfers between devices  22.3 us (35%)
  waiting for transfers between devices  13.5 us (21%)
  local copies, waits for them, and re-layouts  2.84 us (4%)
  between operations  1 us (2%)
  loops' own time  0.68 us (1%)
    all_to_all x1, starting transfers between devices, one_round(): arrived = lax.all_to_all(message, 'dp', split_axis=0, concat_axis=0)  10.9 us
    all_to_all x1, waiting for transfers between devices, one_round(): arrived = lax.all_to_all(message, 'dp', split_axis=0, concat_axis=0)  6.21 us
    ppermute x6, starting transfers between devices, moved(): return lax.ppermute(shard, 'group', pairs)  5.82 us
    all_to_all x1, starting transfers between devices, body(): got = lax.all_to_all(sent, 'group', split_axis=0, concat_axis=0)  5.56 us
    pallas_call x1, Pallas kernels, body(): call(pick_kernel, (four, four, eight), 3, 4 << 30, 4 << 20, scalars=1)  5.3 us
    ppermute x6, waiting for transfers between devices, moved(): return lax.ppermute(shard, 'group', pairs)  4.28 us
    pallas_call x1, Pallas kernels, one_round(): call(functools.partial(update_kernel, fresh), (shape((SHARE, LANES), F32)...  3.7 us
    pallas_call x1, Pallas kernels, route(): call(route_kernel, (message, shape((PARTS, LANES), F32)), 6, 2 << 30, 2 <...  3.65 us
  transfers between devices with their start and end apart: 8, of which 5 were waited for; matrix products, arithmetic and copies ran while one was open for 0% of the time, Pallas kernels for 25%

profile of v5, /device:TPU:32, one launch (start us, length us, event | category | flops | bytes accessed | tf_op | source)
XLA Modules:
  0.0 63.2 jit_solution(18123105344422176680)
XLA Ops:
  0.7 3.4 %shard_map.111 = bf16[16,144,128]{2,1,0:T(8,128)(2,1)} custom-call(bf16[256,256]{1,0:T(8,128)(2,1)} %frames_hbm.1, s32[1,8]{1,0:T(1,128)} %clips_hbm.1, bf16[768,2048]{1,0:T(8,128)(2,1)} %weight_hbm.5), custom_call_target="tpu_custom_call" | custom-call | flops 419430400 | bytes 4194304 | tf_op jit(solution)/shard_map/pallas_call | solution.py:428
  4.1 5.6 %all-to-all-start.1 = ((bf16[16,144,128]{2,1,0:T(8,128)(2,1)}), bf16[16,144,128]{2,1,0:T(8,128)(2,1)}, u32[]{:S(2)}, u32[]{:S(2)}) async-start(bf16[16,144,128]{2,1,0:T(8,128)(2,1)} %shard_map.111), calls=%async_computation.1 | async-start | bytes 1179648 | tf_op jit(solution)/shard_map/all_to_all | solution.py:444
  9.6 0.1 pad_add_fusion.place_ref.spot_ref
  9.7 5.3 %shard_map.112 = (bf16[4,128,128]{2,1,0:T(8,128)(2,1)S(1)}, bf16[4,128,128]{2,1,0:T(8,128)(2,1)S(1)}, bf16[8,128,128]{2,1,0:T(8,128)(2,1)S(1)}) custom-call(s32[4]{0:T(128)S(1)} %pad_add_fusion.place_ref.spot_ref, s32[1,2048]{1,0:T(1,128)S(1)} %copy-done.12, bf16[8192,128]{1,0:T(8,128)(2,1)S(1)} %bitcast.15), custom_call_target="tpu_custom_call" | custom-call | flops 4294967296 | bytes 4194304 | tf_op jit(solution)/shard_map/pallas_call | solution.py:441
  15.1 2.0 %collective-permute-start = (bf16[8,128,128]{2,1,0:T(8,128)(2,1)S(1)}, bf16[8,128,128]{2,1,0:T(8,128)(2,1)S(1)}, u32[]{:S(2)}, u32[]{:S(2)}) collective-permute-start(bf16[8,128,128]{2,1,0:T(8,128)(2,1)S(1)} %get-tuple-element.111.beside_ref), channel_id=1, source_target_pairs={{0,8},{1,9},{2,10},{3,11},{4,12},{5,13},{6,14},{7,15},{8,0},{9,1},... | collective-permute-start | bytes 786440 | tf_op jit(solution)/shard_map/ppermute | solution.py:417
  17.0 1.7 %shard_map.113 = (s32[1,2048]{1,0:T(1,128)S(1)}, f32[16,8,128]{2,1,0:T(8,128)S(1)}) custom-call(s32[1,1]{1,0:T(1,128)} %constant.15.clone.1.round_ref, s32[1,2048]{1,0:T(1,128)S(1)} %copy-done.12), custom_call_target="tpu_custom_call" | custom-call | flops 524288000 | bytes 1048576 | tf_op jit(solution)/shard_map/pallas_call | solution.py:449
  18.8 3.0 %all-to-all-done.1.got_ref = bf16[16,144,128]{2,1,0:T(8,128)(2,1)} async-done(((bf16[16,144,128]{2,1,0:T(8,128)(2,1)}), bf16[16,144,128]{2,1,0:T(8,128)(2,1)}, u32[]{:S(2)}, u32[]{:S(2)}) %all-to-all-start.1) | async-done | bytes 589856 | tf_op jit(solution)/shard_map/all_to_all | solution.py:444
  21.8 3.6 %shard_map.114 = (bf16[16,192,128]{2,1,0:T(8,128)(2,1)S(1)}, f32[16,128]{1,0:T(8,128)S(1)}) custom-call(s32[4]{0:T(128)S(1)} %pad_add_fusion.place_ref.spot_ref, s32[1,2048]{1,0:T(1,128)S(1)} %get-tuple-element.107.place_ref, s32[1,2048]{1,0:T(1,128)S(1)} %copy-done.12, f32[16,8,128]{2,1,0:T(8,128)S(1)} %get-tuple-element.108.meta_ref, ...), custom_call_target="tpu_custom_call" | custom-call | flops 2147483648 | bytes 2097152 | tf_op jit(solution)/shard_map/pallas_call | solution.py:455
  25.5 0.9 %copy-done.1 = bf16[16,192,128]{2,1,0:T(8,128)(2,1)} copy-done((bf16[16,192,128]{2,1,0:T(8,128)(2,1)}, bf16[16,192,128]{2,1,0:T(8,128)(2,1)S(1)}, u32[]{:S(2)}) %copy-start.1) | copy-done | bytes 786456
  26.4 10.9 %all-to-all-start.2 = ((bf16[16,192,128]{2,1,0:T(8,128)(2,1)}), bf16[16,192,128]{2,1,0:T(8,128)(2,1)S(1)}, u32[]{:S(2)}, u32[]{:S(2)}) async-start(bf16[16,192,128]{2,1,0:T(8,128)(2,1)} %copy-done.1), calls=%async_computation.2 | async-start | bytes 1572864 | tf_op jit(solution)/shard_map/all_to_all | solution.py:466
  37.3 0.1 collective-permute-start.2
  37.4 1.3 %collective-permute-done.2.across_ref = bf16[4,128,128]{2,1,0:T(8,128)(2,1)S(1)} collective-permute-done((bf16[4,128,128]{2,1,0:T(8,128)(2,1)S(1)}, bf16[4,128,128]{2,1,0:T(8,128)(2,1)S(1)}, u32[]{:S(2)}, u32[]{:S(2)}) %collective-permute-start.2) | collective-permute-done | bytes 131104 | tf_op jit(solution)/shard_map/ppermute | solution.py:417
  38.7 0.8 %shard_map.115 = (bf16[4,128,128]{2,1,0:T(8,128)(2,1)}, bf16[4,128,128]{2,1,0:T(8,128)(2,1)}, bf16[4,128,128]{2,1,0:T(8,128)(2,1)}) custom-call(bf16[4,128,128]{2,1,0:T(8,128)(2,1)S(1)} %get-tuple-element.106.near_ref, bf16[4,128,128]{2,1,0:T(8,128)(2,1)S(1)} %collective-permute-done.1.far_ref, bf16[8,128,128]{2,1,0:T(8,128)(2,1)S(1)} %collective-permute-done.beside_ref, ...), custom_call_target="tpu_custom_call" | custom-call | flops 1048576 | bytes 1048576 | tf_op jit(solution)/shard_map/pallas_call | solution.py:491
  39.5 2.5 %collective-permute-start.4 = (bf16[4,128,128]{2,1,0:T(8,128)(2,1)}, bf16[4,128,128]{2,1,0:T(8,128)(2,1)}, u32[]{:S(2)}, u32[]{:S(2)}) collective-permute-start(bf16[4,128,128]{2,1,0:T(8,128)(2,1)} %get-tuple-element.116), channel_id=1, source_target_pairs={{0,4},{1,5},{2,6},{3,7},{4,0},{5,1},{6,2},{7,3},{8,12},{9,13},{10,... | collective-permute-start | bytes 393224 | tf_op jit(solution)/shard_map/ppermute | solution.py:417
  41.9 1.3 %collective-permute-start.5 = (bf16[4,128,128]{2,1,0:T(8,128)(2,1)}, bf16[4,128,128]{2,1,0:T(8,128)(2,1)}, u32[]{:S(2)}, u32[]{:S(2)}) collective-permute-start(bf16[4,128,128]{2,1,0:T(8,128)(2,1)} %get-tuple-element.117), channel_id=1, source_target_pairs={{0,6},{1,7},{2,0},{3,1},{4,2},{5,3},{6,4},{7,5},{8,14},{9,15},{10,... | collective-permute-start | bytes 393224 | tf_op jit(solution)/shard_map/ppermute | solution.py:417
  43.2 0.9 %copy-done.3 = bf16[8,128,128]{2,1,0:T(8,128)(2,1)S(1)} copy-done((bf16[8,128,128]{2,1,0:T(8,128)(2,1)S(1)}, bf16[8,128,128]{2,1,0:T(8,128)(2,1)}, u32[]{:S(2)}) %copy-start.3) | copy-done | bytes 262168
  44.2 0.9 %copy-done.5 = bf16[4,128,128]{2,1,0:T(8,128)(2,1)S(1)} copy-done((bf16[4,128,128]{2,1,0:T(8,128)(2,1)S(1)}, bf16[4,128,128]{2,1,0:T(8,128)(2,1)}, u32[]{:S(2)}) %copy-start.5) | copy-done | bytes 131096
  45.1 1.9 %shard_map.117 = (f32[1,2048]{1,0:T(1,128)S(1)}, f32[8,128]{1,0:T(8,128)}) custom-call(s32[4]{0:T(128)} %copy-done.10, f32[16,128]{1,0:T(8,128)S(1)} %get-tuple-element.119.firsts_ref, bf16[16,144,128]{2,1,0:T(8,128)(2,1)} %all-to-all-done.1.got_ref, bf16[4,128,128]{2,1,0:T(8,128)(2,1)S(1)} %get-tuple-element.106.near_ref, ...), custom_call_target="tpu_custom_call" | custom-call | flops 1048576 | bytes 1048576 | tf_op jit(solution)/shard_map/pallas_call | solution.py:486
  47.0 2.3 %collective-permute-done.3.y1_ref = bf16[4,128,128]{2,1,0:T(8,128)(2,1)} collective-permute-done((bf16[4,128,128]{2,1,0:T(8,128)(2,1)}, bf16[4,128,128]{2,1,0:T(8,128)(2,1)}, u32[]{:S(2)}, u32[]{:S(2)}) %collective-permute-start.3) | collective-permute-done | bytes 131104 | tf_op jit(solution)/shard_map/ppermute | solution.py:417
  49.4 0.6 collective-permute-done.5.y3_ref
  50.0 2.4 %shard_map.116 = bf16[256,256]{1,0:T(8,128)(2,1)} custom-call(s32[4]{0:T(128)} %copy-done.10, bf16[4,128,128]{2,1,0:T(8,128)(2,1)S(1)} %get-tuple-element.106.near_ref, bf16[4,128,128]{2,1,0:T(8,128)(2,1)S(1)} %collective-permute-done.1.far_ref, bf16[8,128,128]{2,1,0:T(8,128)(2,1)S(1)} %collective-permute-done.beside_ref, ...), custom_call_target="tpu_custom_call" | custom-call | flops 314572800 | bytes 4194304 | tf_op jit(solution)/shard_map/pallas_call | solution.py:493
  52.3 6.2 %all-to-all-done.2.message_ref = bf16[16,192,128]{2,1,0:T(8,128)(2,1)S(1)} async-done(((bf16[16,192,128]{2,1,0:T(8,128)(2,1)}), bf16[16,192,128]{2,1,0:T(8,128)(2,1)S(1)}, u32[]{:S(2)}, u32[]{:S(2)}) %all-to-all-start.2) | async-done | bytes 786464 | tf_op jit(solution)/shard_map/all_to_all | solution.py:466
  58.6 3.7 %shard_map.118 = (f32[512,128]{1,0:T(8,128)}, f32[1,512]{1,0:T(1,128)}, f32[512,256]{1,0:T(8,128)S(1)}, f32[1,2048]{1,0:T(1,128)}, s32[1,1]{1,0:T(1,128)}) custom-call(s32[4]{0:T(128)} %copy-done.10, bf16[16,192,128]{2,1,0:T(8,128)(2,1)S(1)} %all-to-all-done.2.message_ref, f32[512,256]{1,0:T(8,128)S(1)} %broadcast_in_dim.6.held_ref, f32[1,512]{1,0:T(1,128)S(1)} %copy-done.9, ...), custom_call_target="tpu_custom_call" | custom-call | flops 838860800 | bytes 2097152 | tf_op jit(solution)/shard_map/pallas_call | solution.py:467
  62.4 0.7 %while.18 = (s32[]{:T(128)}, f32[512,128]{1,0:T(8,128)}, f32[1,512]{1,0:T(1,128)}, f32[512,256]{1,0:T(8,128)S(1)}, f32[1,2048]{1,0:T(1,128)}, /*index=5*/s32[1,1...) while((s32[]{:T(128)}, f32[512,128]{1,0:T(8,128)}, ...), condition=%wide.region_1.0_spmd, body=%wide.region_0.0_spmd.sunk | while | flops 3510632448 | bytes 8650925 | solution.py:506
  (32 shorter events, 0.1 us)
Async XLA Ops:
  0.6 9.1 %copy-start.6 = (bf16[1,8192,128]{2,1,0:T(8,128)(2,1)S(1)}, bf16[1,8192,128]{2,1,0:T(8,128)(2,1)}, u32[]{:S(2)}) copy-start(bf16[1,8192,128]{2,1,0:T(8,128)(2,1)} %param.14) | copy-start | bytes 6291460
  0.6 9.1 %copy-start.12 = (s32[1,2048]{1,0:T(1,128)S(1)}, s32[1,2048]{1,0:T(1,128)}, u32[]{:S(2)}) copy-start(s32[1,2048]{1,0:T(1,128)} %ids_ref.4) | copy-start | bytes 24580
  4.1 17.7 %all-to-all-start.1 = ((bf16[16,144,128]{2,1,0:T(8,128)(2,1)}), bf16[16,144,128]{2,1,0:T(8,128)(2,1)}, u32[]{:S(2)}, u32[]{:S(2)}) async-start(bf16[16,144,128]{2,1,0:T(8,128)(2,1)} %shard_map.111), calls=%async_computation.1 | async-start | bytes 1179648 | tf_op jit(solution)/shard_map/all_to_all | solution.py:444
  9.7 12.1 %copy-start.10 = (s32[4]{0:T(128)}, s32[4]{0:T(128)S(1)}, u32[]{:S(2)}) copy-start(s32[4]{0:T(128)S(1)} %pad_add_fusion.place_ref.spot_ref) | copy-start | bytes 52
  15.0 10.4 %copy-start.2 = (bf16[8,128,128]{2,1,0:T(8,128)(2,1)}, bf16[8,128,128]{2,1,0:T(8,128)(2,1)S(1)}, u32[]{:S(2)}) copy-start(bf16[8,128,128]{2,1,0:T(8,128)(2,1)S(1)} %get-tuple-element.111.beside_ref) | copy-start | bytes 786436
  15.0 10.4 %copy-start.4 = (bf16[4,128,128]{2,1,0:T(8,128)(2,1)}, bf16[4,128,128]{2,1,0:T(8,128)(2,1)S(1)}, u32[]{:S(2)}) copy-start(bf16[4,128,128]{2,1,0:T(8,128)(2,1)S(1)} %get-tuple-element.112.far_ref) | copy-start | bytes 393220
  15.1 11.3 %collective-permute-start = (bf16[8,128,128]{2,1,0:T(8,128)(2,1)S(1)}, bf16[8,128,128]{2,1,0:T(8,128)(2,1)S(1)}, u32[]{:S(2)}, u32[]{:S(2)}) collective-permute-start(bf16[8,128,128]{2,1,0:T(8,128)(2,1)S(1)} %get-tuple-element.111.beside_ref), channel_id=1, source_target_pairs={{0,8},{1,9},{2,10},{3,11},{4,12},{5,13},{6,14},{7,15},{8,0},{9,1},... | collective-permute-start | bytes 786440 | tf_op jit(solution)/shard_map/ppermute | solution.py:417
  17.0 9.3 %collective-permute-start.1 = (bf16[4,128,128]{2,1,0:T(8,128)(2,1)S(1)}, bf16[4,128,128]{2,1,0:T(8,128)(2,1)S(1)}, u32[]{:S(2)}, u32[]{:S(2)}) collective-permute-start(bf16[4,128,128]{2,1,0:T(8,128)(2,1)S(1)} %get-tuple-element.112.far_ref), channel_id=1, source_target_pairs={{0,1},{1,0},{2,3},{3,2},{4,5},{5,4},{6,7},{7,6},{8,9},{9,8},{10,11... | collective-permute-start | bytes 393224 | tf_op jit(solution)/shard_map/ppermute | solution.py:417
  25.5 0.9 %copy-start.1 = (bf16[16,192,128]{2,1,0:T(8,128)(2,1)}, bf16[16,192,128]{2,1,0:T(8,128)(2,1)S(1)}, u32[]{:S(2)}) copy-start(bf16[16,192,128]{2,1,0:T(8,128)(2,1)S(1)} %get-tuple-element.118) | copy-start | bytes 2359300
  26.3 23.6 %copy-start = (bf16[2048,512]{1,0:T(8,128)(2,1)S(1)}, bf16[2048,512]{1,0:T(8,128)(2,1)}, u32[]{:S(2)}) copy-start(bf16[2048,512]{1,0:T(8,128)(2,1)} %weight_ref.1) | copy-start | bytes 6291460
  26.4 32.2 %all-to-all-start.2 = ((bf16[16,192,128]{2,1,0:T(8,128)(2,1)}), bf16[16,192,128]{2,1,0:T(8,128)(2,1)S(1)}, u32[]{:S(2)}, u32[]{:S(2)}) async-start(bf16[16,192,128]{2,1,0:T(8,128)(2,1)} %copy-done.1), calls=%async_computation.2 | async-start | bytes 1572864 | tf_op jit(solution)/shard_map/all_to_all | solution.py:466
  37.3 1.4 %collective-permute-start.2 = (bf16[4,128,128]{2,1,0:T(8,128)(2,1)S(1)}, bf16[4,128,128]{2,1,0:T(8,128)(2,1)S(1)}, u32[]{:S(2)}, u32[]{:S(2)}) collective-permute-start(bf16[4,128,128]{2,1,0:T(8,128)(2,1)S(1)} %slice.3), channel_id=1, source_target_pairs={{0,1},{1,0},{2,3},{3,2},{4,5},{5,4},{6,7},{7,6},{8,9},{9,8},{10,11... | collective-permute-start | bytes 393224 | tf_op jit(solution)/shard_map/ppermute | solution.py:417
  39.5 9.9 %collective-permute-start.3 = (bf16[4,128,128]{2,1,0:T(8,128)(2,1)}, bf16[4,128,128]{2,1,0:T(8,128)(2,1)}, u32[]{:S(2)}, u32[]{:S(2)}) collective-permute-start(bf16[4,128,128]{2,1,0:T(8,128)(2,1)} %get-tuple-element.115), channel_id=1, source_target_pairs={{0,2},{1,3},{2,4},{3,5},{4,6},{5,7},{6,0},{7,1},{8,10},{9,11},{10,... | collective-permute-start | bytes 393224 | tf_op jit(solution)/shard_map/ppermute | solution.py:417
  39.5 9.9 %collective-permute-start.4 = (bf16[4,128,128]{2,1,0:T(8,128)(2,1)}, bf16[4,128,128]{2,1,0:T(8,128)(2,1)}, u32[]{:S(2)}, u32[]{:S(2)}) collective-permute-start(bf16[4,128,128]{2,1,0:T(8,128)(2,1)} %get-tuple-element.116), channel_id=1, source_target_pairs={{0,4},{1,5},{2,6},{3,7},{4,0},{5,1},{6,2},{7,3},{8,12},{9,13},{10,... | collective-permute-start | bytes 393224 | tf_op jit(solution)/shard_map/ppermute | solution.py:417
  41.9 8.0 %collective-permute-start.5 = (bf16[4,128,128]{2,1,0:T(8,128)(2,1)}, bf16[4,128,128]{2,1,0:T(8,128)(2,1)}, u32[]{:S(2)}, u32[]{:S(2)}) collective-permute-start(bf16[4,128,128]{2,1,0:T(8,128)(2,1)} %get-tuple-element.117), channel_id=1, source_target_pairs={{0,6},{1,7},{2,0},{3,1},{4,2},{5,3},{6,4},{7,5},{8,14},{9,15},{10,... | collective-permute-start | bytes 393224 | tf_op jit(solution)/shard_map/ppermute | solution.py:417
  43.2 0.9 %copy-start.3 = (bf16[8,128,128]{2,1,0:T(8,128)(2,1)S(1)}, bf16[8,128,128]{2,1,0:T(8,128)(2,1)}, u32[]{:S(2)}) copy-start(bf16[8,128,128]{2,1,0:T(8,128)(2,1)} %copy-done.2) | copy-start | bytes 786436
  44.2 0.9 %copy-start.5 = (bf16[4,128,128]{2,1,0:T(8,128)(2,1)S(1)}, bf16[4,128,128]{2,1,0:T(8,128)(2,1)}, u32[]{:S(2)}) copy-start(bf16[4,128,128]{2,1,0:T(8,128)(2,1)} %copy-done.4) | copy-start | bytes 393220
  47.0 11.6 %copy-start.8 = (f32[8,128]{1,0:T(8,128)S(1)}, f32[8,128]{1,0:T(8,128)}, u32[]{:S(2)}) copy-start(f32[8,128]{1,0:T(8,128)} %get-tuple-element.265.picked_ref) | copy-start | bytes 12292
  47.0 11.6 %copy-start.9 = (f32[1,512]{1,0:T(1,128)S(1)}, f32[1,512]{1,0:T(1,128)}, u32[]{:S(2)}) copy-start(f32[1,512]{1,0:T(1,128)} %ema_counts_ref.1) | copy-start | bytes 6148
  58.6 3.7 %copy-start.7 = (f32[1,512,128]{2,1,0:T(8,128)S(1)}, f32[1,512,128]{2,1,0:T(8,128)}, u32[]{:S(2)}) copy-start(f32[1,512,128]{2,1,0:T(8,128)} %param.15) | copy-start | bytes 786436
  58.6 3.7 %copy-start.11 = (s32[4]{0:T(128)S(1)}, s32[4]{0:T(128)}, u32[]{:S(2)}) copy-start(s32[4]{0:T(128)} %copy-done.10) | copy-start | bytes 52
  58.6 3.7 %copy-start.13 = (s32[1,2048]{1,0:T(1,128)S(1)}, s32[1,2048]{1,0:T(1,128)}, u32[]{:S(2)}) copy-start(s32[1,2048]{1,0:T(1,128)} %ids_ref.4) | copy-start | bytes 24580
